TPU v7x, 256 devices: a whole 4x4x8 slice. The times are simulated.
256 devices in a mesh: sail: 32 (over y, z), cable: 8 (over x, core).
Axes of the slice: x: 4, y: 4, z: 8, core: 2. Of those that a mesh axis runs over, the one named last changes fastest.
Arguments:
- traces: bfloat16 [524288, 512], P(('sail', 'cable')), may hold values from -6 to 6
- src_index: int32 [16384, 128], P(('sail', 'cable')), may hold values from 0 to 2175
- rcv_index: int32 [16384, 128], P(('sail', 'cable')), may hold values from 0 to 4095
- taper_index: int32 [16384, 128], P(('sail', 'cable')), may hold values from 0 to 15
- fetch_rows: int32 [8192, 128], P(('sail', 'cable')), may hold values from 0 to 2047, as said below
- line_owner: int32 [32], replicated, may hold values from 0 to 31, each once
- taper_table: float32 [16], replicated, may hold values from 0.2 to 1
Outputs:
- predicted: bfloat16 [16384, 512], P(('sail', 'cable'))
Inputs may be any that keep to these rules, and one draw needn't show every extreme that they name: Each row of fetch_rows names exactly 64 distinct traces.
All inputs are finite; a program needn't handle non-finite values.
Results may differ from a plain program's by a relative error of at most 0.0084.
Values may be sent and summed in bfloat16 or wider, within the bound.
No kernel may reach another device: no remote copies, remote signals or barrier semaphores. Data moves between devices by JAX's collectives and lax.ppermute only.
A program may use at most 64 MiB of HBM per device.

v0:
```python
import math

import jax
import jax.numpy as jnp
from jax import lax
from jax.sharding import PartitionSpec as P

HALO = 64


def with_halo(shard, sides, width):
    for axis, dim in sides:
        peers, length = (lax.axis_size(axis), shard.shape[dim])
        up = [(i, (i + 1) % peers) for i in range(peers - 1)]
        down = [(j, i) for i, j in up]
        last = lax.slice_in_dim(shard, length - width, length, axis=dim)
        leading = lax.slice_in_dim(shard, 0, width, axis=dim)
        before = lax.ppermute(last, axis, up)
        after = lax.ppermute(leading, axis, down)
        shard = jnp.concatenate([before, shard, after], axis=dim)
    return shard


def forward_table(samples):
    times = jnp.arange(samples, dtype=jnp.int32)
    freqs = jnp.arange(samples // 2, dtype=jnp.int32)
    turns = times[:, None] * freqs[None, :] % samples
    angle = turns.astype(jnp.float32) * (2.0 * math.pi / samples)
    scale = 1.0 / math.sqrt(samples)
    return (jnp.concatenate([jnp.cos(angle), -jnp.sin(angle)], axis=1) * scale).astype(jnp.bfloat16)


def synthesis_table(samples, aperture):
    freqs = jnp.arange(samples // 2, dtype=jnp.int32)
    times = jnp.arange(samples, dtype=jnp.int32)
    turns = freqs[:, None] * times[None, :] % samples
    angle = turns.astype(jnp.float32) * (2.0 * math.pi / samples)
    scale = 1.0 / math.sqrt(aperture * (samples // 2))
    return (jnp.concatenate([jnp.cos(angle), -jnp.sin(angle)], axis=0) * scale).astype(jnp.bfloat16)


def predict_block(src_rows, rcv_rows, weights):
    half = src_rows.shape[-1] // 2
    left = src_rows.astype(jnp.float32)
    right = rcv_rows.astype(jnp.float32)
    real_part = left[..., :half] * right[..., :half] - left[..., half:] * right[..., half:]
    imag_part = left[..., :half] * right[..., half:] + left[..., half:] * right[..., :half]
    scaled = weights[..., None]
    return jnp.concatenate(
        [jnp.sum(scaled * real_part, axis=1), jnp.sum(scaled * imag_part, axis=1)], axis=-1
    )


def body(traces, src_index, rcv_index, taper_index, fetch_rows, line_owner, taper_table):
    sail_count = lax.axis_size("sail")
    tr_rows, samples = traces.shape
    out_rows, aperture = src_index.shape
    fetch_cap = fetch_rows.shape[1]
    forward = forward_table(samples)
    synth = synthesis_table(samples, aperture)
    line_of_peer = (
        jnp.zeros((sail_count,), jnp.int32)
        .at[line_owner]
        .set(jnp.arange(sail_count, dtype=jnp.int32))
    )
    by_peer = jnp.take(fetch_rows, line_of_peer, axis=0)
    own_spectra = jnp.dot(traces, forward, preferred_element_type=jnp.float32).astype(jnp.bfloat16)
    widened = with_halo(own_spectra, (("cable", 0),), HALO)
    cap_ids = jnp.arange(fetch_cap, dtype=jnp.int32)
    asked = lax.all_to_all(by_peer, "sail", split_axis=0, concat_axis=0, tiled=True)
    outgoing = jnp.take(own_spectra, asked.reshape(-1), axis=0).reshape(
        sail_count, fetch_cap, samples
    )
    coming = lax.all_to_all(outgoing, "sail", split_axis=0, concat_axis=0, tiled=True)
    arrived = coming.reshape(sail_count * fetch_cap, samples)
    slot_map = (line_owner[:, None] * fetch_cap + cap_ids[None, :]).reshape(-1)
    rcv_rows_index = jnp.take(slot_map, rcv_index, axis=0)
    taper_ids = jnp.arange(taper_table.shape[0], dtype=jnp.int32)
    block = min(16, out_rows)
    count = out_rows // block

    def one_block(pieces):
        s_idx, r_idx, t_idx = pieces
        src_rows = jnp.take(widened, s_idx, axis=0)
        rcv_rows = jnp.take(arrived, r_idx, axis=0)
        weights = jnp.sum(
            jnp.where(t_idx[..., None] == taper_ids, taper_table, jnp.zeros_like(taper_table)),
            axis=-1,
        )
        return predict_block(src_rows, rcv_rows, weights).astype(jnp.bfloat16)

    summed = lax.map(
        one_block,
        (
            src_index.reshape(count, block, aperture),
            rcv_rows_index.reshape(count, block, aperture),
            taper_index.reshape(count, block, aperture),
        ),
    )
    summed = summed.reshape(out_rows, samples)
    return jnp.dot(summed, synth, preferred_element_type=jnp.float32).astype(jnp.bfloat16)


def solution(mesh):
    return jax.shard_map(
        body,
        mesh=mesh,
        in_specs=(
            P(("sail", "cable"), None),
            P(("sail", "cable"), None),
            P(("sail", "cable"), None),
            P(("sail", "cable"), None),
            P(("sail", "cable"), None),
            P(),
            P(),
        ),
        out_specs=P(("sail", "cable"), None),
        check_vma=False,
    )
```

profile of v0, /device:TPU:4, one launch (start us, length us, event | category | flops | bytes accessed | tf_op | source)
XLA Modules:
  0.0 275.7 jit_solution(9012029421630741061)
XLA Ops:
  3.5 11.5 %all-to-all-start = ((s32[32,1,128]{2,1,0:T(1,128)}), s32[32,1,128]{2,1,0:T(1,128)S(1)}, u32[]{:S(2)}, u32[]{:S(2)}) async-start(s32[32,1,128]{2,1,0:T(1,128)} %bitcast.8), calls=%async_computation | async-start | bytes 32768 | tf_op jit(solution)/shard_map/all_to_all | solution.py:70
  15.0 2.1 sine_negate_fusion.1
  17.1 2.7 fusion.6
  19.8 3.9 %copy.16 = bf16[2048,512]{1,0:T(8,128)(2,1)} copy(bf16[2048,512]{0,1:T(8,128)(2,1)} %fusion.6) | data formatting | bytes 4194304 | tf_op jit(solution)/shard_map/convert_element_type | solution.py:67
  24.8 19.3 %gather_fusion.4 = bf16[4096,512]{1,0:T(8,128)(2,1)} fusion(bf16[2048,512]{1,0:T(8,128)(2,1)} %copy.16, s32[4096]{0:T(1024)S(1)} %broadcast_clamp_fusion), kind=kCustom, calls=%fused_computation.4 | custom fusion | bytes 8404992 | tf_op jit(solution)/shard_map/jit(_take)/gather | solution.py:71
  44.1 3.9 %broadcast_select_fusion = bf16[32,128,512]{2,1,0:T(8,128)(2,1)} fusion(bf16[32,128,512]{2,1,0:T(8,128)(2,1)} %bitcast.71, pred[32,128]{1,0:T(8,128)(4,1)S(1)} %compare_and_fusion.2), kind=kLoop, calls=%fused_computation.27 | loop fusion | flops 2097152 | bytes 8392704 | tf_op jit(solution)/shard_map/jit(_take)/select_n | solution.py:71
  48.0 9.0 %all-to-all-start.1 = ((bf16[32,128,512]{2,1,0:T(8,128)(2,1)}), bf16[32,128,512]{2,1,0:T(8,128)(2,1)}, u32[]{:S(2)}, u32[]{:S(2)}) async-start(bf16[32,128,512]{2,1,0:T(8,128)(2,1)} %broadcast_select_fusion), calls=%async_computation.1 | async-start | bytes 8388608 | tf_op jit(solution)/shard_map/all_to_all | solution.py:74
  57.1 1.7 fusion.33
  58.8 1.9 collective-permute-start
  60.7 3.8 %collective-permute-start.1 = (bf16[64,512]{0,1:T(8,128)(2,1)}, bf16[64,512]{0,1:T(8,128)(2,1)S(1)}, u32[]{:S(2)}, u32[]{:S(2)}) collective-permute-start(bf16[64,512]{0,1:T(8,128)(2,1)} %get-tuple-element.125), channel_id=1, source_target_pairs={{1,0},{2,1},{3,2},{4,3},{5,4},{6,5},{7,6},{9,8},{10,9},{11,10},{12... | collective-permute-start | bytes 196616 | tf_op jit(solution)/shard_map/ppermute | solution.py:19
  64.6 45.5 %gather_fusion.2 = s32[8192]{0:T(1024)S(1)} fusion(s32[4096]{0:T(1024)S(1)} %add_bitcast_fusion, s32[8192]{0:T(1024)S(1)} %bitcast_clamp_fusion), kind=kCustom, calls=%fused_computation.2 | custom fusion | bytes 98304 | tf_op jit(solution)/shard_map/jit(_take)/gather | solution.py:77
  110.2 2.1 sine_negate_fusion
  112.3 5.3 %concatenate.25 = bf16[2176,512]{0,1:T(8,128)(2,1)} concatenate(bf16[64,512]{0,1:T(8,128)(2,1)S(1)} %collective-permute-done, bf16[2048,512]{0,1:T(8,128)(2,1)} %fusion.6, bf16[64,512]{0,1:T(8,128)(2,1)S(1)} %collective-permute-done.1), dimensions={0} | concatenate | bytes 4456448 | tf_op jit(solution)/shard_map/concatenate | solution.py:20
  117.6 4.2 %copy.17 = bf16[2176,512]{1,0:T(8,128)(2,1)} copy(bf16[2176,512]{0,1:T(8,128)(2,1)} %concatenate.25) | data formatting | bytes 4456448
  121.8 31.8 %all-to-all-done.1 = bf16[32,128,512]{2,1,0:T(8,128)(2,1)} async-done(((bf16[32,128,512]{2,1,0:T(8,128)(2,1)}), bf16[32,128,512]{2,1,0:T(8,128)(2,1)}, u32[]{:S(2)}, u32[]{:S(2)}) %all-to-all-start.1) | async-done | bytes 4194336 | tf_op jit(solution)/shard_map/all_to_all | solution.py:74
  153.6 121.2 %while.11 = (s32[]{:T(128)}, bf16[4,16,512]{2,1,0:T(8,128)(2,1)S(1)}, s32[4,16,128]{2,1,0:T(8,128)}, f32[16]{0:T(128)S(1)}, s32[4,16,128]{2,1,0:T(8,128)S(1)}, /...) while((s32[]{:T(128)}, ...), condition=%wide.region_5.6_spmd.clone, body=%wide.region_1.5_spmd.clone.sunk | while | flops 9598978 | bytes 46301384 | solution.py:92
  153.6 12.0 %gather_fusion = bf16[2048,512]{1,0:T(8,128)(2,1)} fusion(bf16[4096,512]{1,0:T(8,128)(2,1)} %get-tuple-element.219, s32[2048]{0:T(1024)S(1)} %get-tuple-element.188), kind=kCustom, calls=%fused_computation.1.clone.clone.1 | custom fusion | bytes 4202496 | tf_op jit(solution)/shard_map/while/body/eval_jaxpr/jit(_take)/gather | solution.py:85
  165.6 3.4 %select_convert_fusion.4 = f32[16,128,512]{2,1,0:T(8,128)} fusion(bf16[16,128,512]{2,1,0:T(8,128)(2,1)} %bitcast.69, pred[16,128]{1,0:T(8,128)(4,1)S(1)} %get-tuple-element.189), kind=kLoop, calls=%fused_computation.9.clone.1 | loop fusion | flops 2097152 | bytes 6293504 | tf_op jit(solution)/shard_map/while/body/eval_jaxpr/convert_element_type | solution.py:45
  169.0 11.2 %gather_fusion.1 = bf16[2048,512]{1,0:T(8,128)(2,1)} fusion(bf16[2176,512]{1,0:T(8,128)(2,1)} %get-tuple-element.217, s32[2048]{0:T(1024)S(1)} %get-tuple-element.190), kind=kCustom, calls=%fused_computation.clone.clone.1 | custom fusion | bytes 4202496 | tf_op jit(solution)/shard_map/while/body/eval_jaxpr/jit(_take)/gather | solution.py:84
  180.2 1.9 select_convert_fusion.5
  183.9 12.0 %gather_fusion = bf16[2048,512]{1,0:T(8,128)(2,1)} fusion(bf16[4096,512]{1,0:T(8,128)(2,1)} %get-tuple-element.219, s32[2048]{0:T(1024)S(1)} %get-tuple-element.188), kind=kCustom, calls=%fused_computation.1.clone.clone.1 | custom fusion | bytes 4202496 | tf_op jit(solution)/shard_map/while/body/eval_jaxpr/jit(_take)/gather | solution.py:85
  195.9 3.4 %select_convert_fusion.4 = f32[16,128,512]{2,1,0:T(8,128)} fusion(bf16[16,128,512]{2,1,0:T(8,128)(2,1)} %bitcast.69, pred[16,128]{1,0:T(8,128)(4,1)S(1)} %get-tuple-element.189), kind=kLoop, calls=%fused_computation.9.clone.1 | loop fusion | flops 2097152 | bytes 6293504 | tf_op jit(solution)/shard_map/while/body/eval_jaxpr/convert_element_type | solution.py:45
  199.3 11.2 %gather_fusion.1 = bf16[2048,512]{1,0:T(8,128)(2,1)} fusion(bf16[2176,512]{1,0:T(8,128)(2,1)} %get-tuple-element.217, s32[2048]{0:T(1024)S(1)} %get-tuple-element.190), kind=kCustom, calls=%fused_computation.clone.clone.1 | custom fusion | bytes 4202496 | tf_op jit(solution)/shard_map/while/body/eval_jaxpr/jit(_take)/gather | solution.py:84
  210.5 1.9 select_convert_fusion.5
  214.2 12.0 %gather_fusion = bf16[2048,512]{1,0:T(8,128)(2,1)} fusion(bf16[4096,512]{1,0:T(8,128)(2,1)} %get-tuple-element.219, s32[2048]{0:T(1024)S(1)} %get-tuple-element.188), kind=kCustom, calls=%fused_computation.1.clone.clone.1 | custom fusion | bytes 4202496 | tf_op jit(solution)/shard_map/while/body/eval_jaxpr/jit(_take)/gather | solution.py:85
  226.2 3.4 %select_convert_fusion.4 = f32[16,128,512]{2,1,0:T(8,128)} fusion(bf16[16,128,512]{2,1,0:T(8,128)(2,1)} %bitcast.69, pred[16,128]{1,0:T(8,128)(4,1)S(1)} %get-tuple-element.189), kind=kLoop, calls=%fused_computation.9.clone.1 | loop fusion | flops 2097152 | bytes 6293504 | tf_op jit(solution)/shard_map/while/body/eval_jaxpr/convert_element_type | solution.py:45
  229.7 11.2 %gather_fusion.1 = bf16[2048,512]{1,0:T(8,128)(2,1)} fusion(bf16[2176,512]{1,0:T(8,128)(2,1)} %get-tuple-element.217, s32[2048]{0:T(1024)S(1)} %get-tuple-element.190), kind=kCustom, calls=%fused_computation.clone.clone.1 | custom fusion | bytes 4202496 | tf_op jit(solution)/shard_map/while/body/eval_jaxpr/jit(_take)/gather | solution.py:84
  240.8 1.9 select_convert_fusion.5
  244.5 12.0 %gather_fusion = bf16[2048,512]{1,0:T(8,128)(2,1)} fusion(bf16[4096,512]{1,0:T(8,128)(2,1)} %get-tuple-element.219, s32[2048]{0:T(1024)S(1)} %get-tuple-element.188), kind=kCustom, calls=%fused_computation.1.clone.clone.1 | custom fusion | bytes 4202496 | tf_op jit(solution)/shard_map/while/body/eval_jaxpr/jit(_take)/gather | solution.py:85
  256.5 3.4 %select_convert_fusion.4 = f32[16,128,512]{2,1,0:T(8,128)} fusion(bf16[16,128,512]{2,1,0:T(8,128)(2,1)} %bitcast.69, pred[16,128]{1,0:T(8,128)(4,1)S(1)} %get-tuple-element.189), kind=kLoop, calls=%fused_computation.9.clone.1 | loop fusion | flops 2097152 | bytes 6293504 | tf_op jit(solution)/shard_map/while/body/eval_jaxpr/convert_element_type | solution.py:45
  260.0 11.2 %gather_fusion.1 = bf16[2048,512]{1,0:T(8,128)(2,1)} fusion(bf16[2176,512]{1,0:T(8,128)(2,1)} %get-tuple-element.217, s32[2048]{0:T(1024)S(1)} %get-tuple-element.190), kind=kCustom, calls=%fused_computation.clone.clone.1 | custom fusion | bytes 4202496 | tf_op jit(solution)/shard_map/while/body/eval_jaxpr/jit(_take)/gather | solution.py:84
  271.1 1.9 select_convert_fusion.5
  (59 shorter events, 12.5 us)
Async XLA Ops:
  0.0 17.1 %copy-start = (bf16[2048,512]{1,0:T(8,128)(2,1)S(1)}, bf16[2048,512]{1,0:T(8,128)(2,1)}, u32[]{:S(2)}) copy-start(bf16[2048,512]{1,0:T(8,128)(2,1)} %param.9) | copy-start | bytes 6291460
  3.5 21.2 %all-to-all-start = ((s32[32,1,128]{2,1,0:T(1,128)}), s32[32,1,128]{2,1,0:T(1,128)S(1)}, u32[]{:S(2)}, u32[]{:S(2)}) async-start(s32[32,1,128]{2,1,0:T(1,128)} %bitcast.8), calls=%async_computation | async-start | bytes 32768 | tf_op jit(solution)/shard_map/all_to_all | solution.py:70
  48.0 16.6 %copy-start.3 = (s32[64,128]{1,0:T(8,128)S(1)}, s32[64,128]{1,0:T(8,128)}, u32[]{:S(2)}) copy-start(s32[64,128]{1,0:T(8,128)} %param.11) | copy-start | bytes 98308
  48.0 105.6 %all-to-all-start.1 = ((bf16[32,128,512]{2,1,0:T(8,128)(2,1)}), bf16[32,128,512]{2,1,0:T(8,128)(2,1)}, u32[]{:S(2)}, u32[]{:S(2)}) async-start(bf16[32,128,512]{2,1,0:T(8,128)(2,1)} %broadcast_select_fusion), calls=%async_computation.1 | async-start | bytes 8388608 | tf_op jit(solution)/shard_map/all_to_all | solution.py:74
  58.8 53.5 %collective-permute-start = (bf16[64,512]{0,1:T(8,128)(2,1)}, bf16[64,512]{0,1:T(8,128)(2,1)S(1)}, u32[]{:S(2)}, u32[]{:S(2)}) collective-permute-start(bf16[64,512]{0,1:T(8,128)(2,1)} %get-tuple-element.126), channel_id=1, source_target_pairs={{0,1},{1,2},{2,3},{3,4},{4,5},{5,6},{6,7},{8,9},{9,10},{10,11},{11... | collective-permute-start | bytes 196616 | tf_op jit(solution)/shard_map/ppermute | solution.py:18
  60.7 51.6 %collective-permute-start.1 = (bf16[64,512]{0,1:T(8,128)(2,1)}, bf16[64,512]{0,1:T(8,128)(2,1)S(1)}, u32[]{:S(2)}, u32[]{:S(2)}) collective-permute-start(bf16[64,512]{0,1:T(8,128)(2,1)} %get-tuple-element.125), channel_id=1, source_target_pairs={{1,0},{2,1},{3,2},{4,3},{5,4},{6,5},{7,6},{9,8},{10,9},{11,10},{12... | collective-permute-start | bytes 196616 | tf_op jit(solution)/shard_map/ppermute | solution.py:19
  117.6 36.0 %copy-start.2 = (s32[64,128]{1,0:T(8,128)S(1)}, s32[64,128]{1,0:T(8,128)}, u32[]{:S(2)}) copy-start(s32[64,128]{1,0:T(8,128)} %param.10) | copy-start | bytes 98308
  117.6 36.0 %copy-start.4 = (f32[16]{0:T(128)S(1)}, f32[16]{0:T(128)}, u32[]{:S(2)}) copy-start(f32[16]{0:T(128)} %param.15) | copy-start | bytes 196
  180.2 2.8 %copy-start.1 = (f32[16,128,512]{2,1,0:T(8,128)S(1)}, f32[16,128,512]{2,1,0:T(8,128)}, u32[]{:S(2)}) copy-start(f32[16,128,512]{2,1,0:T(8,128)} %select_convert_fusion.4) | copy-start | bytes 12582916 | tf_op jit(solution)/shard_map/while
  210.5 2.8 %copy-start.1 = (f32[16,128,512]{2,1,0:T(8,128)S(1)}, f32[16,128,512]{2,1,0:T(8,128)}, u32[]{:S(2)}) copy-start(f32[16,128,512]{2,1,0:T(8,128)} %select_convert_fusion.4) | copy-start | bytes 12582916 | tf_op jit(solution)/shard_map/while
  240.8 2.8 %copy-start.1 = (f32[16,128,512]{2,1,0:T(8,128)S(1)}, f32[16,128,512]{2,1,0:T(8,128)}, u32[]{:S(2)}) copy-start(f32[16,128,512]{2,1,0:T(8,128)} %select_convert_fusion.4) | copy-start | bytes 12582916 | tf_op jit(solution)/shard_map/while
  271.1 2.8 %copy-start.1 = (f32[16,128,512]{2,1,0:T(8,128)S(1)}, f32[16,128,512]{2,1,0:T(8,128)}, u32[]{:S(2)}) copy-start(f32[16,128,512]{2,1,0:T(8,128)} %select_convert_fusion.4) | copy-start | bytes 12582916 | tf_op jit(solution)/shard_map/while
where the time goes:
time: 277 us; the launch traced here: 276 us
  local copies, waits for them, and re-layouts  178 us (64%)
  other arithmetic  35.1 us (13%)
  waiting for transfers between devices  32.9 us (12%)
  starting transfers between devices  26.2 us (9%)
  matrix products  3.54 us (1%)
    gather x4, local copies, waits for them, and re-layouts, one_block(): rcv_rows = jnp.take(arrived, r_idx, axis=0)  47.9 us
    gather x1, local copies, waits for them, and re-layouts, body(): rcv_rows_index = jnp.take(slot_map, rcv_index, axis=0)  45.5 us
    gather x4, local copies, waits for them, and re-layouts, one_block(): src_rows = jnp.take(widened, s_idx, axis=0)  44.6 us
    all_to_all x1, waiting for transfers between devices, body(): lax.all_to_all(outgoing, 'sail', split_axis=0, concat_axis=0, tiled=True)  31.8 us
    gather x1, local copies, waits for them, and re-layouts, body(): jnp.take(own_spectra, asked.reshape(-1), axis=0)  19.3 us
    convert_element_type x4, other arithmetic, predict_block(): right = rcv_rows.astype(jnp.float32)  13.8 us
    all_to_all x1, starting transfers between devices, body(): lax.all_to_all(by_peer, 'sail', split_axis=0, concat_axis=0, tiled=True)  11.5 us
    all_to_all x1, starting transfers between devices, body(): lax.all_to_all(outgoing, 'sail', split_axis=0, concat_axis=0, tiled=True)  9.02 us
  transfers between devices with their start and end apart: 4, of which 2 were waited for; matrix products, arithmetic and copies ran while one was open for 25% of the time, Pallas kernels for 0%

commit v1 on v0

v1 whole, which is shorter than its diff:
```python
import functools
import math

import jax
import jax.numpy as jnp
from jax import lax
from jax.experimental import pallas as pl
from jax.experimental.pallas import tpu as pltpu
from jax.sharding import PartitionSpec as P

HALO = 64
DISTINCT = 64
F32 = jnp.float32
BF16 = jnp.bfloat16


def forward_table(samples):
    times = jnp.arange(samples, dtype=jnp.int32)
    freqs = jnp.arange(samples // 2, dtype=jnp.int32)
    turns = times[:, None] * freqs[None, :] % samples
    angle = turns.astype(jnp.float32) * (2.0 * math.pi / samples)
    scale = 1.0 / math.sqrt(samples)
    return (jnp.concatenate([jnp.cos(angle), -jnp.sin(angle)], axis=1) * scale).astype(jnp.bfloat16)


def synthesis_table(samples, aperture):
    freqs = jnp.arange(samples // 2, dtype=jnp.int32)
    times = jnp.arange(samples, dtype=jnp.int32)
    turns = freqs[:, None] * times[None, :] % samples
    angle = turns.astype(jnp.float32) * (2.0 * math.pi / samples)
    scale = 1.0 / math.sqrt(aperture * (samples // 2))
    return (jnp.concatenate([jnp.cos(angle), -jnp.sin(angle)], axis=0) * scale).astype(jnp.bfloat16)


def distinct_kernel(owner_ref, rows_ref, asked_ref, place_ref):
    lines, cap = rows_ref.shape
    rows = rows_ref[...]
    sub = lax.broadcasted_iota(jnp.int32, (cap, cap), 0)
    lane = lax.broadcasted_iota(jnp.int32, (cap, cap), 1)
    pad = jnp.zeros((cap - lines, cap), jnp.int32)

    def turned(values):
        return jnp.concatenate([values, pad], axis=0).T

    columns = turned(rows)
    once = []
    for g in range(lines):
        column = columns[:, g : g + 1]
        row = rows[g : g + 1, :]
        repeats = jnp.sum(((column == row) & (sub < lane)).astype(jnp.int32), axis=0, keepdims=True)
        once.append(jnp.where(repeats == 0, row, 1 << 20))
    once_columns = turned(jnp.concatenate(once, axis=0))
    ranks = []
    for g in range(lines):
        smaller = (once_columns[:, g : g + 1] < rows[g : g + 1, :]).astype(jnp.int32)
        ranks.append(jnp.sum(smaller, axis=0, keepdims=True))
    rank_columns = turned(jnp.concatenate(ranks, axis=0))
    for g in range(lines):
        match = rank_columns[:, g : g + 1] == lane
        picked = jnp.max(jnp.where(match, columns[:, g : g + 1], 0), axis=0, keepdims=True)
        asked_ref[owner_ref[g]] = picked
        place_ref[g : g + 1, :] = ranks[g] + owner_ref[g] * DISTINCT


def quarters(block):
    return [block[:, 128 * q : 128 * (q + 1)] for q in range(4)]


def put_sources(wide_ref, start, block):
    r0, r1, i0, i1 = quarters(block)
    for j, piece in enumerate((r0, r1, i0, i1, i0, i1, r0, r1)):
        wide_ref[pl.ds(start * 8 + j, block.shape[0], stride=8), :] = piece


def forward_kernel(traces_ref, table_ref, wide_ref, first_ref, last_ref):
    rows = traces_ref.shape[0]
    step = 256

    def one(b, _):
        at = pl.multiple_of(b * step, step)
        spectra = jnp.dot(
            traces_ref[pl.ds(at, step), :], table_ref[...], preferred_element_type=F32
        ).astype(BF16)
        put_sources(wide_ref, at, spectra.astype(F32))

        @pl.when(b == 0)
        def _():
            first_ref[...] = spectra[:HALO]

        @pl.when(b == rows // step - 1)
        def _():
            last_ref[...] = spectra[step - HALO :]

        return 0

    lax.fori_loop(0, rows // step, one, 0)


def fetch_kernel(asked_ref, wide_ref, out_ref, held_ref):
    peers = asked_ref.shape[0]
    sub = lax.broadcasted_iota(jnp.int32, (8, 128), 0)

    def one(p, _):
        base = pl.multiple_of(p * (DISTINCT * 4), DISTINCT * 4)
        for k in range(0, DISTINCT, 2):
            a = wide_ref[asked_ref[p, 0, k]]
            b = pltpu.roll(wide_ref[asked_ref[p, 0, k + 1]], 4, 0)
            held_ref[pl.ds(base + 4 * k, 8), :] = jnp.where(sub < 4, a, b)
        out_ref[pl.ds(base, DISTINCT * 4), :] = held_ref[pl.ds(base, DISTINCT * 4), :].astype(BF16)
        return 0

    lax.fori_loop(0, peers, one, 0)


def slots_kernel(place_ref, rcv_ref, out_ref):
    outs, aper = rcv_ref.shape

    def one(o, _):
        for a in range(aper):
            slot = rcv_ref[o, a]
            out_ref[o, a] = place_ref[slot]
        return 0

    lax.fori_loop(0, outs, one, 0)


def pairs_kernel(
    src_ref, rcv_ref, weight_ref, wide_ref, before_ref, after_ref, arrived_ref, synth_ref, out_ref,
    source_ref, receiver_ref, sum_ref, sem,
):
    outs, aper = src_ref.shape
    own = wide_ref.shape[0] // 8
    copy = pltpu.make_async_copy(wide_ref, source_ref.at[pl.ds(HALO * 8, own * 8)], sem)
    copy.start()
    put_sources(source_ref, 0, before_ref[...].astype(F32))
    put_sources(source_ref, own + HALO, after_ref[...].astype(F32))
    step = 64
    sub = lax.broadcasted_iota(jnp.int32, (8, 128), 0)

    def widen(b, _):
        at = pl.multiple_of(b * (step * 4), step * 4)
        rows = arrived_ref[pl.ds(at, step * 4), :].astype(F32)
        for k in range(0, step, 2):
            x = rows[4 * k : 4 * k + 8]
            y = pltpu.roll(x, 4, 0)
            to = pl.multiple_of(at * 2, step * 8) + 8 * k
            receiver_ref[pl.ds(to, 8), :] = jnp.where(sub < 4, x, y)
            receiver_ref[pl.ds(to + 8, 8), :] = jnp.where(sub < 4, y, x)
        return 0

    lax.fori_loop(0, arrived_ref.shape[0] // (step * 4), widen, 0)
    copy.wait()

    def one(o, _):
        totals = [jnp.zeros((8, 128), F32) for _ in range(4)]

        def some(c, totals):
            totals = list(totals)
            for u in range(16):
                a = c * 16 + u
                s = source_ref[pl.ds(pl.multiple_of(src_ref[o, a], 8), 8), :]
                r = receiver_ref[pl.ds(pl.multiple_of(rcv_ref[o, a], 8), 8), :]
                totals[u % 4] += (s * r) * weight_ref[o, a]
            return tuple(totals)

        totals = lax.fori_loop(0, aper // 16, some, tuple(totals))
        total = (totals[0] + totals[1]) + (totals[2] + totals[3])
        sum_ref[o] = total
        return 0

    lax.fori_loop(0, outs, one, 0)
    pieces = [sum_ref[:, j, :] for j in range(8)]
    summed = jnp.concatenate(
        [pieces[0] - pieces[2], pieces[1] - pieces[3], pieces[4] + pieces[6], pieces[5] + pieces[7]],
        axis=1,
    ).astype(BF16)
    out_ref[...] = jnp.dot(summed, synth_ref[...], preferred_element_type=F32).astype(BF16)


VMEM = pl.BlockSpec(memory_space=pltpu.VMEM)
SMEM = pl.BlockSpec(memory_space=pltpu.SMEM)
ANY = pl.BlockSpec(memory_space=pl.ANY)


def shape(dims, kind):
    return jax.ShapeDtypeStruct(dims, kind)


def params(mib):
    return pltpu.CompilerParams(vmem_limit_bytes=mib << 20)


def body(traces, src_index, rcv_index, taper_index, fetch_rows, line_owner, taper_table):
    sails = lax.axis_size("sail")
    cables = lax.axis_size("cable")
    tr_rows, samples = traces.shape
    outs, aper = src_index.shape
    cap = fetch_rows.shape[1]
    asked, place = pl.pallas_call(
        distinct_kernel,
        in_specs=[SMEM, VMEM],
        out_specs=[VMEM, VMEM],
        out_shape=[shape((sails, 1, cap), jnp.int32), shape((sails, cap), jnp.int32)],
        compiler_params=params(8),
        name="distinct",
    )(line_owner, fetch_rows)
    asked = lax.all_to_all(asked, "sail", split_axis=0, concat_axis=0, tiled=True)
    wide, first, last = pl.pallas_call(
        forward_kernel,
        in_specs=[VMEM, VMEM],
        out_specs=[VMEM, VMEM, VMEM],
        out_shape=[
            shape((tr_rows * 8, 128), F32),
            shape((HALO, samples), BF16),
            shape((HALO, samples), BF16),
        ],
        compiler_params=params(24),
        name="forward",
        cost_estimate=pl.CostEstimate(
            flops=2 * tr_rows * samples * samples, bytes_accessed=12 << 20, transcendentals=0
        ),
    )(traces, forward_table(samples))
    outgoing = pl.pallas_call(
        fetch_kernel,
        in_specs=[SMEM, VMEM],
        out_specs=VMEM,
        out_shape=shape((sails * DISTINCT * 4, 128), BF16),
        scratch_shapes=[pltpu.VMEM((sails * DISTINCT * 4, 128), F32)],
        compiler_params=params(32),
        name="fetch",
    )(asked, wide.reshape(tr_rows, 8, 128))
    arrived = lax.all_to_all(
        outgoing.reshape(sails, DISTINCT * 4, 128), "sail", split_axis=0, concat_axis=0, tiled=True
    ).reshape(sails * DISTINCT * 4, 128)
    up = [(i, i + 1) for i in range(cables - 1)]
    before = lax.ppermute(last, "cable", up)
    after = lax.ppermute(first, "cable", [(j, i) for i, j in up])
    rcv_rows = pl.pallas_call(
        slots_kernel,
        in_specs=[SMEM, SMEM],
        out_specs=SMEM,
        out_shape=shape((outs, aper), jnp.int32),
        name="slots",
        cost_estimate=pl.CostEstimate(flops=0, bytes_accessed=32 << 20, transcendentals=0),
    )(place.reshape(-1) * 8, rcv_index)
    taper_ids = jnp.arange(taper_table.shape[0], dtype=jnp.int32)
    weights = jnp.sum(
        jnp.where(taper_index[..., None] == taper_ids, taper_table, jnp.zeros_like(taper_table)),
        axis=-1,
    )
    return pl.pallas_call(
        pairs_kernel,
        in_specs=[SMEM, SMEM, SMEM, ANY, VMEM, VMEM, VMEM, VMEM],
        out_specs=VMEM,
        out_shape=shape((outs, samples), BF16),
        scratch_shapes=[
            pltpu.VMEM(((tr_rows + 2 * HALO) * 8, 128), F32),
            pltpu.VMEM((sails * DISTINCT * 8, 128), F32),
            pltpu.VMEM((outs, 8, 128), F32),
            pltpu.SemaphoreType.DMA,
        ],
        compiler_params=params(32),
        name="pairs",
    )(src_index * 8, rcv_rows, weights, wide, before, after, arrived, synthesis_table(samples, aper))


def solution(mesh):
    split = P(("sail", "cable"), None)
    return jax.shard_map(
        body,
        mesh=mesh,
        in_specs=(split, split, split, split, split, P(), P()),
        out_specs=split,
        check_vma=False,
    )
```

time: 277 us -> 133 us (0.48)
  local copies, waits for them, and re-layouts: 178 us -> 11.4 us
  Pallas kernels: 0 us -> 63.9 us
  other arithmetic: 35.1 us -> 5.18 us
  waiting for transfers between devices: 32.9 us -> 26.3 us
  matrix products: 3.54 us -> 0 us
    gather x11 -> x0, local copies, waits for them, and re-layouts: 159 us -> none  [the longest x4 47.9 us: one_block(): rcv_rows = jnp.take(arrived, r_idx, axis=0)]
    pallas_call x0 -> x5, Pallas kernels: none -> 63.9 us  [the longest x1 37 us: body(): pl.pallas_call(pairs_kernel, in_specs=[SMEM, SMEM, SMEM, ANY, VMEM, VMEM,...]
    convert_element_type x8 -> x2, other arithmetic: 21.5 us -> 0.21 us  [the longest x1 0.13 us: synthesis_table(): (jnp.concatenate([jnp.cos(angle), -jnp.sin(angle)], axis=0) * scale).asty...]
    unnamed x9 -> x20, local copies, waits for them, and re-layouts: 4.17 us -> 11.4 us
    all_to_all x2, waiting for transfers between devices: 32.8 us -> 26.3 us  [the longest x1 25.3 us: body(): lax.all_to_all(outgoing.reshape(sails, DISTINCT * 4, 128), 'sail', split_...]
    select_n x6 -> x0, other arithmetic: 5.44 us -> none  [the longest x2 3.94 us: body(): jnp.take(own_spectra, asked.reshape(-1), axis=0)]
    concatenate x1 -> x0, local copies, waits for them, and re-layouts: 5.3 us -> none  [with_halo(): shard = jnp.concatenate([before, shard, after], axis=dim)]
    convert_element_type x1 -> x0, local copies, waits for them, and re-layouts: 3.91 us -> none  [body(): jnp.dot(traces, forward, preferred_element_type=jnp.float32)]
  transfers between devices with their start and end apart: 4 -> 4, of which waited for: 2 -> 2; matrix products, arithmetic and copies ran while one was open for 25% -> 4% of each run, Pallas kernels for 0% -> 14%
where the time goes in v1:
time: 133 us
  Pallas kernels  63.9 us (48%)
  waiting for transfers between devices  26.3 us (20%)
  starting transfers between devices  26 us (20%)
  local copies, waits for them, and re-layouts  11.4 us (9%)
  other arithmetic  5.18 us (4%)
    pallas_call x1, Pallas kernels, body(): pl.pallas_call(pairs_kernel, in_specs=[SMEM, SMEM, SMEM, ANY, VMEM, VMEM,...  37 us
    all_to_all x1, waiting for transfers between devices, body(): lax.all_to_all(outgoing.reshape(sails, DISTINCT * 4, 128), 'sail', split_...  25.3 us
    pallas_call x1, Pallas kernels, body(): pl.pallas_call(slots_kernel, in_specs=[SMEM, SMEM], out_specs=SMEM, out_s...  15.6 us
    all_to_all x1, starting transfers between devices, body(): lax.all_to_all(asked, 'sail', split_axis=0, concat_axis=0, tiled=True)  11.5 us
    unnamed x20, local copies, waits for them, and re-layouts  11.4 us
    all_to_all x1, starting transfers between devices, body(): lax.all_to_all(outgoing.reshape(sails, DISTINCT * 4, 128), 'sail', split_...  8.95 us
    pallas_call x1, Pallas kernels, body(): pl.pallas_call(fetch_kernel, in_specs=[SMEM, VMEM], out_specs=VMEM, out_s...  4.57 us
    ppermute x1, starting transfers between devices, body(): after = lax.ppermute(first, 'cable', [(j, i) for i, j in up])  3.64 us
  transfers between devices with their start and end apart: 4, of which 2 were waited for; matrix products, arithmetic and copies ran while one was open for 4% of the time, Pallas kernels for 14%

profile of v1, /device:TPU:4, one launch (start us, length us, event | category | flops | bytes accessed | tf_op | source)
XLA Modules:
  0.0 132.9 jit_solution(4690945124557419325)
XLA Ops:
  0.0 0.7 copy-done.4
  0.7 0.7 copy-done.5
  1.4 3.4 %distinct.1 = (s32[32,1,128]{2,1,0:T(1,128)}, s32[32,128]{1,0:T(8,128)S(1)}) custom-call(s32[32]{0:T(128)S(1)} %copy-done.5, s32[32,128]{1,0:T(8,128)S(1)} %copy-done.4), custom_call_target="tpu_custom_call" | custom-call | tf_op jit(solution)/shard_map/distinct/pallas_call | solution.py:199
  4.7 11.5 %all-to-all-start = ((s32[32,1,128]{2,1,0:T(1,128)}), s32[32,1,128]{2,1,0:T(1,128)S(1)}, u32[]{:S(2)}, u32[]{:S(2)}) async-start(s32[32,1,128]{2,1,0:T(1,128)} %get-tuple-element.14), calls=%async_computation | async-start | bytes 32768 | tf_op jit(solution)/shard_map/all_to_all | solution.py:207
  16.2 0.0 copy-start.6
  16.2 2.1 %sine_negate_fusion.1 = (f32[512,256]{1,0:T(8,128)S(1)}, f32[512,256]{1,0:T(8,128)S(1)}) fusion(), kind=kLoop, calls=%fused_computation.19 | loop fusion | flops 1966080 | bytes 1048576 | tf_op jit(solution)/shard_map/neg | solution.py:23
  18.3 0.1 fusion.table_ref
  18.4 0.0 copy-done.6
  18.4 3.3 %forward.1 = (f32[16384,128]{1,0:T(8,128)S(1)}, bf16[64,512]{1,0:T(8,128)(2,1)S(1)}, bf16[64,512]{1,0:T(8,128)(2,1)S(1)}) custom-call(bf16[2048,512]{1,0:T(8,128)(2,1)S(1)} %copy-done.6, bf16[512,512]{1,0:T(8,128)(2,1)S(1)} %fusion.table_ref), custom_call_target="tpu_custom_call" | custom-call | flops 1073741824 | bytes 12582912 | tf_op jit(solution)/shard_map/forward/pallas_call | solution.py:208
  21.7 0.0 copy-start
  21.8 3.2 %copy-done = f32[16384,128]{1,0:T(8,128)} copy-done((f32[16384,128]{1,0:T(8,128)}, f32[16384,128]{1,0:T(8,128)S(1)}, u32[]{:S(2)}) %copy-start) | copy-done | bytes 8388632
  25.0 1.0 all-to-all-done.asked_ref
  25.9 3.4 %copy-done.1 = f32[16384,128]{1,0:T(8,128)S(1)} copy-done((f32[16384,128]{1,0:T(8,128)S(1)}, f32[16384,128]{1,0:T(8,128)}, u32[]{:S(2)}) %copy-start.1) | copy-done | bytes 8388632
  29.3 4.6 %fetch.1 = bf16[8192,128]{1,0:T(8,128)(2,1)} custom-call(s32[32,1,128]{2,1,0:T(1,128)S(1)} %all-to-all-done.asked_ref, f32[2048,8,128]{2,1,0:T(8,128)S(1)} %bitcast.5), custom_call_target="tpu_custom_call" | custom-call | tf_op jit(solution)/shard_map/fetch/pallas_call | solution.py:223
  33.9 8.9 %all-to-all-start.1 = ((bf16[32,256,128]{2,1,0:T(8,128)(2,1)}), bf16[32,256,128]{2,1,0:T(8,128)(2,1)S(1)}, u32[]{:S(2)}, u32[]{:S(2)}) async-start(bf16[32,256,128]{2,1,0:T(8,128)(2,1)} %bitcast.2), calls=%async_computation.1 | async-start | bytes 4194304 | tf_op jit(solution)/shard_map/all_to_all | solution.py:232
  42.9 1.9 %collective-permute-start = (bf16[64,512]{1,0:T(8,128)(2,1)S(1)}, bf16[64,512]{1,0:T(8,128)(2,1)S(1)}, u32[]{:S(2)}, u32[]{:S(2)}) collective-permute-start(bf16[64,512]{1,0:T(8,128)(2,1)S(1)} %get-tuple-element.12), channel_id=1, source_target_pairs={{0,1},{1,2},{2,3},{3,4},{4,5},{5,6},{6,7},{8,9},{9,10},{10,11},{11... | collective-permute-start | bytes 196616 | tf_op jit(solution)/shard_map/ppermute | solution.py:236
  44.8 3.6 %collective-permute-start.1 = (bf16[64,512]{1,0:T(8,128)(2,1)S(1)}, bf16[64,512]{1,0:T(8,128)(2,1)S(1)}, u32[]{:S(2)}, u32[]{:S(2)}) collective-permute-start(bf16[64,512]{1,0:T(8,128)(2,1)S(1)} %get-tuple-element.13), channel_id=1, source_target_pairs={{1,0},{2,1},{3,2},{4,3},{5,4},{6,5},{7,6},{9,8},{10,9},{11,10},{12... | collective-permute-start | bytes 196616 | tf_op jit(solution)/shard_map/ppermute | solution.py:237
  48.4 0.6 multiply_bitcast_fusion.place_ref
  49.0 15.6 %slots.1.rcv_ref = s32[64,128]{1,0:T(8,128)} custom-call(s32[4096]{0:T(1024)} %multiply_bitcast_fusion.place_ref, s32[64,128]{1,0:T(8,128)} %rcv_ref.1), custom_call_target="tpu_custom_call" | custom-call | bytes 33554432 | tf_op jit(solution)/shard_map/slots/pallas_call | solution.py:238
  64.7 0.0 copy-done.7
  64.7 0.0 copy-done.9
  64.7 0.0 copy-start.3
  64.7 0.2 select_reduce_fusion.weight_ref
  64.9 2.1 %sine_negate_fusion = (f32[256,512]{1,0:T(8,128)S(1)}, f32[256,512]{1,0:T(8,128)S(1)}) fusion(), kind=kLoop, calls=%fused_computation.16 | loop fusion | flops 1966080 | bytes 1048576 | tf_op jit(solution)/shard_map/neg | solution.py:32
  67.0 0.0 copy-done.8
  67.0 0.1 fusion.1.synth_ref
  67.2 0.0 collective-permute-done.before_ref
  67.2 0.0 collective-permute-done.1.after_ref
  67.2 25.3 %all-to-all-done.1 = bf16[32,256,128]{2,1,0:T(8,128)(2,1)S(1)} async-done(((bf16[32,256,128]{2,1,0:T(8,128)(2,1)}), bf16[32,256,128]{2,1,0:T(8,128)(2,1)S(1)}, u32[]{:S(2)}, u32[]{:S(2)}) %all-to-all-start.1) | async-done | bytes 2097184 | tf_op jit(solution)/shard_map/all_to_all | solution.py:232
  92.5 0.0 copy-done.3
  92.5 3.4 %copy-done.2 = f32[16384,128]{1,0:T(8,128)S(1)} copy-done((f32[16384,128]{1,0:T(8,128)S(1)}, f32[16384,128]{1,0:T(8,128)}, u32[]{:S(2)}) %copy-start.2) | copy-done | bytes 8388632
  95.9 37.0 %pairs.1 = bf16[64,512]{1,0:T(8,128)(2,1)} custom-call(s32[64,128]{1,0:T(8,128)S(1)} %broadcast_multiply_fusion.src_ref, s32[64,128]{1,0:T(8,128)S(1)} %copy-done.3, f32[64,128]{1,0:T(8,128)S(1)} %select_reduce_fusion.weight_ref, f32[16384,128]{1,0:T(8,128)S(1)} %copy-done.2, bf16[64,512]{1,0:T(8,128)(2,1)S(1)} %collective-permute-done.before_ref, ...), custom_call_target="tpu_custom_call" | custom-call | tf_op jit(solution)/shard_map/pairs/pallas_call | solution.py:251
  (8 shorter events, 0.0 us)
Async XLA Ops:
  0.0 0.7 copy-start.4
  0.7 0.7 copy-start.5
  4.7 21.2 %all-to-all-start = ((s32[32,1,128]{2,1,0:T(1,128)}), s32[32,1,128]{2,1,0:T(1,128)S(1)}, u32[]{:S(2)}, u32[]{:S(2)}) async-start(s32[32,1,128]{2,1,0:T(1,128)} %get-tuple-element.14), calls=%async_computation | async-start | bytes 32768 | tf_op jit(solution)/shard_map/all_to_all | solution.py:207
  16.2 2.2 %copy-start.6 = (bf16[2048,512]{1,0:T(8,128)(2,1)S(1)}, bf16[2048,512]{1,0:T(8,128)(2,1)}, u32[]{:S(2)}) copy-start(bf16[2048,512]{1,0:T(8,128)(2,1)} %traces_ref.1) | copy-start | bytes 6291460
  21.7 3.2 %copy-start = (f32[16384,128]{1,0:T(8,128)}, f32[16384,128]{1,0:T(8,128)S(1)}, u32[]{:S(2)}) copy-start(f32[16384,128]{1,0:T(8,128)S(1)} %get-tuple-element.11.wide_ref) | copy-start | bytes 25165828
  25.9 3.4 %copy-start.1 = (f32[16384,128]{1,0:T(8,128)S(1)}, f32[16384,128]{1,0:T(8,128)}, u32[]{:S(2)}) copy-start(f32[16384,128]{1,0:T(8,128)} %copy-done) | copy-start | bytes 25165828
  33.9 30.8 %copy-start.7 = (s32[64,128]{1,0:T(8,128)S(1)}, s32[64,128]{1,0:T(8,128)}, u32[]{:S(2)}) copy-start(s32[64,128]{1,0:T(8,128)} %param.10) | copy-start | bytes 98308
  33.9 30.8 %copy-start.9 = (f32[16]{0:T(128)S(1)}, f32[16]{0:T(128)}, u32[]{:S(2)}) copy-start(f32[16]{0:T(128)} %param.13) | copy-start | bytes 196
  33.9 33.1 %copy-start.8 = (s32[64,128]{1,0:T(8,128)S(1)}, s32[64,128]{1,0:T(8,128)}, u32[]{:S(2)}) copy-start(s32[64,128]{1,0:T(8,128)} %param.8) | copy-start | bytes 98308
  33.9 58.6 %all-to-all-start.1 = ((bf16[32,256,128]{2,1,0:T(8,128)(2,1)}), bf16[32,256,128]{2,1,0:T(8,128)(2,1)S(1)}, u32[]{:S(2)}, u32[]{:S(2)}) async-start(bf16[32,256,128]{2,1,0:T(8,128)(2,1)} %bitcast.2), calls=%async_computation.1 | async-start | bytes 4194304 | tf_op jit(solution)/shard_map/all_to_all | solution.py:232
  42.9 24.3 %collective-permute-start = (bf16[64,512]{1,0:T(8,128)(2,1)S(1)}, bf16[64,512]{1,0:T(8,128)(2,1)S(1)}, u32[]{:S(2)}, u32[]{:S(2)}) collective-permute-start(bf16[64,512]{1,0:T(8,128)(2,1)S(1)} %get-tuple-element.12), channel_id=1, source_target_pairs={{0,1},{1,2},{2,3},{3,4},{4,5},{5,6},{6,7},{8,9},{9,10},{10,11},{11... | collective-permute-start | bytes 196616 | tf_op jit(solution)/shard_map/ppermute | solution.py:236
  44.8 22.4 %collective-permute-start.1 = (bf16[64,512]{1,0:T(8,128)(2,1)S(1)}, bf16[64,512]{1,0:T(8,128)(2,1)S(1)}, u32[]{:S(2)}, u32[]{:S(2)}) collective-permute-start(bf16[64,512]{1,0:T(8,128)(2,1)S(1)} %get-tuple-element.13), channel_id=1, source_target_pairs={{1,0},{2,1},{3,2},{4,3},{5,4},{6,5},{7,6},{9,8},{10,9},{11,10},{12... | collective-permute-start | bytes 196616 | tf_op jit(solution)/shard_map/ppermute | solution.py:237
  64.7 27.8 %copy-start.3 = (s32[64,128]{1,0:T(8,128)S(1)}, s32[64,128]{1,0:T(8,128)}, u32[]{:S(2)}) copy-start(s32[64,128]{1,0:T(8,128)} %slots.1.rcv_ref) | copy-start | bytes 98308
  92.5 3.4 %copy-start.2 = (f32[16384,128]{1,0:T(8,128)S(1)}, f32[16384,128]{1,0:T(8,128)}, u32[]{:S(2)}) copy-start(f32[16384,128]{1,0:T(8,128)} %copy-done) | copy-start | bytes 25165828

commit v2 on v1

v2 whole, which is shorter than its diff:
```python
import math

import jax
import jax.numpy as jnp
import ml_dtypes
import numpy as np
from jax import lax
from jax.experimental import pallas as pl
from jax.experimental.pallas import tpu as pltpu
from jax.sharding import PartitionSpec as P

HALO = 64
DISTINCT = 64
PAD = 8
TILE = 256
CHUNKS = 4
F32 = jnp.float32
BF16 = jnp.bfloat16


def forward_table(samples):
    turns = np.arange(samples)[:, None] * np.arange(samples // 2)[None, :] % samples
    angle = turns * (2.0 * math.pi / samples)
    table = np.concatenate([np.cos(angle), -np.sin(angle)], axis=1) / math.sqrt(samples)
    return jnp.asarray(table.astype(np.float32).astype(ml_dtypes.bfloat16))


def synthesis_table(samples, aperture):
    turns = np.arange(samples // 2)[:, None] * np.arange(samples)[None, :] % samples
    angle = turns * (2.0 * math.pi / samples)
    scale = math.sqrt(aperture * (samples // 2))
    table = np.concatenate([np.cos(angle), -np.sin(angle)], axis=0) / scale
    return jnp.asarray(table.astype(np.float32).astype(ml_dtypes.bfloat16))


def distinct_kernel(owner_ref, rows_ref, asked_ref, place_ref):
    lines, cap = rows_ref.shape
    rows = rows_ref[...]
    sub = lax.broadcasted_iota(jnp.int32, (cap, cap), 0)
    lane = lax.broadcasted_iota(jnp.int32, (cap, cap), 1)
    pad = jnp.zeros((cap - lines, cap), jnp.int32)

    def turned(values):
        return jnp.concatenate([values, pad], axis=0).T

    columns = turned(rows)
    once = []
    for g in range(lines):
        column = columns[:, g : g + 1]
        row = rows[g : g + 1, :]
        repeats = jnp.sum(((column == row) & (sub < lane)).astype(jnp.int32), axis=0, keepdims=True)
        once.append(jnp.where(repeats == 0, row, 1 << 20))
    once_columns = turned(jnp.concatenate(once, axis=0))
    ranks = []
    for g in range(lines):
        smaller = (once_columns[:, g : g + 1] < rows[g : g + 1, :]).astype(jnp.int32)
        ranks.append(jnp.sum(smaller, axis=0, keepdims=True))
    rank_columns = turned(jnp.concatenate(ranks, axis=0))
    for g in range(lines):
        match = rank_columns[:, g : g + 1] == lane
        picked = jnp.max(jnp.where(match, columns[:, g : g + 1], 0), axis=0, keepdims=True)
        asked_ref[owner_ref[g]] = picked * 4
        place_ref[g : g + 1, :] = ranks[g] + owner_ref[g] * DISTINCT


def put_rows(ref, start, block):
    for q in range(4):
        at = pl.ds(start + q, block.shape[0], stride=4)
        ref[at, :] = block[:, 128 * q : 128 * (q + 1)]


def forward_kernel(traces_ref, table_ref, rows_ref, first_ref, last_ref):
    step = pl.program_id(0)
    spectra = jnp.dot(traces_ref[...], table_ref[...], preferred_element_type=F32).astype(BF16)
    put_rows(rows_ref, 0, spectra.astype(F32))

    @pl.when(step == 0)
    def _():
        first_ref[...] = spectra[:HALO]

    @pl.when(step == pl.num_programs(0) - 1)
    def _():
        last_ref[...] = spectra[spectra.shape[0] - HALO :]


def gather_rows(index, rows_ref, held_ref, out_ref, base, count):
    sub = lax.broadcasted_iota(jnp.int32, (8, 128), 0)
    for k in range(0, count, 2):
        a = rows_ref[pl.ds(index(k) + PAD, 8), :]
        b = rows_ref[pl.ds(index(k + 1) + PAD - 4, 8), :]
        held_ref[pl.ds(pl.multiple_of(base * 4, 8) + 4 * k, 8), :] = jnp.where(sub < 4, a, b)
    for q in range(4):
        part = held_ref[pl.ds(base * 4 + q, count, stride=4), :]
        out_ref[pl.ds(base, count), 128 * q : 128 * (q + 1)] = part.astype(BF16)


def fetch_kernel(asked_ref, rows_ref, out_ref, own_ref, held_ref, sem):
    own = rows_ref.shape[0]
    copy = pltpu.make_async_copy(rows_ref, own_ref.at[pl.ds(PAD, own)], sem)
    copy.start()
    copy.wait()

    def one(p, _):
        base = pl.multiple_of(p * DISTINCT, DISTINCT)
        gather_rows(lambda k: asked_ref[p, 0, k], own_ref, held_ref, out_ref, base, DISTINCT)
        return 0

    lax.fori_loop(0, asked_ref.shape[0], one, 0)


def slots_kernel(place_ref, src_ref, rcv_ref, taper_ref, key_ref, value_ref):
    lines, cap = place_ref.shape
    outs = rcv_ref.shape[0]
    place = place_ref[...]
    rank = (place & (DISTINCT - 1)).astype(F32).astype(BF16)
    first = (place - (place & (DISTINCT - 1))).astype(F32)
    sub = lax.broadcasted_iota(jnp.int32, (cap, cap), 0)
    line = lax.broadcasted_iota(jnp.int32, (lines, cap), 0)

    def some(b, _):
        at = pl.multiple_of(b * 8, 8)
        slots = rcv_ref[pl.ds(at, 8), :]
        rows = []
        for u in range(8):
            slot = slots[u : u + 1, :]
            at_slot = (sub == (slot & (cap - 1))).astype(F32).astype(BF16)
            found = jnp.dot(rank, at_slot, preferred_element_type=F32) + first
            rows.append(
                jnp.sum(jnp.where(line == slot // cap, found, 0.0), axis=0, keepdims=True)
            )
        rows = jnp.concatenate(rows, axis=0).astype(jnp.int32)
        out = lax.broadcasted_iota(jnp.int32, (8, cap), 0) + at
        key_ref[pl.ds(at, 8), :] = (rows * outs + out) * 16 + taper_ref[pl.ds(at, 8), :]
        value_ref[pl.ds(at, 8), :] = src_ref[pl.ds(at, 8), :] * 4
        return 0

    lax.fori_loop(0, outs // 8, some, 0)


def sources_kernel(
    src_ref, ends_ref, rows_ref, before_ref, after_ref, out_ref, tile_ref, block_ref, all_ref, held_ref, sem
):
    step = pl.program_id(0)

    @pl.when(step == 0)
    def _():
        own = rows_ref.shape[0]
        copy = pltpu.make_async_copy(rows_ref, all_ref.at[pl.ds(PAD + HALO * 4, own)], sem)
        copy.start()
        put_rows(all_ref, PAD, before_ref[...].astype(F32))
        put_rows(all_ref, PAD + HALO * 4 + own, after_ref[...].astype(F32))
        tiles = ends_ref.shape[1]
        meets = tile_ref.shape[0]

        def blank(e, _):
            tile_ref[e] = tiles - 1
            block_ref[e] = meets - tiles
            return 0

        lax.fori_loop(0, meets, blank, 0)

        def meet(t, count):
            def add(b, count):
                tile_ref[count] = t
                block_ref[count] = b
                return count + 1

            return lax.fori_loop(ends_ref[0, t], ends_ref[1, t] + 1, add, count)

        lax.fori_loop(0, tiles, meet, 0)
        copy.wait()

    def one(c, _):
        base = pl.multiple_of(c * 64, 64)
        first = step * out_ref.shape[0] + base
        gather_rows(lambda k: src_ref[first + k], all_ref, held_ref, out_ref, base, 64)
        return 0

    lax.fori_loop(0, out_ref.shape[0] // 64, one, 0)


def plan_kernel(taper_ref, key_ref, local_ref, weight_ref, block_ref):
    outs, cap = key_ref.shape
    key = key_ref[...]
    rows = key // (16 * outs)
    local = (rows & (TILE - 1)).T
    lane = lax.broadcasted_iota(jnp.int32, (cap, TILE), 1)
    entry = key & 15
    weights = jnp.zeros(key.shape, F32)
    for k in range(taper_ref.shape[0]):
        weights = jnp.where(entry == k, taper_ref[k], weights)
    out = (key // 16) & (outs - 1)
    blocks = rows // TILE
    sub = lax.broadcasted_iota(jnp.int32, (outs, cap), 0)
    per = TILE // cap
    for o in range(outs):
        hot = (local[:, o : o + 1] == lane).astype(F32).astype(BF16)
        local_ref[o // per, cap * (o % per) : cap * (o % per + 1), :] = hot
        at = slice(cap * (o % per), cap * (o % per + 1))
        spread = jnp.where(sub == out[o : o + 1, :], weights[o : o + 1, :], 0.0)
        weight_ref[o // per, :, at] = spread.astype(BF16)
        block_ref[o // per, :, at] = jnp.broadcast_to(blocks[o : o + 1, :], (8, cap))


def pairs_kernel(
    tile_ref, meet_ref, local_hbm, weight_hbm, block_hbm, source_hbm, arrived_ref, synth_ref, out_ref,
    local_ref, weight_ref, block_ref, source_ref, sum_ref, sems,
):
    half = source_ref.shape[2] // 2
    last = arrived_ref.shape[0] // TILE - 1
    chunk = local_ref.shape[0] // CHUNKS
    unroll = 4
    held = ((local_hbm, local_ref), (weight_hbm, weight_ref), (block_hbm, block_ref), (source_hbm, source_ref))

    def copies(c):
        at = pl.ds(c * chunk, chunk)
        return [
            pltpu.make_async_copy(a.at[at], b.at[at], sems.at[i, c]) for i, (a, b) in enumerate(held)
        ]

    for c in range(CHUNKS):
        for copy in copies(c):
            copy.start()
    sum_ref[...] = jnp.zeros_like(sum_ref)

    def some(c, _):
        @pl.when((c * unroll % chunk == 0) & (c * unroll < chunk * CHUNKS))
        def _():
            for copy in copies(c * unroll // chunk):
                copy.wait()

        total = sum_ref[...]
        for u in range(unroll):
            t = tile_ref[c * unroll + u]
            b = meet_ref[c * unroll + u]
            at = pl.multiple_of(jnp.minimum(b, last) * TILE, TILE)
            right = jnp.dot(
                local_ref[t], arrived_ref[pl.ds(at, TILE), :], preferred_element_type=F32
            )
            left = source_ref[t].astype(F32)
            sr, si, rr, ri = left[:, :half], left[:, half:], right[:, :half], right[:, half:]
            product = jnp.concatenate([sr * rr - si * ri, sr * ri + si * rr], axis=1).astype(BF16)
            weight = weight_ref[t]
            here = block_ref[t][:1, :] == b
            weight = jnp.where(here, weight.astype(F32), 0.0).astype(BF16)
            total += jnp.dot(weight, product, preferred_element_type=F32)
        sum_ref[...] = total
        return 0

    lax.fori_loop(0, tile_ref.shape[0] // unroll, some, 0)
    summed = sum_ref[...].astype(BF16)
    out_ref[...] = jnp.dot(summed, synth_ref[...], preferred_element_type=F32).astype(BF16)


VMEM = pl.BlockSpec(memory_space=pltpu.VMEM)
SMEM = pl.BlockSpec(memory_space=pltpu.SMEM)
HBM = pl.BlockSpec(memory_space=pltpu.HBM)


def shape(dims, kind):
    return jax.ShapeDtypeStruct(dims, kind)


def params(mib):
    return pltpu.CompilerParams(vmem_limit_bytes=mib << 20)


def cost(flops, moved):
    return pl.CostEstimate(flops=flops, bytes_accessed=moved, transcendentals=0)


def body(traces, src_index, rcv_index, taper_index, fetch_rows, line_owner, taper_table):
    sails = lax.axis_size("sail")
    cables = lax.axis_size("cable")
    tr_rows, samples = traces.shape
    outs, aper = src_index.shape
    cap = fetch_rows.shape[1]
    asked, place = pl.pallas_call(
        distinct_kernel,
        in_specs=[SMEM, VMEM],
        out_specs=[VMEM, VMEM],
        out_shape=[shape((sails, 1, cap), jnp.int32), shape((sails, cap), jnp.int32)],
        compiler_params=params(56),
        name="distinct",
    )(line_owner, fetch_rows)
    asked = lax.all_to_all(asked, "sail", split_axis=0, concat_axis=0, tiled=True)
    step = 256
    rows, first, last = pl.pallas_call(
        forward_kernel,
        grid=(tr_rows // step,),
        in_specs=[
            pl.BlockSpec((step, samples), lambda b: (b, 0)),
            pl.BlockSpec((samples, samples), lambda b: (0, 0)),
        ],
        out_specs=[
            pl.BlockSpec((step * 4, 128), lambda b: (b, 0)),
            pl.BlockSpec((HALO, samples), lambda b: (0, 0)),
            pl.BlockSpec((HALO, samples), lambda b: (0, 0)),
        ],
        out_shape=[
            shape((tr_rows * 4, 128), F32),
            shape((HALO, samples), BF16),
            shape((HALO, samples), BF16),
        ],
        compiler_params=params(56),
        name="forward",
        cost_estimate=cost(2 * tr_rows * samples * samples, 8 << 20),
    )(traces, forward_table(samples))
    fetched = sails * DISTINCT
    outgoing = pl.pallas_call(
        fetch_kernel,
        in_specs=[SMEM, HBM],
        out_specs=VMEM,
        out_shape=shape((fetched, samples), BF16),
        scratch_shapes=[
            pltpu.VMEM((tr_rows * 4 + 2 * PAD, 128), F32),
            pltpu.VMEM((fetched * 4, 128), F32),
            pltpu.SemaphoreType.DMA,
        ],
        compiler_params=params(50),
        name="fetch",
    )(asked, rows)
    arrived = lax.all_to_all(
        outgoing.reshape(sails, DISTINCT, samples), "sail", split_axis=0, concat_axis=0, tiled=True
    ).reshape(fetched, samples)
    up = [(i, i + 1) for i in range(cables - 1)]
    before = lax.ppermute(last, "cable", up)
    after = lax.ppermute(first, "cable", [(j, i) for i, j in up])
    key, value = pl.pallas_call(
        slots_kernel,
        in_specs=[VMEM] * 4,
        out_specs=[VMEM, VMEM],
        out_shape=[shape((outs, aper), jnp.int32)] * 2,
        compiler_params=params(56),
        name="slots",
        cost_estimate=cost(0, 10 << 20),
    )(place, src_index, rcv_index, taper_index)
    count = outs * aper
    key, value = lax.sort((key.reshape(-1), value.reshape(-1)), num_keys=1, is_stable=False)
    tiles = count // TILE
    blocks = fetched // TILE
    ends = key.reshape(tiles, TILE)[:, :: TILE - 1].T // (16 * outs * TILE)
    meets = tiles + blocks
    sources, tile, meet = pl.pallas_call(
        sources_kernel,
        grid=(8,),
        in_specs=[SMEM, SMEM, HBM, VMEM, VMEM],
        out_specs=[pl.BlockSpec((count // 8, samples), lambda b: (b, 0)), SMEM, SMEM],
        out_shape=[
            shape((count, samples), BF16), shape((meets,), jnp.int32), shape((meets,), jnp.int32)
        ],
        scratch_shapes=[
            pltpu.VMEM(((tr_rows + 2 * HALO) * 4 + 2 * PAD, 128), F32),
            pltpu.VMEM((count // 8 * 4, 128), F32),
            pltpu.SemaphoreType.DMA,
        ],
        compiler_params=params(56),
        name="sources",
        cost_estimate=cost(0, 40 << 20),
    )(value, ends, rows, before, after)
    local, weights, where = pl.pallas_call(
        plan_kernel,
        in_specs=[SMEM, VMEM],
        out_specs=[VMEM, VMEM, VMEM],
        out_shape=[
            shape((tiles, TILE, TILE), BF16),
            shape((tiles, outs, TILE), BF16),
            shape((tiles, 8, TILE), jnp.int32),
        ],
        compiler_params=params(56),
        name="plan",
        cost_estimate=cost(0, 10 << 20),
    )(taper_table, key.reshape(outs, aper))
    return pl.pallas_call(
        pairs_kernel,
        in_specs=[SMEM, SMEM, HBM, HBM, HBM, HBM, VMEM, VMEM],
        out_specs=VMEM,
        out_shape=shape((outs, samples), BF16),
        scratch_shapes=[
            pltpu.VMEM((tiles, TILE, TILE), BF16),
            pltpu.VMEM((tiles, outs, TILE), BF16),
            pltpu.VMEM((tiles, 8, TILE), jnp.int32),
            pltpu.VMEM((tiles, TILE, samples), BF16),
            pltpu.VMEM((outs, samples), F32),
            pltpu.SemaphoreType.DMA((4, CHUNKS)),
        ],
        compiler_params=params(50),
        name="pairs",
    )(
        tile, meet, local, weights, where, sources.reshape(tiles, TILE, samples), arrived,
        synthesis_table(samples, aper),
    )


def solution(mesh):
    split = P(("sail", "cable"), None)
    return jax.shard_map(
        body,
        mesh=mesh,
        in_specs=(split, split, split, split, split, P(), P()),
        out_specs=split,
        check_vma=False,
    )
```

time: 133 us -> 106 us (0.80)
  Pallas kernels: 63.9 us -> 53.4 us
  waiting for transfers between devices: 26.3 us -> 16.5 us
  local copies, waits for them, and re-layouts: 11.4 us -> 3.06 us
  other arithmetic: 5.18 us -> 7.64 us
  starting transfers between devices: 26 us -> 24.4 us
    all_to_all x1, waiting for transfers between devices: 25.3 us -> 14.1 us  [body(): lax.all_to_all(outgoing.reshape(sails, DISTINCT, samples), 'sail', split_...]
    pallas_call x4 -> x6, Pallas kernels: 60.5 us -> 49.9 us  [the longest x1 14.4 us: body(): pl.pallas_call(pairs_kernel, in_specs=[SMEM, SMEM, HBM, HBM, HBM, HBM, VM...]
    unnamed x20 -> x17, local copies, waits for them, and re-layouts: 11.4 us -> 2.98 us
    sort x0 -> x1, other arithmetic: none -> 7.09 us  [body(): lax.sort((key.reshape(-1), value.reshape(-1)), num_keys=1, is_stable=False)]
    neg x2 -> x0, other arithmetic: 4.14 us -> none  [the longest x1 2.07 us: forward_table(): -jnp.sin(angle)]
    all_to_all x1, starting transfers between devices: 8.95 us -> 7.35 us  [body(): lax.all_to_all(outgoing.reshape(sails, DISTINCT, samples), 'sail', split_...]
    all_to_all x1, waiting for transfers between devices: 0.97 us -> 2.46 us  [body(): lax.all_to_all(asked, 'sail', split_axis=0, concat_axis=0, tiled=True)]
  transfers between devices with their start and end apart: 4 -> 4, of which waited for: 2 -> 2; matrix products, arithmetic and copies ran while one was open for 4% -> 7% of each run, Pallas kernels for 14% -> 27%
where the time goes in v2:
time: 106 us; the launch traced here: 105 us
  Pallas kernels  53.4 us (50%)
  starting transfers between devices  24.4 us (23%)
  waiting for transfers between devices  16.5 us (16%)
  other arithmetic  7.64 us (7%)
  local copies, waits for them, and re-layouts  3.06 us (3%)
    pallas_call x1, Pallas kernels, body(): pl.pallas_call(pairs_kernel, in_specs=[SMEM, SMEM, HBM, HBM, HBM, HBM, VM...  14.4 us
    pallas_call x1, Pallas kernels, body(): pl.pallas_call(sources_kernel, grid=(8,), in_specs=[SMEM, SMEM, HBM, VMEM...  14.1 us
    all_to_all x1, waiting for transfers between devices, body(): lax.all_to_all(outgoing.reshape(sails, DISTINCT, samples), 'sail', split_...  14.1 us
    all_to_all x1, starting transfers between devices, body(): lax.all_to_all(asked, 'sail', split_axis=0, concat_axis=0, tiled=True)  11.5 us
    all_to_all x1, starting transfers between devices, body(): lax.all_to_all(outgoing.reshape(sails, DISTINCT, samples), 'sail', split_...  7.35 us
    pallas_call x1, Pallas kernels, body(): pl.pallas_call(forward_kernel, grid=(tr_rows // step,), in_specs=[pl.Bloc...  7.32 us
    sort x1, other arithmetic, body(): lax.sort((key.reshape(-1), value.reshape(-1)), num_keys=1, is_stable=False)  7.09 us
    pallas_call x1, Pallas kernels, body(): pl.pallas_call(fetch_kernel, in_specs=[SMEM, HBM], out_specs=VMEM, out_sh...  6.64 us
  transfers between devices with their start and end apart: 4, of which 2 were waited for; matrix products, arithmetic and copies ran while one was open for 7% of the time, Pallas kernels for 27%

profile of v2, /device:TPU:4, one launch (start us, length us, event | category | flops | bytes accessed | tf_op | source)
XLA Modules:
  0.0 105.2 jit_solution(9489595681049508207)
XLA Ops:
  0.0 3.5 %distinct.1 = (s32[32,1,128]{2,1,0:T(1,128)}, s32[32,128]{1,0:T(8,128)}) custom-call(s32[32]{0:T(128)} %owner_ref.1, s32[32,128]{1,0:T(8,128)} %rows_ref.1), custom_call_target="tpu_custom_call" | custom-call | tf_op jit(solution)/shard_map/distinct/pallas_call | solution.py:278
  3.5 11.5 %all-to-all-start = ((s32[32,1,128]{2,1,0:T(1,128)}), s32[32,1,128]{2,1,0:T(1,128)S(1)}, u32[]{:S(2)}, u32[]{:S(2)}) async-start(s32[32,1,128]{2,1,0:T(1,128)} %get-tuple-element.34), calls=%async_computation | async-start | bytes 32768 | tf_op jit(solution)/shard_map/all_to_all | solution.py:286
  15.0 7.3 %forward.1 = (f32[8192,128]{1,0:T(8,128)}, bf16[64,512]{1,0:T(8,128)(2,1)}, bf16[64,512]{1,0:T(8,128)(2,1)}) custom-call(bf16[2048,512]{1,0:T(8,128)(2,1)} %traces_ref.1, bf16[512,512]{1,0:T(8,128)(2,1)} %constant.20.clone.table_ref), custom_call_target="tpu_custom_call" | custom-call | flops 1073741824 | bytes 8388608 | tf_op jit(solution)/shard_map/forward/pallas_call | solution.py:288
  22.4 2.5 %all-to-all-done.asked_ref = s32[32,1,128]{2,1,0:T(1,128)S(1)} async-done(((s32[32,1,128]{2,1,0:T(1,128)}), s32[32,1,128]{2,1,0:T(1,128)S(1)}, u32[]{:S(2)}, u32[]{:S(2)}) %all-to-all-start) | async-done | bytes 16416 | tf_op jit(solution)/shard_map/all_to_all | solution.py:286
  24.8 6.6 %fetch.1 = bf16[2048,512]{1,0:T(8,128)(2,1)} custom-call(s32[32,1,128]{2,1,0:T(1,128)S(1)} %all-to-all-done.asked_ref, f32[8192,128]{1,0:T(8,128)} %get-tuple-element.25.rows_ref), custom_call_target="tpu_custom_call" | custom-call | tf_op jit(solution)/shard_map/fetch/pallas_call | solution.py:310
  31.5 7.3 %all-to-all-start.1 = ((bf16[32,64,512]{2,1,0:T(8,128)(2,1)}), bf16[32,64,512]{2,1,0:T(8,128)(2,1)S(1)}, u32[]{:S(2)}, u32[]{:S(2)}) async-start(bf16[32,64,512]{2,1,0:T(8,128)(2,1)} %bitcast.5), calls=%async_computation.1 | async-start | bytes 4194304 | tf_op jit(solution)/shard_map/all_to_all | solution.py:323
  38.8 1.9 %collective-permute-start = (bf16[64,512]{1,0:T(8,128)(2,1)}, bf16[64,512]{1,0:T(8,128)(2,1)S(1)}, u32[]{:S(2)}, u32[]{:S(2)}) collective-permute-start(bf16[64,512]{1,0:T(8,128)(2,1)} %get-tuple-element.26), channel_id=1, source_target_pairs={{0,1},{1,2},{2,3},{3,4},{4,5},{5,6},{6,7},{8,9},{9,10},{10,11},{11... | collective-permute-start | bytes 196616 | tf_op jit(solution)/shard_map/ppermute | solution.py:327
  40.7 3.6 %collective-permute-start.1 = (bf16[64,512]{1,0:T(8,128)(2,1)}, bf16[64,512]{1,0:T(8,128)(2,1)S(1)}, u32[]{:S(2)}, u32[]{:S(2)}) collective-permute-start(bf16[64,512]{1,0:T(8,128)(2,1)} %get-tuple-element.27), channel_id=1, source_target_pairs={{1,0},{2,1},{3,2},{4,3},{5,4},{6,5},{7,6},{9,8},{10,9},{11,10},{12... | collective-permute-start | bytes 196616 | tf_op jit(solution)/shard_map/ppermute | solution.py:328
  44.4 3.1 %slots.1 = (s32[64,128]{1,0:T(8,128)}, s32[64,128]{1,0:T(8,128)}) custom-call(s32[32,128]{1,0:T(8,128)} %get-tuple-element.20.place_ref, s32[64,128]{1,0:T(8,128)} %src_ref.1, s32[64,128]{1,0:T(8,128)} %rcv_ref.1, s32[64,128]{1,0:T(8,128)} %taper_ref.2), custom_call_target="tpu_custom_call" | custom-call | bytes 10485760 | tf_op jit(solution)/shard_map/slots/pallas_call | solution.py:329
  47.5 7.1 %sort.15 = (s32[8192]{0:T(1024)S(1)}, s32[8192]{0:T(1024)}) sort(s32[8192]{0:T(1024)} %bitcast.17, s32[8192]{0:T(1024)} %bitcast.18), dimensions={0}, to_apply=%region_0.0 | sort | flops 106496 | bytes 131072 | tf_op jit(solution)/shard_map/sort | solution.py:339
  54.5 0.0 copy-start.5
  54.6 0.1 slice.3
  54.6 0.1 copy.11
  54.7 0.6 and_select_fusion.ends_ref
  55.3 0.0 copy-done.5
  55.3 4.3 %plan.1 = (bf16[32,256,256]{2,1,0:T(8,128)(2,1)}, bf16[32,64,256]{2,1,0:T(8,128)(2,1)}, s32[32,8,256]{2,1,0:T(8,128)}) custom-call(f32[16]{0:T(128)} %taper_ref.3, s32[64,128]{1,0:T(8,128)} %bitcast.16), custom_call_target="tpu_custom_call" | custom-call | bytes 10485760 | tf_op jit(solution)/shard_map/plan/pallas_call | solution.py:361
  59.6 0.0 copy-start
  59.6 0.0 copy-start.2
  59.6 0.0 collective-permute-done.before_ref
  59.6 0.0 copy-start.6
  59.6 0.0 collective-permute-done.1.after_ref
  59.6 0.0 copy-start.7
  59.7 0.6 copy-done.6
  60.2 0.0 copy-done.7
  60.3 14.1 %sources.1 = (bf16[8192,512]{1,0:T(8,128)(2,1)}, s32[40]{0:T(128)}, s32[40]{0:T(128)}) custom-call(s32[8192]{0:T(1024)} %get-tuple-element.23.src_ref, s32[2,32]{1,0:T(2,128)} %and_select_fusion.ends_ref, f32[8192,128]{1,0:T(8,128)} %get-tuple-element.25.rows_ref, bf16[64,512]{1,0:T(8,128)(2,1)} %copy-done.6, bf16[64,512]{1,0:T(8,128)(2,1)} %copy-done.7), custom_call_target="tpu_custom_call" | custom-call | bytes 41943040 | tf_op jit(solution)/shard_map/sources/pallas_call | solution.py:344
  74.4 14.1 %all-to-all-done.1 = bf16[32,64,512]{2,1,0:T(8,128)(2,1)S(1)} async-done(((bf16[32,64,512]{2,1,0:T(8,128)(2,1)}), bf16[32,64,512]{2,1,0:T(8,128)(2,1)S(1)}, u32[]{:S(2)}, u32[]{:S(2)}) %all-to-all-start.1) | async-done | bytes 2097184 | tf_op jit(solution)/shard_map/all_to_all | solution.py:323
  88.5 0.0 copy-done
  88.5 0.0 copy-done.2
  88.5 1.0 copy-done.1
  89.5 0.6 copy-done.3
  90.1 0.6 copy-done.4
  90.7 14.4 %pairs.1 = bf16[64,512]{1,0:T(8,128)(2,1)} custom-call(s32[40]{0:T(128)S(1)} %copy-done.3, s32[40]{0:T(128)S(1)} %copy-done.4, bf16[32,256,256]{2,1,0:T(8,128)(2,1)} %get-tuple-element.30.local_hbm, bf16[32,64,256]{2,1,0:T(8,128)(2,1)S(1)} %copy-done, s32[32,8,256]{2,1,0:T(8,128)S(1)} %copy-done.2, bf16[32,256,512]{2,1,0:T(8,128)(2,1)} %bitcast.15, ...), custom_call_target="tpu_custom_call" | custom-call | tf_op jit(solution)/shard_map/pairs/pallas_call | solution.py:374
  (4 shorter events, 0.0 us)
Async XLA Ops:
  3.5 21.3 %all-to-all-start = ((s32[32,1,128]{2,1,0:T(1,128)}), s32[32,1,128]{2,1,0:T(1,128)S(1)}, u32[]{:S(2)}, u32[]{:S(2)}) async-start(s32[32,1,128]{2,1,0:T(1,128)} %get-tuple-element.34), calls=%async_computation | async-start | bytes 32768 | tf_op jit(solution)/shard_map/all_to_all | solution.py:286
  31.5 57.0 %all-to-all-start.1 = ((bf16[32,64,512]{2,1,0:T(8,128)(2,1)}), bf16[32,64,512]{2,1,0:T(8,128)(2,1)S(1)}, u32[]{:S(2)}, u32[]{:S(2)}) async-start(bf16[32,64,512]{2,1,0:T(8,128)(2,1)} %bitcast.5), calls=%async_computation.1 | async-start | bytes 4194304 | tf_op jit(solution)/shard_map/all_to_all | solution.py:323
  38.8 20.8 %collective-permute-start = (bf16[64,512]{1,0:T(8,128)(2,1)}, bf16[64,512]{1,0:T(8,128)(2,1)S(1)}, u32[]{:S(2)}, u32[]{:S(2)}) collective-permute-start(bf16[64,512]{1,0:T(8,128)(2,1)} %get-tuple-element.26), channel_id=1, source_target_pairs={{0,1},{1,2},{2,3},{3,4},{4,5},{5,6},{6,7},{8,9},{9,10},{10,11},{11... | collective-permute-start | bytes 196616 | tf_op jit(solution)/shard_map/ppermute | solution.py:327
  40.7 18.9 %collective-permute-start.1 = (bf16[64,512]{1,0:T(8,128)(2,1)}, bf16[64,512]{1,0:T(8,128)(2,1)S(1)}, u32[]{:S(2)}, u32[]{:S(2)}) collective-permute-start(bf16[64,512]{1,0:T(8,128)(2,1)} %get-tuple-element.27), channel_id=1, source_target_pairs={{1,0},{2,1},{3,2},{4,3},{5,4},{6,5},{7,6},{9,8},{10,9},{11,10},{12... | collective-permute-start | bytes 196616 | tf_op jit(solution)/shard_map/ppermute | solution.py:328
  54.5 0.7 copy-start.5
  59.6 28.9 %copy-start = (bf16[32,64,256]{2,1,0:T(8,128)(2,1)S(1)}, bf16[32,64,256]{2,1,0:T(8,128)(2,1)}, u32[]{:S(2)}) copy-start(bf16[32,64,256]{2,1,0:T(8,128)(2,1)} %get-tuple-element.31.weight_hbm) | copy-start | bytes 3145732
  59.6 28.9 %copy-start.2 = (s32[32,8,256]{2,1,0:T(8,128)S(1)}, s32[32,8,256]{2,1,0:T(8,128)}, u32[]{:S(2)}) copy-start(s32[32,8,256]{2,1,0:T(8,128)} %get-tuple-element.32.block_hbm) | copy-start | bytes 786436
  59.6 0.6 copy-start.6
  59.6 0.6 copy-start.7
  88.5 1.0 copy-start.1
  89.5 0.6 copy-start.3
  90.1 0.6 copy-start.4

commit v3 on v2

v3 whole, which is shorter than its diff:
```python
import math

import jax
import jax.numpy as jnp
import ml_dtypes
import numpy as np
from jax import lax
from jax.experimental import pallas as pl
from jax.experimental.pallas import tpu as pltpu
from jax.sharding import PartitionSpec as P

HALO = 64
DISTINCT = 64
PAD = 8
TILE = 256
STEP = 512
GROUPS = 4
CHUNKS = 8
UNROLL = 8
F32 = jnp.float32
BF16 = jnp.bfloat16


def forward_table(samples):
    turns = np.arange(samples)[:, None] * np.arange(samples // 2)[None, :] % samples
    angle = turns * (2.0 * math.pi / samples)
    table = np.concatenate([np.cos(angle), -np.sin(angle)], axis=1) / math.sqrt(samples)
    return jnp.asarray(table.astype(np.float32).astype(ml_dtypes.bfloat16))


def synthesis_table(samples, aperture):
    turns = np.arange(samples // 2)[:, None] * np.arange(samples)[None, :] % samples
    angle = turns * (2.0 * math.pi / samples)
    scale = math.sqrt(aperture * (samples // 2))
    table = np.concatenate([np.cos(angle), -np.sin(angle)], axis=0) / scale
    return jnp.asarray(table.astype(np.float32).astype(ml_dtypes.bfloat16))


def turned(values):
    lines, cap = values.shape
    return jnp.concatenate([values, jnp.zeros((cap - lines, cap), values.dtype)], axis=0).T


def distinct_kernel(owner_ref, rows_ref, asked_ref, place_ref):
    lines, cap = rows_ref.shape
    rows = rows_ref[...]
    sub = lax.broadcasted_iota(jnp.int32, (cap, cap), 0)
    lane = lax.broadcasted_iota(jnp.int32, (cap, cap), 1)
    earlier = sub < lane
    columns = turned(rows)
    repeats = []
    for g in range(lines):
        same = (columns[:, g : g + 1] == rows[g : g + 1, :]) & earlier
        repeats.append(jnp.max(jnp.where(same, 1.0, 0.0), axis=0, keepdims=True))
    once = 1.0 - jnp.concatenate(repeats, axis=0)
    before = jnp.where(earlier, 1.0, 0.0).astype(BF16)
    place = jnp.dot(once.astype(BF16), before, preferred_element_type=F32)
    place = jnp.where(once > 0.0, place, -1.0).astype(jnp.int32)
    place_ref[...] = place
    places = turned(place)
    for g in range(lines):
        match = places[:, g : g + 1] == lane
        picked = jnp.max(jnp.where(match, columns[:, g : g + 1], 0), axis=0, keepdims=True)
        asked_ref[owner_ref[g]] = picked * 4


def put_rows(ref, start, block):
    for q in range(4):
        at = pl.ds(start + q, block.shape[0], stride=4)
        ref[at, :] = block[:, 128 * q : 128 * (q + 1)]


def gather_rows(index, rows_ref, held_ref, out_ref, base, count):
    sub = lax.broadcasted_iota(jnp.int32, (8, 128), 0)
    for k in range(0, count, 2):
        a = rows_ref[pl.ds(index(k) + PAD, 8), :]
        b = rows_ref[pl.ds(index(k + 1) + PAD - 4, 8), :]
        held_ref[pl.ds(pl.multiple_of(base * 4, 8) + 4 * k, 8), :] = jnp.where(sub < 4, a, b)
    for q in range(4):
        part = held_ref[pl.ds(base * 4 + q, count, stride=4), :]
        out_ref[pl.ds(base, count), 128 * q : 128 * (q + 1)] = part.astype(BF16)


def spectra_kernel(
    asked_ref, traces_hbm, table_ref, rows_hbm, first_ref, last_ref, out_hbm,
    traces_ref, rows_ref, held_ref, out_ref, in_sems, row_sems, out_sems,
):
    parts = len(range(0, traces_ref.shape[0], STEP))
    loads = []
    stores = []
    for b in range(parts):
        at = pl.ds(b * STEP, STEP)
        loads.append(pltpu.make_async_copy(traces_hbm.at[at], traces_ref.at[at], in_sems.at[b]))
        stores.append(
            pltpu.make_async_copy(
                rows_ref.at[pl.ds(PAD + b * STEP * 4, STEP * 4)],
                rows_hbm.at[pl.ds(b * STEP * 4, STEP * 4)],
                row_sems.at[b],
            )
        )
        loads[b].start()
    for b in range(parts):
        loads[b].wait()
        spectra = jnp.dot(
            traces_ref[b * STEP : (b + 1) * STEP, :], table_ref[...], preferred_element_type=F32
        ).astype(BF16)
        put_rows(rows_ref, PAD + b * STEP * 4, spectra.astype(F32))
        if b == 0:
            first_ref[...] = spectra[:HALO]
        if b == parts - 1:
            last_ref[...] = spectra[STEP - HALO :]
    peers = asked_ref.shape[0]
    each = peers // GROUPS
    sends = []
    for g in range(GROUPS):

        def one(p, _):
            base = pl.multiple_of(p * DISTINCT, DISTINCT)
            gather_rows(lambda k: asked_ref[p, 0, k], rows_ref, held_ref, out_ref, base, DISTINCT)
            return 0

        lax.fori_loop(g * each, (g + 1) * each, one, 0)
        at = pl.ds(g * each * DISTINCT, each * DISTINCT)
        sends.append(pltpu.make_async_copy(out_ref.at[at], out_hbm.at[at], out_sems.at[g]))
        sends[g].start()
    for b in range(parts):
        stores[b].start()
    for copy in sends + stores:
        copy.wait()


def slots_kernel(
    owner_ref, rows_ref, place_ref, src_ref, rcv_ref, taper_ref, key_ref, value_ref, rank_ref
):
    lines, cap = place_ref.shape
    outs = rcv_ref.shape[0]
    rows = rows_ref[...]
    columns = turned(rows)
    places = turned(place_ref[...])
    for g in range(lines):
        same = columns[:, g : g + 1] == rows[g : g + 1, :]
        rank_ref[g : g + 1, :] = jnp.max(
            jnp.where(same, places[:, g : g + 1], -1), axis=0, keepdims=True
        )
    line = lax.broadcasted_iota(jnp.int32, (lines, cap), 0)
    first = jnp.zeros((lines, cap), F32)
    for g in range(lines):
        first = jnp.where(line == g, (owner_ref[g] * DISTINCT).astype(F32), first)
    rank = rank_ref[...].astype(F32).astype(BF16)
    sub = lax.broadcasted_iota(jnp.int32, (cap, cap), 0)

    def some(b, _):
        at = pl.multiple_of(b * 8, 8)
        slots = rcv_ref[pl.ds(at, 8), :]
        rows = []
        for u in range(8):
            slot = slots[u : u + 1, :]
            at_slot = (sub == (slot & (cap - 1))).astype(F32).astype(BF16)
            found = jnp.dot(rank, at_slot, preferred_element_type=F32) + first
            rows.append(
                jnp.sum(jnp.where(line == slot // cap, found, 0.0), axis=0, keepdims=True)
            )
        rows = jnp.concatenate(rows, axis=0).astype(jnp.int32)
        out = lax.broadcasted_iota(jnp.int32, (8, cap), 0) + at
        key_ref[pl.ds(at, 8), :] = (rows * outs + out) * 16 + taper_ref[pl.ds(at, 8), :]
        value_ref[pl.ds(at, 8), :] = src_ref[pl.ds(at, 8), :] * 4
        return 0

    lax.fori_loop(0, outs // 8, some, 0)


def sources_kernel(
    src_ref, ends_ref, rows_ref, before_ref, after_ref, out_ref, meet_ref, all_ref, held_ref, sem
):
    step = pl.program_id(0)

    @pl.when(step == 0)
    def _():
        own = rows_ref.shape[0]
        copy = pltpu.make_async_copy(rows_ref, all_ref.at[pl.ds(PAD + HALO * 4, own)], sem)
        copy.start()
        put_rows(all_ref, PAD, before_ref[...].astype(F32))
        put_rows(all_ref, PAD + HALO * 4 + own, after_ref[...].astype(F32))
        tiles = ends_ref.shape[1]
        meets = meet_ref.shape[0]

        def blank(e, _):
            meet_ref[e] = (meets - tiles) * 64 + tiles - 1
            return 0

        lax.fori_loop(0, meets, blank, 0)

        def meet(t, count):
            def add(b, count):
                meet_ref[count] = b * 64 + t
                return count + 1

            return lax.fori_loop(ends_ref[0, t], ends_ref[1, t] + 1, add, count)

        lax.fori_loop(0, tiles, meet, 0)
        copy.wait()

    def one(c, _):
        base = pl.multiple_of(c * 64, 64)
        first = step * out_ref.shape[0] + base
        gather_rows(lambda k: src_ref[first + k], all_ref, held_ref, out_ref, base, 64)
        return 0

    lax.fori_loop(0, out_ref.shape[0] // 64, one, 0)


def pairs_kernel(
    meet_ref, key_ref, taper_ref, source_hbm, arrived_ref, synth_hbm, out_ref,
    source_ref, synth_ref, sum_ref, weight_ref, hot_ref, product_ref, sems, synth_sem,
):
    tiles, _, samples = source_ref.shape
    outs = out_ref.shape[0]
    half = samples // 2
    last = arrived_ref.shape[0] // TILE - 1
    chunk = tiles // CHUNKS

    def load(c):
        at = pl.ds(c * chunk, chunk)
        return pltpu.make_async_copy(source_hbm.at[at], source_ref.at[at], sems.at[c])

    for c in range(CHUNKS):
        load(c).start()
    synth_copy = pltpu.make_async_copy(synth_hbm, synth_ref, synth_sem)
    synth_copy.start()
    entry = key_ref[...] & 15
    weights = jnp.zeros(entry.shape, F32)
    for k in range(taper_ref.shape[0]):
        weights = jnp.where(entry == k, taper_ref[k], weights)
    weight_ref[...] = weights
    sum_ref[...] = jnp.zeros_like(sum_ref)
    sub = lax.broadcasted_iota(jnp.int32, (TILE, TILE), 0)
    out = lax.broadcasted_iota(jnp.int32, (outs, TILE), 0)

    def some(c, _):
        @pl.when(c * UNROLL < tiles)
        def _():
            for u in range(UNROLL // chunk):
                load(c * (UNROLL // chunk) + u).wait()

        for u in range(UNROLL):
            meet = meet_ref[c * UNROLL + u]
            t = meet & 63
            b = meet // 64
            at = pl.multiple_of(jnp.minimum(b, last) * TILE, TILE)
            key = key_ref[pl.ds(t, 1), :]
            row = key // (16 * outs)
            here = jnp.where(row // TILE == b, weight_ref[pl.ds(t, 1), :], 0.0)
            spread = jnp.where(out == ((key // 16) & (outs - 1)), here, 0.0).astype(BF16)
            hot = jnp.where(sub == (row & (TILE - 1)), 1.0, 0.0).astype(BF16)
            right = lax.dot_general(
                hot, arrived_ref[pl.ds(at, TILE), :], (((0,), (0,)), ((), ())),
                preferred_element_type=F32,
            )
            left = source_ref[t].astype(F32)
            sr, si, rr, ri = left[:, :half], left[:, half:], right[:, :half], right[:, half:]
            product = jnp.concatenate([sr * rr - si * ri, sr * ri + si * rr], axis=1)
            product_ref[u * TILE : (u + 1) * TILE, :] = product.astype(BF16)
            hot_ref[:, u * TILE : (u + 1) * TILE] = spread
        sum_ref[...] += jnp.dot(hot_ref[...], product_ref[...], preferred_element_type=F32)
        return 0

    lax.fori_loop(0, meet_ref.shape[0] // UNROLL, some, 0)
    synth_copy.wait()
    summed = sum_ref[...].astype(BF16)
    out_ref[...] = jnp.dot(summed, synth_ref[...], preferred_element_type=F32).astype(BF16)


VMEM = pl.BlockSpec(memory_space=pltpu.VMEM)
SMEM = pl.BlockSpec(memory_space=pltpu.SMEM)
HBM = pl.BlockSpec(memory_space=pltpu.HBM)


def shape(dims, kind):
    return jax.ShapeDtypeStruct(dims, kind)


def params(mib):
    return pltpu.CompilerParams(vmem_limit_bytes=mib << 20)


def cost(flops, moved):
    return pl.CostEstimate(flops=flops, bytes_accessed=moved, transcendentals=0)


def body(traces, src_index, rcv_index, taper_index, fetch_rows, line_owner, taper_table):
    sails = lax.axis_size("sail")
    cables = lax.axis_size("cable")
    tr_rows, samples = traces.shape
    outs, aper = src_index.shape
    cap = fetch_rows.shape[1]
    asked, place = pl.pallas_call(
        distinct_kernel,
        in_specs=[SMEM, VMEM],
        out_specs=[VMEM, VMEM],
        out_shape=[shape((sails, 1, cap), jnp.int32), shape((sails, cap), jnp.int32)],
        compiler_params=params(56),
        name="distinct",
    )(line_owner, fetch_rows)
    asked = lax.all_to_all(asked, "sail", split_axis=0, concat_axis=0, tiled=True)
    fetched = sails * DISTINCT
    parts = tr_rows // STEP
    rows, first, last, outgoing = pl.pallas_call(
        spectra_kernel,
        in_specs=[SMEM, HBM, VMEM],
        out_specs=[HBM, VMEM, VMEM, HBM],
        out_shape=[
            shape((tr_rows * 4, 128), F32),
            shape((HALO, samples), BF16),
            shape((HALO, samples), BF16),
            shape((fetched, samples), BF16),
        ],
        scratch_shapes=[
            pltpu.VMEM((tr_rows, samples), BF16),
            pltpu.VMEM((tr_rows * 4 + 2 * PAD, 128), F32),
            pltpu.VMEM((fetched * 4, 128), F32),
            pltpu.VMEM((fetched, samples), BF16),
            pltpu.SemaphoreType.DMA((parts,)),
            pltpu.SemaphoreType.DMA((parts,)),
            pltpu.SemaphoreType.DMA((GROUPS,)),
        ],
        compiler_params=params(56),
        name="spectra",
    )(asked, traces, forward_table(samples))
    arrived = lax.all_to_all(
        outgoing.reshape(sails, DISTINCT, samples), "sail", split_axis=0, concat_axis=0, tiled=True
    ).reshape(fetched, samples)
    up = [(i, i + 1) for i in range(cables - 1)]
    before = lax.ppermute(last, "cable", up)
    after = lax.ppermute(first, "cable", [(j, i) for i, j in up])
    key, value = pl.pallas_call(
        slots_kernel,
        in_specs=[SMEM] + [VMEM] * 5,
        out_specs=[VMEM, VMEM],
        out_shape=[shape((outs, aper), jnp.int32)] * 2,
        scratch_shapes=[pltpu.VMEM((sails, cap), jnp.int32)],
        compiler_params=params(56),
        name="slots",
        cost_estimate=cost(0, 10 << 20),
    )(line_owner, fetch_rows, place, src_index, rcv_index, taper_index)
    count = outs * aper
    key, value = lax.sort((key.reshape(-1), value.reshape(-1)), num_keys=1, is_stable=False)
    tiles = count // TILE
    blocks = fetched // TILE
    ends = key.reshape(tiles, TILE)[:, :: TILE - 1].T // (16 * outs * TILE)
    meets = -(-(tiles + blocks) // UNROLL) * UNROLL
    sources, meet = pl.pallas_call(
        sources_kernel,
        grid=(8,),
        in_specs=[SMEM, SMEM, HBM, VMEM, VMEM],
        out_specs=[pl.BlockSpec((count // 8, samples), lambda b: (b, 0)), SMEM],
        out_shape=[shape((count, samples), BF16), shape((meets,), jnp.int32)],
        scratch_shapes=[
            pltpu.VMEM(((tr_rows + 2 * HALO) * 4 + 2 * PAD, 128), F32),
            pltpu.VMEM((count // 8 * 4, 128), F32),
            pltpu.SemaphoreType.DMA,
        ],
        compiler_params=params(56),
        name="sources",
        cost_estimate=cost(0, 40 << 20),
    )(value, ends, rows, before, after)
    return pl.pallas_call(
        pairs_kernel,
        in_specs=[SMEM, VMEM, SMEM, HBM, VMEM, HBM],
        out_specs=VMEM,
        out_shape=shape((outs, samples), BF16),
        scratch_shapes=[
            pltpu.VMEM((tiles, TILE, samples), BF16),
            pltpu.VMEM((samples, samples), BF16),
            pltpu.VMEM((outs, samples), F32),
            pltpu.VMEM((tiles, TILE), F32),
            pltpu.VMEM((outs, UNROLL * TILE), BF16),
            pltpu.VMEM((UNROLL * TILE, samples), BF16),
            pltpu.SemaphoreType.DMA((CHUNKS,)),
            pltpu.SemaphoreType.DMA,
        ],
        compiler_params=params(50),
        name="pairs",
    )(
        meet, key.reshape(tiles, TILE), taper_table, sources.reshape(tiles, TILE, samples), arrived,
        synthesis_table(samples, aper),
    )


def solution(mesh):
    split = P(("sail", "cable"), None)
    return jax.shard_map(
        body,
        mesh=mesh,
        in_specs=(split, split, split, split, split, P(), P()),
        out_specs=split,
        check_vma=False,
    )
```

time: 106 us -> 97.9 us (0.924)
  blocking collectives: 0 us -> 21.3 us
  starting transfers between devices: 24.4 us -> 9.71 us
  Pallas kernels: 53.4 us -> 40.6 us
    all_to_all x0 -> x1, blocking collectives: none -> 21.3 us  [body(): lax.all_to_all(asked, 'sail', split_axis=0, concat_axis=0, tiled=True)]
    pallas_call x5 -> x3, Pallas kernels: 35.8 us -> 23.4 us  [the longest x1 10.1 us: body(): pl.pallas_call(pairs_kernel, in_specs=[SMEM, VMEM, SMEM, HBM, VMEM, HBM],...]
    all_to_all x1 -> x0, starting transfers between devices: 11.5 us -> none  [body(): lax.all_to_all(asked, 'sail', split_axis=0, concat_axis=0, tiled=True)]
    all_to_all x1, starting transfers between devices: 7.35 us -> 4.15 us  [body(): lax.all_to_all(outgoing.reshape(sails, DISTINCT, samples), 'sail', split_...]
    all_to_all x1 -> x0, waiting for transfers between devices: 2.46 us -> none  [body(): lax.all_to_all(asked, 'sail', split_axis=0, concat_axis=0, tiled=True)]
    unnamed x17 -> x14, local copies, waits for them, and re-layouts: 2.98 us -> 1.31 us
    ppermute x1, waiting for transfers between devices: 0.01 us -> 1.22 us  [body(): after = lax.ppermute(first, 'cable', [(j, i) for i, j in up])]
    all_to_all x1, waiting for transfers between devices: 14.1 us -> 15.2 us  [body(): lax.all_to_all(outgoing.reshape(sails, DISTINCT, samples), 'sail', split_...]
  transfers between devices with their start and end apart: 4 -> 3, of which waited for: 2 -> 2; matrix products, arithmetic and copies ran while one was open for 7% -> 8% of each run, Pallas kernels for 27% -> 19%
where the time goes in v3:
time: 97.9 us; the launch traced here: 97.3 us
  Pallas kernels  40.6 us (41%)
  blocking collectives  21.3 us (22%)
  waiting for transfers between devices  16.4 us (17%)
  starting transfers between devices  9.71 us (10%)
  other arithmetic  7.1 us (7%)
  local copies, waits for them, and re-layouts  2.04 us (2%)
    all_to_all x1, blocking collectives, body(): lax.all_to_all(asked, 'sail', split_axis=0, concat_axis=0, tiled=True)  21.3 us
    all_to_all x1, waiting for transfers between devices, body(): lax.all_to_all(outgoing.reshape(sails, DISTINCT, samples), 'sail', split_...  15.2 us
    pallas_call x1, Pallas kernels, body(): pl.pallas_call(sources_kernel, grid=(8,), in_specs=[SMEM, SMEM, HBM, VMEM...  14.3 us
    pallas_call x1, Pallas kernels, body(): pl.pallas_call(pairs_kernel, in_specs=[SMEM, VMEM, SMEM, HBM, VMEM, HBM],...  10.1 us
    pallas_call x1, Pallas kernels, body(): pl.pallas_call(spectra_kernel, in_specs=[SMEM, HBM, VMEM], out_specs=[HBM...  8.97 us
    sort x1, other arithmetic, body(): lax.sort((key.reshape(-1), value.reshape(-1)), num_keys=1, is_stable=False)  7.09 us
    pallas_call x1, Pallas kernels, body(): pl.pallas_call(slots_kernel, in_specs=[SMEM] + [VMEM] * 5, out_specs=[VME...  4.37 us
    all_to_all x1, starting transfers between devices, body(): lax.all_to_all(outgoing.reshape(sails, DISTINCT, samples), 'sail', split_...  4.15 us
  transfers between devices with their start and end apart: 3, of which 2 were waited for; matrix products, arithmetic and copies ran while one was open for 8% of the time, Pallas kernels for 19%

profile of v3, /device:TPU:4, one launch (start us, length us, event | category | flops | bytes accessed | tf_op | source)
XLA Modules:
  0.0 97.3 jit_solution(7741423706771456714)
XLA Ops:
  0.0 3.0 %distinct.1 = (s32[32,1,128]{2,1,0:T(1,128)}, s32[32,128]{1,0:T(8,128)}) custom-call(s32[32]{0:T(128)} %owner_ref.3, s32[32,128]{1,0:T(8,128)} %rows_ref.3), custom_call_target="tpu_custom_call" | custom-call | tf_op jit(solution)/shard_map/distinct/pallas_call | solution.py:296
  3.0 21.3 %all_to_all.10.asked_ref = s32[32,1,128]{2,1,0:T(1,128)} all-to-all(s32[32,1,128]{2,1,0:T(1,128)} %get-tuple-element.22), channel_id=1, replica_groups=mesh['sail'=32,'cable'=8] {'sail'}, dimensions={0} | all-to-all | bytes 32768 | tf_op jit(solution)/shard_map/all_to_all | solution.py:304
  24.3 9.0 %spectra.1 = (f32[8192,128]{1,0:T(8,128)}, bf16[64,512]{1,0:T(8,128)(2,1)}, bf16[64,512]{1,0:T(8,128)(2,1)}, bf16[2048,512]{1,0:T(8,128)(2,1)}) custom-call(s32[32,1,128]{2,1,0:T(1,128)} %all_to_all.10.asked_ref, bf16[2048,512]{1,0:T(8,128)(2,1)} %traces_hbm.1, bf16[512,512]{1,0:T(8,128)(2,1)} %constant.20.clone.table_ref), custom_call_target="tpu_custom_call" | custom-call | tf_op jit(solution)/shard_map/spectra/pallas_call | solution.py:307
  33.2 0.0 copy-start.6
  33.2 0.0 copy-start.5
  33.3 4.2 %all-to-all-start.1 = ((bf16[32,64,512]{2,1,0:T(8,128)(2,1)}), bf16[32,64,512]{2,1,0:T(8,128)(2,1)S(1)}, u32[]{:S(2)}, u32[]{:S(2)}) async-start(bf16[32,64,512]{2,1,0:T(8,128)(2,1)} %bitcast.23), calls=%async_computation.1 | async-start | bytes 4194304 | tf_op jit(solution)/shard_map/all_to_all | solution.py:329
  37.4 4.4 %slots.1 = (s32[64,128]{1,0:T(8,128)}, s32[64,128]{1,0:T(8,128)}) custom-call(s32[32]{0:T(128)} %owner_ref.3, s32[32,128]{1,0:T(8,128)} %rows_ref.3, s32[32,128]{1,0:T(8,128)} %get-tuple-element.17.place_ref, s32[64,128]{1,0:T(8,128)} %src_ref.1, s32[64,128]{1,0:T(8,128)} %rcv_ref.1, s32[64,128]{1,0:T(8,128)} %taper_ref.2), custom_call_target="tpu_custom_call" | custom-call | bytes 10485760 | tf_op jit(solution)/shard_map/slots/pallas_call | solution.py:335
  41.8 7.1 %sort.15 = (s32[8192]{0:T(1024)S(1)}, s32[8192]{0:T(1024)}) sort(s32[8192]{0:T(1024)} %bitcast.24, s32[8192]{0:T(1024)} %bitcast.25), dimensions={0}, to_apply=%region_0.0 | sort | flops 106496 | bytes 131072 | tf_op jit(solution)/shard_map/sort | solution.py:346
  48.9 0.1 slice.3
  49.0 0.0 copy-done.6
  49.0 1.9 %collective-permute-start = (bf16[64,512]{1,0:T(8,128)(2,1)S(1)}, bf16[64,512]{1,0:T(8,128)(2,1)S(1)}, u32[]{:S(2)}, u32[]{:S(2)}) collective-permute-start(bf16[64,512]{1,0:T(8,128)(2,1)S(1)} %copy-done.6), channel_id=1, source_target_pairs={{0,1},{1,2},{2,3},{3,4},{4,5},{5,6},{6,7},{8,9},{9,10},{10,11},{11... | collective-permute-start | bytes 196616 | tf_op jit(solution)/shard_map/ppermute | solution.py:333
  50.9 0.0 copy-done.5
  50.9 3.6 %collective-permute-start.1 = (bf16[64,512]{1,0:T(8,128)(2,1)S(1)}, bf16[64,512]{1,0:T(8,128)(2,1)S(1)}, u32[]{:S(2)}, u32[]{:S(2)}) collective-permute-start(bf16[64,512]{1,0:T(8,128)(2,1)S(1)} %copy-done.5), channel_id=1, source_target_pairs={{1,0},{2,1},{3,2},{4,3},{5,4},{6,5},{7,6},{9,8},{10,9},{11,10},{12... | collective-permute-start | bytes 196616 | tf_op jit(solution)/shard_map/ppermute | solution.py:334
  54.6 0.6 copy.10.ends_ref
  55.2 0.0 collective-permute-done.before_ref
  55.2 0.0 copy-start.3
  55.2 1.2 %collective-permute-done.1.after_ref = bf16[64,512]{1,0:T(8,128)(2,1)S(1)} collective-permute-done((bf16[64,512]{1,0:T(8,128)(2,1)S(1)}, bf16[64,512]{1,0:T(8,128)(2,1)S(1)}, u32[]{:S(2)}, u32[]{:S(2)}) %collective-permute-start.1) | collective-permute-done | bytes 65568 | tf_op jit(solution)/shard_map/ppermute | solution.py:334
  56.4 0.0 copy-start.4
  56.4 0.0 copy-done.3
  56.4 0.6 copy-done.4
  57.1 0.0 copy-start
  57.1 0.0 copy-start.1
  57.1 14.3 %sources.1 = (bf16[8192,512]{1,0:T(8,128)(2,1)}, s32[40]{0:T(128)}) custom-call(s32[8192]{0:T(1024)} %get-tuple-element.20.src_ref, s32[2,32]{1,0:T(2,128)} %copy.10.ends_ref, f32[8192,128]{1,0:T(8,128)} %get-tuple-element.23.rows_ref, bf16[64,512]{1,0:T(8,128)(2,1)} %copy-done.3, bf16[64,512]{1,0:T(8,128)(2,1)} %copy-done.4), custom_call_target="tpu_custom_call" | custom-call | bytes 41943040 | tf_op jit(solution)/shard_map/sources/pallas_call | solution.py:351
  71.3 15.2 %all-to-all-done.1 = bf16[32,64,512]{2,1,0:T(8,128)(2,1)S(1)} async-done(((bf16[32,64,512]{2,1,0:T(8,128)(2,1)}), bf16[32,64,512]{2,1,0:T(8,128)(2,1)S(1)}, u32[]{:S(2)}, u32[]{:S(2)}) %all-to-all-start.1) | async-done | bytes 2097184 | tf_op jit(solution)/shard_map/all_to_all | solution.py:329
  86.5 0.0 copy-done
  86.5 0.0 copy-done.1
  86.5 0.0 copy-start.2
  86.5 0.7 copy-done.2
  87.2 10.1 %pairs.1 = bf16[64,512]{1,0:T(8,128)(2,1)} custom-call(s32[40]{0:T(128)S(1)} %copy-done.2, s32[32,256]{1,0:T(8,128)S(1)} %reshape.21.key_ref, f32[16]{0:T(128)S(1)} %copy-done.1, bf16[32,256,512]{2,1,0:T(8,128)(2,1)} %bitcast.22, bf16[2048,512]{1,0:T(8,128)(2,1)S(1)} %bitcast.21, bf16[512,512]{1,0:T(8,128)(2,1)S(1)} %copy-done), custom_call_target="tpu_custom_call" | custom-call | tf_op jit(solution)/shard_map/pairs/pallas_call | solution.py:366
  (2 shorter events, 0.0 us)
Async XLA Ops:
  33.2 15.7 %copy-start.6 = (bf16[64,512]{1,0:T(8,128)(2,1)S(1)}, bf16[64,512]{1,0:T(8,128)(2,1)}, u32[]{:S(2)}) copy-start(bf16[64,512]{1,0:T(8,128)(2,1)} %get-tuple-element.24) | copy-start | bytes 196612
  33.2 17.6 %copy-start.5 = (bf16[64,512]{1,0:T(8,128)(2,1)S(1)}, bf16[64,512]{1,0:T(8,128)(2,1)}, u32[]{:S(2)}) copy-start(bf16[64,512]{1,0:T(8,128)(2,1)} %get-tuple-element.25) | copy-start | bytes 196612
  33.3 53.2 %all-to-all-start.1 = ((bf16[32,64,512]{2,1,0:T(8,128)(2,1)}), bf16[32,64,512]{2,1,0:T(8,128)(2,1)S(1)}, u32[]{:S(2)}, u32[]{:S(2)}) async-start(bf16[32,64,512]{2,1,0:T(8,128)(2,1)} %bitcast.23), calls=%async_computation.1 | async-start | bytes 4194304 | tf_op jit(solution)/shard_map/all_to_all | solution.py:329
  49.0 6.2 %collective-permute-start = (bf16[64,512]{1,0:T(8,128)(2,1)S(1)}, bf16[64,512]{1,0:T(8,128)(2,1)S(1)}, u32[]{:S(2)}, u32[]{:S(2)}) collective-permute-start(bf16[64,512]{1,0:T(8,128)(2,1)S(1)} %copy-done.6), channel_id=1, source_target_pairs={{0,1},{1,2},{2,3},{3,4},{4,5},{5,6},{6,7},{8,9},{9,10},{10,11},{11... | collective-permute-start | bytes 196616 | tf_op jit(solution)/shard_map/ppermute | solution.py:333
  50.9 5.5 %collective-permute-start.1 = (bf16[64,512]{1,0:T(8,128)(2,1)S(1)}, bf16[64,512]{1,0:T(8,128)(2,1)S(1)}, u32[]{:S(2)}, u32[]{:S(2)}) collective-permute-start(bf16[64,512]{1,0:T(8,128)(2,1)S(1)} %copy-done.5), channel_id=1, source_target_pairs={{1,0},{2,1},{3,2},{4,3},{5,4},{6,5},{7,6},{9,8},{10,9},{11,10},{12... | collective-permute-start | bytes 196616 | tf_op jit(solution)/shard_map/ppermute | solution.py:334
  55.2 1.2 %copy-start.3 = (bf16[64,512]{1,0:T(8,128)(2,1)}, bf16[64,512]{1,0:T(8,128)(2,1)S(1)}, u32[]{:S(2)}) copy-start(bf16[64,512]{1,0:T(8,128)(2,1)S(1)} %collective-permute-done.before_ref) | copy-start | bytes 196612
  56.4 0.6 copy-start.4
  57.1 29.4 %copy-start = (bf16[512,512]{1,0:T(8,128)(2,1)S(1)}, bf16[512,512]{1,0:T(8,128)(2,1)}, u32[]{:S(2)}) copy-start(bf16[512,512]{1,0:T(8,128)(2,1)} %constant.21.clone.synth_hbm) | copy-start | bytes 1572868
  57.1 29.4 %copy-start.1 = (f32[16]{0:T(128)S(1)}, f32[16]{0:T(128)}, u32[]{:S(2)}) copy-start(f32[16]{0:T(128)} %taper_ref.3) | copy-start | bytes 196
  86.5 0.7 copy-start.2

commit v4 on v3

--- a/solution.py
+++ b/solution.py
@@ -82,33 +82,31 @@
 
 
 def spectra_kernel(
-    asked_ref, traces_hbm, table_ref, rows_hbm, first_ref, last_ref, out_hbm,
-    traces_ref, rows_ref, held_ref, out_ref, in_sems, row_sems, out_sems,
+    asked_ref, traces_hbm, table_hbm, spectra_hbm, out_hbm,
+    traces_ref, table_ref, spectra_ref, rows_ref, held_ref, out_ref, in_sems, table_sem, store_sems, out_sems,
 ):
     parts = len(range(0, traces_ref.shape[0], STEP))
+    table = pltpu.make_async_copy(table_hbm, table_ref, table_sem)
+    table.start()
     loads = []
     stores = []
     for b in range(parts):
         at = pl.ds(b * STEP, STEP)
         loads.append(pltpu.make_async_copy(traces_hbm.at[at], traces_ref.at[at], in_sems.at[b]))
         stores.append(
-            pltpu.make_async_copy(
-                rows_ref.at[pl.ds(PAD + b * STEP * 4, STEP * 4)],
-                rows_hbm.at[pl.ds(b * STEP * 4, STEP * 4)],
-                row_sems.at[b],
-            )
+            pltpu.make_async_copy(spectra_ref.at[at], spectra_hbm.at[at], store_sems.at[b])
         )
         loads[b].start()
+    table.wait()
     for b in range(parts):
+        at = pl.ds(b * STEP, STEP)
         loads[b].wait()
         spectra = jnp.dot(
-            traces_ref[b * STEP : (b + 1) * STEP, :], table_ref[...], preferred_element_type=F32
+            traces_ref[at, :], table_ref[...], preferred_element_type=F32
         ).astype(BF16)
+        spectra_ref[at, :] = spectra
         put_rows(rows_ref, PAD + b * STEP * 4, spectra.astype(F32))
-        if b == 0:
-            first_ref[...] = spectra[:HALO]
-        if b == parts - 1:
-            last_ref[...] = spectra[STEP - HALO :]
+        stores[b].start()
     peers = asked_ref.shape[0]
     each = peers // GROUPS
     sends = []
@@ -123,9 +121,7 @@
         at = pl.ds(g * each * DISTINCT, each * DISTINCT)
         sends.append(pltpu.make_async_copy(out_ref.at[at], out_hbm.at[at], out_sems.at[g]))
         sends[g].start()
-    for b in range(parts):
-        stores[b].start()
-    for copy in sends + stores:
+    for copy in stores + sends:
         copy.wait()
 
 
@@ -170,35 +166,26 @@
 
 
 def sources_kernel(
-    src_ref, ends_ref, rows_ref, before_ref, after_ref, out_ref, meet_ref, all_ref, held_ref, sem
+    src_ref, spectra_hbm, before_ref, after_ref, out_ref, spectra_ref, all_ref, held_ref, sem
 ):
     step = pl.program_id(0)
 
     @pl.when(step == 0)
     def _():
-        own = rows_ref.shape[0]
-        copy = pltpu.make_async_copy(rows_ref, all_ref.at[pl.ds(PAD + HALO * 4, own)], sem)
+        own = spectra_ref.shape[0]
+        copy = pltpu.make_async_copy(spectra_hbm, spectra_ref, sem)
         copy.start()
         put_rows(all_ref, PAD, before_ref[...].astype(F32))
-        put_rows(all_ref, PAD + HALO * 4 + own, after_ref[...].astype(F32))
-        tiles = ends_ref.shape[1]
-        meets = meet_ref.shape[0]
-
-        def blank(e, _):
-            meet_ref[e] = (meets - tiles) * 64 + tiles - 1
+        put_rows(all_ref, PAD + (HALO + own) * 4, after_ref[...].astype(F32))
+        copy.wait()
+
+        def one(b, _):
+            at = pl.multiple_of(b * TILE, TILE)
+            block = spectra_ref[pl.ds(at, TILE), :].astype(F32)
+            put_rows(all_ref, PAD + HALO * 4 + at * 4, block)
             return 0
 
-        lax.fori_loop(0, meets, blank, 0)
-
-        def meet(t, count):
-            def add(b, count):
-                meet_ref[count] = b * 64 + t
-                return count + 1
-
-            return lax.fori_loop(ends_ref[0, t], ends_ref[1, t] + 1, add, count)
-
-        lax.fori_loop(0, tiles, meet, 0)
-        copy.wait()
+        lax.fori_loop(0, own // TILE, one, 0)
 
     def one(c, _):
         base = pl.multiple_of(c * 64, 64)
@@ -210,8 +197,8 @@
 
 
 def pairs_kernel(
-    meet_ref, key_ref, taper_ref, source_hbm, arrived_ref, synth_hbm, out_ref,
-    source_ref, synth_ref, sum_ref, weight_ref, hot_ref, product_ref, sems, synth_sem,
+    ends_ref, taper_ref, key_ref, source_hbm, arrived_ref, synth_hbm, out_ref,
+    source_ref, synth_ref, sum_ref, weight_ref, hot_ref, product_ref, meet_ref, sems, synth_sem,
 ):
     tiles, _, samples = source_ref.shape
     outs = out_ref.shape[0]
@@ -227,6 +214,22 @@
         load(c).start()
     synth_copy = pltpu.make_async_copy(synth_hbm, synth_ref, synth_sem)
     synth_copy.start()
+    meets = meet_ref.shape[0]
+
+    def blank(e, _):
+        meet_ref[e] = (meets - tiles) * 64 + tiles - 1
+        return 0
+
+    lax.fori_loop(tiles, meets, blank, 0)
+
+    def meet(t, count):
+        def add(b, count):
+            meet_ref[count] = b * 64 + t
+            return count + 1
+
+        return lax.fori_loop(ends_ref[0, t], ends_ref[1, t] + 1, add, count)
+
+    lax.fori_loop(0, tiles, meet, 0)
     entry = key_ref[...] & 15
     weights = jnp.zeros(entry.shape, F32)
     for k in range(taper_ref.shape[0]):
@@ -256,10 +259,11 @@
                 hot, arrived_ref[pl.ds(at, TILE), :], (((0,), (0,)), ((), ())),
                 preferred_element_type=F32,
             )
-            left = source_ref[t].astype(F32)
+            right = right.astype(BF16)
+            left = source_ref[t]
             sr, si, rr, ri = left[:, :half], left[:, half:], right[:, :half], right[:, half:]
             product = jnp.concatenate([sr * rr - si * ri, sr * ri + si * rr], axis=1)
-            product_ref[u * TILE : (u + 1) * TILE, :] = product.astype(BF16)
+            product_ref[u * TILE : (u + 1) * TILE, :] = product
             hot_ref[:, u * TILE : (u + 1) * TILE] = spread
         sum_ref[...] += jnp.dot(hot_ref[...], product_ref[...], preferred_element_type=F32)
         return 0
@@ -304,22 +308,20 @@
     asked = lax.all_to_all(asked, "sail", split_axis=0, concat_axis=0, tiled=True)
     fetched = sails * DISTINCT
     parts = tr_rows // STEP
-    rows, first, last, outgoing = pl.pallas_call(
+    spectra, outgoing = pl.pallas_call(
         spectra_kernel,
-        in_specs=[SMEM, HBM, VMEM],
-        out_specs=[HBM, VMEM, VMEM, HBM],
-        out_shape=[
-            shape((tr_rows * 4, 128), F32),
-            shape((HALO, samples), BF16),
-            shape((HALO, samples), BF16),
-            shape((fetched, samples), BF16),
-        ],
+        in_specs=[SMEM, HBM, HBM],
+        out_specs=[HBM, HBM],
+        out_shape=[shape((tr_rows, samples), BF16), shape((fetched, samples), BF16)],
         scratch_shapes=[
+            pltpu.VMEM((tr_rows, samples), BF16),
+            pltpu.VMEM((samples, samples), BF16),
             pltpu.VMEM((tr_rows, samples), BF16),
             pltpu.VMEM((tr_rows * 4 + 2 * PAD, 128), F32),
             pltpu.VMEM((fetched * 4, 128), F32),
             pltpu.VMEM((fetched, samples), BF16),
             pltpu.SemaphoreType.DMA((parts,)),
+            pltpu.SemaphoreType.DMA,
             pltpu.SemaphoreType.DMA((parts,)),
             pltpu.SemaphoreType.DMA((GROUPS,)),
         ],
@@ -330,8 +332,8 @@
         outgoing.reshape(sails, DISTINCT, samples), "sail", split_axis=0, concat_axis=0, tiled=True
     ).reshape(fetched, samples)
     up = [(i, i + 1) for i in range(cables - 1)]
-    before = lax.ppermute(last, "cable", up)
-    after = lax.ppermute(first, "cable", [(j, i) for i, j in up])
+    before = lax.ppermute(spectra[tr_rows - HALO :], "cable", up)
+    after = lax.ppermute(spectra[:HALO], "cable", [(j, i) for i, j in up])
     key, value = pl.pallas_call(
         slots_kernel,
         in_specs=[SMEM] + [VMEM] * 5,
@@ -348,13 +350,14 @@
     blocks = fetched // TILE
     ends = key.reshape(tiles, TILE)[:, :: TILE - 1].T // (16 * outs * TILE)
     meets = -(-(tiles + blocks) // UNROLL) * UNROLL
-    sources, meet = pl.pallas_call(
+    sources = pl.pallas_call(
         sources_kernel,
         grid=(8,),
-        in_specs=[SMEM, SMEM, HBM, VMEM, VMEM],
-        out_specs=[pl.BlockSpec((count // 8, samples), lambda b: (b, 0)), SMEM],
-        out_shape=[shape((count, samples), BF16), shape((meets,), jnp.int32)],
+        in_specs=[SMEM, HBM, VMEM, VMEM],
+        out_specs=pl.BlockSpec((count // 8, samples), lambda b: (b, 0)),
+        out_shape=shape((count, samples), BF16),
         scratch_shapes=[
+            pltpu.VMEM((tr_rows, samples), BF16),
             pltpu.VMEM(((tr_rows + 2 * HALO) * 4 + 2 * PAD, 128), F32),
             pltpu.VMEM((count // 8 * 4, 128), F32),
             pltpu.SemaphoreType.DMA,
@@ -362,10 +365,10 @@
         compiler_params=params(56),
         name="sources",
         cost_estimate=cost(0, 40 << 20),
-    )(value, ends, rows, before, after)
+    )(value, spectra, before, after)
     return pl.pallas_call(
         pairs_kernel,
-        in_specs=[SMEM, VMEM, SMEM, HBM, VMEM, HBM],
+        in_specs=[SMEM, SMEM, VMEM, HBM, VMEM, HBM],
         out_specs=VMEM,
         out_shape=shape((outs, samples), BF16),
         scratch_shapes=[
@@ -375,13 +378,14 @@
             pltpu.VMEM((tiles, TILE), F32),
             pltpu.VMEM((outs, UNROLL * TILE), BF16),
             pltpu.VMEM((UNROLL * TILE, samples), BF16),
+            pltpu.SMEM((meets,), jnp.int32),
             pltpu.SemaphoreType.DMA((CHUNKS,)),
             pltpu.SemaphoreType.DMA,
         ],
         compiler_params=params(50),
         name="pairs",
     )(
-        meet, key.reshape(tiles, TILE), taper_table, sources.reshape(tiles, TILE, samples), arrived,
+        ends, taper_table, key.reshape(tiles, TILE), sources.reshape(tiles, TILE, samples), arrived,
         synthesis_table(samples, aper),
     )
 

time: 97.9 us -> 94.1 us (0.961)
  Pallas kernels: 40.6 us -> 37.3 us
    pallas_call x3, Pallas kernels: 33.3 us -> 29.9 us  [the longest x1 14 us: body(): pl.pallas_call(sources_kernel, grid=(8,), in_specs=[SMEM, HBM, VMEM, VMEM...]
  transfers between devices with their start and end apart: 3 -> 3, of which waited for: 2 -> 2; matrix products, arithmetic and copies ran while one was open for 8% -> 9% of each run, Pallas kernels for 19% -> 20%
where the time goes in v4:
time: 94.1 us; the launch traced here: 93.4 us
  Pallas kernels  37.3 us (40%)
  blocking collectives  21.1 us (22%)
  waiting for transfers between devices  16.5 us (18%)
  starting transfers between devices  9.59 us (10%)
  other arithmetic  7.11 us (8%)
  local copies, waits for them, and re-layouts  1.67 us (2%)
    all_to_all x1, blocking collectives, body(): lax.all_to_all(asked, 'sail', split_axis=0, concat_axis=0, tiled=True)  21.1 us
    all_to_all x1, waiting for transfers between devices, body(): lax.all_to_all(outgoing.reshape(sails, DISTINCT, samples), 'sail', split_...  14.7 us
    pallas_call x1, Pallas kernels, body(): pl.pallas_call(sources_kernel, grid=(8,), in_specs=[SMEM, HBM, VMEM, VMEM...  14 us
    pallas_call x1, Pallas kernels, body(): pl.pallas_call(pairs_kernel, in_specs=[SMEM, SMEM, VMEM, HBM, VMEM, HBM],...  8.61 us
    pallas_call x1, Pallas kernels, body(): pl.pallas_call(spectra_kernel, in_specs=[SMEM, HBM, HBM], out_specs=[HBM,...  7.36 us
    sort x1, other arithmetic, body(): lax.sort((key.reshape(-1), value.reshape(-1)), num_keys=1, is_stable=False)  7.1 us
    pallas_call x1, Pallas kernels, body(): pl.pallas_call(slots_kernel, in_specs=[SMEM] + [VMEM] * 5, out_specs=[VME...  4.39 us
    all_to_all x1, starting transfers between devices, body(): lax.all_to_all(outgoing.reshape(sails, DISTINCT, samples), 'sail', split_...  4.02 us
  transfers between devices with their start and end apart: 3, of which 2 were waited for; matrix products, arithmetic and copies ran while one was open for 9% of the time, Pallas kernels for 20%

profile of v4, /device:TPU:4, one launch (start us, length us, event | category | flops | bytes accessed | tf_op | source)
XLA Modules:
  0.0 93.4 jit_solution(4556679879376758622)
XLA Ops:
  0.0 3.0 %distinct.1 = (s32[32,1,128]{2,1,0:T(1,128)}, s32[32,128]{1,0:T(8,128)}) custom-call(s32[32]{0:T(128)} %owner_ref.3, s32[32,128]{1,0:T(8,128)} %rows_ref.3), custom_call_target="tpu_custom_call" | custom-call | tf_op jit(solution)/shard_map/distinct/pallas_call | solution.py:300
  3.0 21.1 %all_to_all.10.asked_ref = s32[32,1,128]{2,1,0:T(1,128)} all-to-all(s32[32,1,128]{2,1,0:T(1,128)} %get-tuple-element.18), channel_id=1, replica_groups=mesh['sail'=32,'cable'=8] {'sail'}, dimensions={0} | all-to-all | bytes 32768 | tf_op jit(solution)/shard_map/all_to_all | solution.py:308
  24.1 7.4 %spectra.1 = (bf16[2048,512]{1,0:T(8,128)(2,1)}, bf16[2048,512]{1,0:T(8,128)(2,1)}) custom-call(s32[32,1,128]{2,1,0:T(1,128)} %all_to_all.10.asked_ref, bf16[2048,512]{1,0:T(8,128)(2,1)} %traces_hbm.1, bf16[512,512]{1,0:T(8,128)(2,1)} %constant.20.clone.table_hbm), custom_call_target="tpu_custom_call" | custom-call | tf_op jit(solution)/shard_map/spectra/pallas_call | solution.py:311
  31.5 4.0 %all-to-all-start.1 = ((bf16[32,64,512]{2,1,0:T(8,128)(2,1)}), bf16[32,64,512]{2,1,0:T(8,128)(2,1)S(1)}, u32[]{:S(2)}, u32[]{:S(2)}) async-start(bf16[32,64,512]{2,1,0:T(8,128)(2,1)} %bitcast.23), calls=%async_computation.1 | async-start | bytes 4194304 | tf_op jit(solution)/shard_map/all_to_all | solution.py:331
  35.5 4.4 %slots.1 = (s32[64,128]{1,0:T(8,128)}, s32[64,128]{1,0:T(8,128)}) custom-call(s32[32]{0:T(128)} %owner_ref.3, s32[32,128]{1,0:T(8,128)} %rows_ref.3, s32[32,128]{1,0:T(8,128)} %get-tuple-element.13.place_ref, s32[64,128]{1,0:T(8,128)} %src_ref.1, s32[64,128]{1,0:T(8,128)} %rcv_ref.1, s32[64,128]{1,0:T(8,128)} %taper_ref.2), custom_call_target="tpu_custom_call" | custom-call | bytes 10485760 | tf_op jit(solution)/shard_map/slots/pallas_call | solution.py:337
  39.9 7.1 %sort.15 = (s32[8192]{0:T(1024)S(1)}, s32[8192]{0:T(1024)}) sort(s32[8192]{0:T(1024)} %bitcast.24, s32[8192]{0:T(1024)} %bitcast.25), dimensions={0}, to_apply=%region_0.0 | sort | flops 106496 | bytes 131072 | tf_op jit(solution)/shard_map/sort | solution.py:348
  47.0 0.1 slice.9
  47.1 0.9 fusion.3
  48.0 1.9 %collective-permute-start = (bf16[64,512]{1,0:T(8,128)(2,1)S(1)}, bf16[64,512]{1,0:T(8,128)(2,1)S(1)}, u32[]{:S(2)}, u32[]{:S(2)}) collective-permute-start(bf16[64,512]{1,0:T(8,128)(2,1)S(1)} %get-tuple-element.22), channel_id=1, source_target_pairs={{0,1},{1,2},{2,3},{3,4},{4,5},{5,6},{6,7},{8,9},{9,10},{10,11},{11... | collective-permute-start | bytes 196616 | tf_op jit(solution)/shard_map/ppermute | solution.py:335
  49.9 3.6 %collective-permute-start.1 = (bf16[64,512]{1,0:T(8,128)(2,1)S(1)}, bf16[64,512]{1,0:T(8,128)(2,1)S(1)}, u32[]{:S(2)}, u32[]{:S(2)}) collective-permute-start(bf16[64,512]{1,0:T(8,128)(2,1)S(1)} %get-tuple-element.21), channel_id=1, source_target_pairs={{1,0},{2,1},{3,2},{4,3},{5,4},{6,5},{7,6},{9,8},{10,9},{11,10},{12... | collective-permute-start | bytes 196616 | tf_op jit(solution)/shard_map/ppermute | solution.py:336
  53.6 0.1 copy.10.ends_ref
  53.6 0.0 collective-permute-done.before_ref
  53.6 0.0 copy-start.2
  53.6 1.8 %collective-permute-done.1.after_ref = bf16[64,512]{1,0:T(8,128)(2,1)S(1)} collective-permute-done((bf16[64,512]{1,0:T(8,128)(2,1)S(1)}, bf16[64,512]{1,0:T(8,128)(2,1)S(1)}, u32[]{:S(2)}, u32[]{:S(2)}) %collective-permute-start.1) | collective-permute-done | bytes 65568 | tf_op jit(solution)/shard_map/ppermute | solution.py:336
  55.4 0.0 copy-start.3
  55.4 0.0 copy-done.2
  55.4 0.6 copy-done.3
  56.1 0.0 copy-start
  56.1 0.0 copy-start.1
  56.1 14.0 %sources.1 = bf16[8192,512]{1,0:T(8,128)(2,1)} custom-call(s32[8192]{0:T(1024)} %get-tuple-element.17.src_ref, bf16[2048,512]{1,0:T(8,128)(2,1)} %get-tuple-element.19.spectra_hbm, bf16[64,512]{1,0:T(8,128)(2,1)} %copy-done.2, bf16[64,512]{1,0:T(8,128)(2,1)} %copy-done.3), custom_call_target="tpu_custom_call" | custom-call | bytes 41943040 | tf_op jit(solution)/shard_map/sources/pallas_call | solution.py:353
  70.0 14.7 %all-to-all-done.1 = bf16[32,64,512]{2,1,0:T(8,128)(2,1)S(1)} async-done(((bf16[32,64,512]{2,1,0:T(8,128)(2,1)}), bf16[32,64,512]{2,1,0:T(8,128)(2,1)S(1)}, u32[]{:S(2)}, u32[]{:S(2)}) %all-to-all-start.1) | async-done | bytes 2097184 | tf_op jit(solution)/shard_map/all_to_all | solution.py:331
  84.8 0.0 copy-done
  84.8 0.0 copy-done.1
  84.8 8.6 %pairs.1 = bf16[64,512]{1,0:T(8,128)(2,1)} custom-call(s32[2,32]{1,0:T(2,128)S(1)} %copy.10.ends_ref, f32[16]{0:T(128)S(1)} %copy-done.1, s32[32,256]{1,0:T(8,128)S(1)} %reshape.21.key_ref, bf16[32,256,512]{2,1,0:T(8,128)(2,1)} %bitcast.22, bf16[2048,512]{1,0:T(8,128)(2,1)S(1)} %bitcast.21, bf16[512,512]{1,0:T(8,128)(2,1)S(1)} %copy-done), custom_call_target="tpu_custom_call" | custom-call | tf_op jit(solution)/shard_map/pairs/pallas_call | solution.py:369
  (2 shorter events, 0.0 us)
Async XLA Ops:
  31.5 53.3 %all-to-all-start.1 = ((bf16[32,64,512]{2,1,0:T(8,128)(2,1)}), bf16[32,64,512]{2,1,0:T(8,128)(2,1)S(1)}, u32[]{:S(2)}, u32[]{:S(2)}) async-start(bf16[32,64,512]{2,1,0:T(8,128)(2,1)} %bitcast.23), calls=%async_computation.1 | async-start | bytes 4194304 | tf_op jit(solution)/shard_map/all_to_all | solution.py:331
  48.0 5.7 %collective-permute-start = (bf16[64,512]{1,0:T(8,128)(2,1)S(1)}, bf16[64,512]{1,0:T(8,128)(2,1)S(1)}, u32[]{:S(2)}, u32[]{:S(2)}) collective-permute-start(bf16[64,512]{1,0:T(8,128)(2,1)S(1)} %get-tuple-element.22), channel_id=1, source_target_pairs={{0,1},{1,2},{2,3},{3,4},{4,5},{5,6},{6,7},{8,9},{9,10},{10,11},{11... | collective-permute-start | bytes 196616 | tf_op jit(solution)/shard_map/ppermute | solution.py:335
  49.9 5.5 %collective-permute-start.1 = (bf16[64,512]{1,0:T(8,128)(2,1)S(1)}, bf16[64,512]{1,0:T(8,128)(2,1)S(1)}, u32[]{:S(2)}, u32[]{:S(2)}) collective-permute-start(bf16[64,512]{1,0:T(8,128)(2,1)S(1)} %get-tuple-element.21), channel_id=1, source_target_pairs={{1,0},{2,1},{3,2},{4,3},{5,4},{6,5},{7,6},{9,8},{10,9},{11,10},{12... | collective-permute-start | bytes 196616 | tf_op jit(solution)/shard_map/ppermute | solution.py:336
  53.6 1.8 %copy-start.2 = (bf16[64,512]{1,0:T(8,128)(2,1)}, bf16[64,512]{1,0:T(8,128)(2,1)S(1)}, u32[]{:S(2)}) copy-start(bf16[64,512]{1,0:T(8,128)(2,1)S(1)} %collective-permute-done.before_ref) | copy-start | bytes 196612
  55.4 0.6 copy-start.3
  56.1 28.7 %copy-start = (bf16[512,512]{1,0:T(8,128)(2,1)S(1)}, bf16[512,512]{1,0:T(8,128)(2,1)}, u32[]{:S(2)}) copy-start(bf16[512,512]{1,0:T(8,128)(2,1)} %constant.21.clone.synth_hbm) | copy-start | bytes 1572868
  56.1 28.7 %copy-start.1 = (f32[16]{0:T(128)S(1)}, f32[16]{0:T(128)}, u32[]{:S(2)}) copy-start(f32[16]{0:T(128)} %taper_ref.3) | copy-start | bytes 196

commit v5 on v4

--- a/solution.py
+++ b/solution.py
@@ -41,9 +41,19 @@
     return jnp.concatenate([values, jnp.zeros((cap - lines, cap), values.dtype)], axis=0).T
 
 
-def distinct_kernel(owner_ref, rows_ref, asked_ref, place_ref):
-    lines, cap = rows_ref.shape
-    rows = rows_ref[...]
+def order_kernel(owner_ref, rows_hbm, out_hbm, sems):
+    copies = []
+    for g in range(rows_hbm.shape[0]):
+        copies.append(
+            pltpu.make_async_copy(rows_hbm.at[g], out_hbm.at[owner_ref[g]], sems.at[g])
+        )
+        copies[g].start()
+    for copy in copies:
+        copy.wait()
+
+
+def first_entries(rows):
+    lines, cap = rows.shape
     sub = lax.broadcasted_iota(jnp.int32, (cap, cap), 0)
     lane = lax.broadcasted_iota(jnp.int32, (cap, cap), 1)
     earlier = sub < lane
@@ -55,13 +65,7 @@
     once = 1.0 - jnp.concatenate(repeats, axis=0)
     before = jnp.where(earlier, 1.0, 0.0).astype(BF16)
     place = jnp.dot(once.astype(BF16), before, preferred_element_type=F32)
-    place = jnp.where(once > 0.0, place, -1.0).astype(jnp.int32)
-    place_ref[...] = place
-    places = turned(place)
-    for g in range(lines):
-        match = places[:, g : g + 1] == lane
-        picked = jnp.max(jnp.where(match, columns[:, g : g + 1], 0), axis=0, keepdims=True)
-        asked_ref[owner_ref[g]] = picked * 4
+    return columns, jnp.where(once > 0.0, place, -1.0).astype(jnp.int32)
 
 
 def put_rows(ref, start, block):
@@ -82,8 +86,9 @@
 
 
 def spectra_kernel(
-    asked_ref, traces_hbm, table_hbm, spectra_hbm, out_hbm,
-    traces_ref, table_ref, spectra_ref, rows_ref, held_ref, out_ref, in_sems, table_sem, store_sems, out_sems,
+    lists_ref, traces_hbm, table_hbm, spectra_hbm, out_hbm,
+    traces_ref, table_ref, spectra_ref, rows_ref, held_ref, out_ref, distinct_ref, asked_ref,
+    in_sems, table_sem, asked_sem, store_sems, out_sems,
 ):
     parts = len(range(0, traces_ref.shape[0], STEP))
     table = pltpu.make_async_copy(table_hbm, table_ref, table_sem)
@@ -97,6 +102,16 @@
             pltpu.make_async_copy(spectra_ref.at[at], spectra_hbm.at[at], store_sems.at[b])
         )
         loads[b].start()
+    lists = lists_ref[...]
+    columns, place = first_entries(lists)
+    places = turned(place)
+    lane = lax.broadcasted_iota(jnp.int32, columns.shape, 1)
+    for g in range(lists.shape[0]):
+        match = places[:, g : g + 1] == lane
+        picked = jnp.max(jnp.where(match, columns[:, g : g + 1], 0), axis=0, keepdims=True)
+        distinct_ref[g : g + 1, :] = picked * 4
+    asking = pltpu.make_async_copy(distinct_ref, asked_ref, asked_sem)
+    asking.start()
     table.wait()
     for b in range(parts):
         at = pl.ds(b * STEP, STEP)
@@ -107,6 +122,7 @@
         spectra_ref[at, :] = spectra
         put_rows(rows_ref, PAD + b * STEP * 4, spectra.astype(F32))
         stores[b].start()
+    asking.wait()
     peers = asked_ref.shape[0]
     each = peers // GROUPS
     sends = []
@@ -114,7 +130,7 @@
 
         def one(p, _):
             base = pl.multiple_of(p * DISTINCT, DISTINCT)
-            gather_rows(lambda k: asked_ref[p, 0, k], rows_ref, held_ref, out_ref, base, DISTINCT)
+            gather_rows(lambda k: asked_ref[p, k], rows_ref, held_ref, out_ref, base, DISTINCT)
             return 0
 
         lax.fori_loop(g * each, (g + 1) * each, one, 0)
@@ -126,13 +142,13 @@
 
 
 def slots_kernel(
-    owner_ref, rows_ref, place_ref, src_ref, rcv_ref, taper_ref, key_ref, value_ref, rank_ref
+    owner_ref, rows_ref, src_ref, rcv_ref, taper_ref, key_ref, value_ref, rank_ref
 ):
-    lines, cap = place_ref.shape
+    lines, cap = rows_ref.shape
     outs = rcv_ref.shape[0]
     rows = rows_ref[...]
-    columns = turned(rows)
-    places = turned(place_ref[...])
+    columns, place = first_entries(rows)
+    places = turned(place)
     for g in range(lines):
         same = columns[:, g : g + 1] == rows[g : g + 1, :]
         rank_ref[g : g + 1, :] = jnp.max(
@@ -297,20 +313,21 @@
     tr_rows, samples = traces.shape
     outs, aper = src_index.shape
     cap = fetch_rows.shape[1]
-    asked, place = pl.pallas_call(
-        distinct_kernel,
-        in_specs=[SMEM, VMEM],
-        out_specs=[VMEM, VMEM],
-        out_shape=[shape((sails, 1, cap), jnp.int32), shape((sails, cap), jnp.int32)],
+    lists = pl.pallas_call(
+        order_kernel,
+        in_specs=[SMEM, HBM],
+        out_specs=HBM,
+        out_shape=shape((sails, 1, cap), jnp.int32),
+        scratch_shapes=[pltpu.SemaphoreType.DMA((sails,))],
         compiler_params=params(56),
-        name="distinct",
-    )(line_owner, fetch_rows)
-    asked = lax.all_to_all(asked, "sail", split_axis=0, concat_axis=0, tiled=True)
+        name="order",
+    )(line_owner, fetch_rows.reshape(sails, 1, cap))
+    lists = lax.all_to_all(lists, "sail", split_axis=0, concat_axis=0, tiled=True)
     fetched = sails * DISTINCT
     parts = tr_rows // STEP
     spectra, outgoing = pl.pallas_call(
         spectra_kernel,
-        in_specs=[SMEM, HBM, HBM],
+        in_specs=[VMEM, HBM, HBM],
         out_specs=[HBM, HBM],
         out_shape=[shape((tr_rows, samples), BF16), shape((fetched, samples), BF16)],
         scratch_shapes=[
@@ -320,14 +337,17 @@
             pltpu.VMEM((tr_rows * 4 + 2 * PAD, 128), F32),
             pltpu.VMEM((fetched * 4, 128), F32),
             pltpu.VMEM((fetched, samples), BF16),
+            pltpu.VMEM((sails, cap), jnp.int32),
+            pltpu.SMEM((sails, cap), jnp.int32),
             pltpu.SemaphoreType.DMA((parts,)),
+            pltpu.SemaphoreType.DMA,
             pltpu.SemaphoreType.DMA,
             pltpu.SemaphoreType.DMA((parts,)),
             pltpu.SemaphoreType.DMA((GROUPS,)),
         ],
         compiler_params=params(56),
         name="spectra",
-    )(asked, traces, forward_table(samples))
+    )(lists.reshape(sails, cap), traces, forward_table(samples))
     arrived = lax.all_to_all(
         outgoing.reshape(sails, DISTINCT, samples), "sail", split_axis=0, concat_axis=0, tiled=True
     ).reshape(fetched, samples)
@@ -336,14 +356,14 @@
     after = lax.ppermute(spectra[:HALO], "cable", [(j, i) for i, j in up])
     key, value = pl.pallas_call(
         slots_kernel,
-        in_specs=[SMEM] + [VMEM] * 5,
+        in_specs=[SMEM] + [VMEM] * 4,
         out_specs=[VMEM, VMEM],
         out_shape=[shape((outs, aper), jnp.int32)] * 2,
         scratch_shapes=[pltpu.VMEM((sails, cap), jnp.int32)],
         compiler_params=params(56),
         name="slots",
         cost_estimate=cost(0, 10 << 20),
-    )(line_owner, fetch_rows, place, src_index, rcv_index, taper_index)
+    )(line_owner, fetch_rows, src_index, rcv_index, taper_index)
     count = outs * aper
     key, value = lax.sort((key.reshape(-1), value.reshape(-1)), num_keys=1, is_stable=False)
     tiles = count // TILE

time: 94.1 us -> 93.5 us (level)
  no operation moved by 1% of the time
where the time goes in v5:
time: 93.5 us; the launch traced here: 92.9 us
  Pallas kernels  37.2 us (40%)
  blocking collectives  21.3 us (23%)
  waiting for transfers between devices  16 us (17%)
  starting transfers between devices  9.59 us (10%)
  other arithmetic  7.1 us (8%)
  local copies, waits for them, and re-layouts  1.67 us (2%)
    all_to_all x1, blocking collectives, body(): lax.all_to_all(lists, 'sail', split_axis=0, concat_axis=0, tiled=True)  21.3 us
    all_to_all x1, waiting for transfers between devices, body(): lax.all_to_all(outgoing.reshape(sails, DISTINCT, samples), 'sail', split_...  14.2 us
    pallas_call x1, Pallas kernels, body(): pl.pallas_call(sources_kernel, grid=(8,), in_specs=[SMEM, HBM, VMEM, VMEM...  14 us
    pallas_call x1, Pallas kernels, body(): pl.pallas_call(pairs_kernel, in_specs=[SMEM, SMEM, VMEM, HBM, VMEM, HBM],...  8.63 us
    pallas_call x1, Pallas kernels, body(): pl.pallas_call(spectra_kernel, in_specs=[VMEM, HBM, HBM], out_specs=[HBM,...  7.28 us
    sort x1, other arithmetic, body(): lax.sort((key.reshape(-1), value.reshape(-1)), num_keys=1, is_stable=False)  7.09 us
    pallas_call x1, Pallas kernels, body(): pl.pallas_call(slots_kernel, in_specs=[SMEM] + [VMEM] * 4, out_specs=[VME...  4.73 us
    all_to_all x1, starting transfers between devices, body(): lax.all_to_all(outgoing.reshape(sails, DISTINCT, samples), 'sail', split_...  4.02 us
  transfers between devices with their start and end apart: 3, of which 2 were waited for; matrix products, arithmetic and copies ran while one was open for 9% of the time, Pallas kernels for 20%

profile of v5, /device:TPU:4, one launch (start us, length us, event | category | flops | bytes accessed | tf_op | source)
XLA Modules:
  0.0 92.9 jit_solution(11315903376105981683)
XLA Ops:
  0.0 2.6 %order.1 = s32[32,1,128]{2,1,0:T(1,128)} custom-call(s32[32]{0:T(128)} %owner_ref.3, s32[32,1,128]{2,1,0:T(1,128)} %bitcast.27), custom_call_target="tpu_custom_call" | custom-call | tf_op jit(solution)/shard_map/order/pallas_call | solution.py:316
  2.6 21.3 %all_to_all.10 = s32[32,1,128]{2,1,0:T(1,128)} all-to-all(s32[32,1,128]{2,1,0:T(1,128)} %order.1), channel_id=1, replica_groups=mesh['sail'=32,'cable'=8] {'sail'}, dimensions={0} | all-to-all | bytes 32768 | tf_op jit(solution)/shard_map/all_to_all | solution.py:325
  23.9 7.3 %spectra.1 = (bf16[2048,512]{1,0:T(8,128)(2,1)}, bf16[2048,512]{1,0:T(8,128)(2,1)}) custom-call(s32[32,128]{1,0:T(8,128)} %bitcast.26, bf16[2048,512]{1,0:T(8,128)(2,1)} %traces_hbm.1, bf16[512,512]{1,0:T(8,128)(2,1)} %constant.20.clone.table_hbm), custom_call_target="tpu_custom_call" | custom-call | tf_op jit(solution)/shard_map/spectra/pallas_call | solution.py:328
  31.2 4.0 %all-to-all-start.1 = ((bf16[32,64,512]{2,1,0:T(8,128)(2,1)}), bf16[32,64,512]{2,1,0:T(8,128)(2,1)S(1)}, u32[]{:S(2)}, u32[]{:S(2)}) async-start(bf16[32,64,512]{2,1,0:T(8,128)(2,1)} %bitcast.25), calls=%async_computation.1 | async-start | bytes 4194304 | tf_op jit(solution)/shard_map/all_to_all | solution.py:351
  35.2 4.7 %slots.1 = (s32[64,128]{1,0:T(8,128)}, s32[64,128]{1,0:T(8,128)}) custom-call(s32[32]{0:T(128)} %owner_ref.3, s32[32,128]{1,0:T(8,128)} %rows_ref.1, s32[64,128]{1,0:T(8,128)} %src_ref.1, s32[64,128]{1,0:T(8,128)} %rcv_ref.1, s32[64,128]{1,0:T(8,128)} %taper_ref.2), custom_call_target="tpu_custom_call" | custom-call | bytes 10485760 | tf_op jit(solution)/shard_map/slots/pallas_call | solution.py:357
  39.9 7.1 %sort.15 = (s32[8192]{0:T(1024)S(1)}, s32[8192]{0:T(1024)}) sort(s32[8192]{0:T(1024)} %bitcast.28, s32[8192]{0:T(1024)} %bitcast.29), dimensions={0}, to_apply=%region_0.0 | sort | flops 106496 | bytes 131072 | tf_op jit(solution)/shard_map/sort | solution.py:368
  47.0 0.1 slice.9
  47.1 0.9 fusion.3
  48.0 1.9 %collective-permute-start = (bf16[64,512]{1,0:T(8,128)(2,1)S(1)}, bf16[64,512]{1,0:T(8,128)(2,1)S(1)}, u32[]{:S(2)}, u32[]{:S(2)}) collective-permute-start(bf16[64,512]{1,0:T(8,128)(2,1)S(1)} %get-tuple-element.18), channel_id=1, source_target_pairs={{0,1},{1,2},{2,3},{3,4},{4,5},{5,6},{6,7},{8,9},{9,10},{10,11},{11... | collective-permute-start | bytes 196616 | tf_op jit(solution)/shard_map/ppermute | solution.py:355
  49.9 3.6 %collective-permute-start.1 = (bf16[64,512]{1,0:T(8,128)(2,1)S(1)}, bf16[64,512]{1,0:T(8,128)(2,1)S(1)}, u32[]{:S(2)}, u32[]{:S(2)}) collective-permute-start(bf16[64,512]{1,0:T(8,128)(2,1)S(1)} %get-tuple-element.17), channel_id=1, source_target_pairs={{1,0},{2,1},{3,2},{4,3},{5,4},{6,5},{7,6},{9,8},{10,9},{11,10},{12... | collective-permute-start | bytes 196616 | tf_op jit(solution)/shard_map/ppermute | solution.py:356
  53.6 0.1 copy.12.ends_ref
  53.7 0.0 collective-permute-done.before_ref
  53.7 0.0 copy-start.2
  53.7 1.8 %collective-permute-done.1.after_ref = bf16[64,512]{1,0:T(8,128)(2,1)S(1)} collective-permute-done((bf16[64,512]{1,0:T(8,128)(2,1)S(1)}, bf16[64,512]{1,0:T(8,128)(2,1)S(1)}, u32[]{:S(2)}, u32[]{:S(2)}) %collective-permute-start.1) | collective-permute-done | bytes 65568 | tf_op jit(solution)/shard_map/ppermute | solution.py:356
  55.5 0.0 copy-start.3
  55.5 0.0 copy-done.2
  55.5 0.6 copy-done.3
  56.1 0.0 copy-start
  56.1 0.0 copy-start.1
  56.1 14.0 %sources.1 = bf16[8192,512]{1,0:T(8,128)(2,1)} custom-call(s32[8192]{0:T(1024)} %get-tuple-element.14.src_ref, bf16[2048,512]{1,0:T(8,128)(2,1)} %get-tuple-element.15.spectra_hbm, bf16[64,512]{1,0:T(8,128)(2,1)} %copy-done.2, bf16[64,512]{1,0:T(8,128)(2,1)} %copy-done.3), custom_call_target="tpu_custom_call" | custom-call | bytes 41943040 | tf_op jit(solution)/shard_map/sources/pallas_call | solution.py:373
  70.0 14.2 %all-to-all-done.1 = bf16[32,64,512]{2,1,0:T(8,128)(2,1)S(1)} async-done(((bf16[32,64,512]{2,1,0:T(8,128)(2,1)}), bf16[32,64,512]{2,1,0:T(8,128)(2,1)S(1)}, u32[]{:S(2)}, u32[]{:S(2)}) %all-to-all-start.1) | async-done | bytes 2097184 | tf_op jit(solution)/shard_map/all_to_all | solution.py:351
  84.3 0.0 copy-done
  84.3 0.0 copy-done.1
  84.3 8.6 %pairs.1 = bf16[64,512]{1,0:T(8,128)(2,1)} custom-call(s32[2,32]{1,0:T(2,128)S(1)} %copy.12.ends_ref, f32[16]{0:T(128)S(1)} %copy-done.1, s32[32,256]{1,0:T(8,128)S(1)} %reshape.27.key_ref, bf16[32,256,512]{2,1,0:T(8,128)(2,1)} %bitcast.24, bf16[2048,512]{1,0:T(8,128)(2,1)S(1)} %bitcast.23, bf16[512,512]{1,0:T(8,128)(2,1)S(1)} %copy-done), custom_call_target="tpu_custom_call" | custom-call | tf_op jit(solution)/shard_map/pairs/pallas_call | solution.py:389
  (2 shorter events, 0.0 us)
Async XLA Ops:
  31.2 53.1 %all-to-all-start.1 = ((bf16[32,64,512]{2,1,0:T(8,128)(2,1)}), bf16[32,64,512]{2,1,0:T(8,128)(2,1)S(1)}, u32[]{:S(2)}, u32[]{:S(2)}) async-start(bf16[32,64,512]{2,1,0:T(8,128)(2,1)} %bitcast.25), calls=%async_computation.1 | async-start | bytes 4194304 | tf_op jit(solution)/shard_map/all_to_all | solution.py:351
  48.0 5.7 %collective-permute-start = (bf16[64,512]{1,0:T(8,128)(2,1)S(1)}, bf16[64,512]{1,0:T(8,128)(2,1)S(1)}, u32[]{:S(2)}, u32[]{:S(2)}) collective-permute-start(bf16[64,512]{1,0:T(8,128)(2,1)S(1)} %get-tuple-element.18), channel_id=1, source_target_pairs={{0,1},{1,2},{2,3},{3,4},{4,5},{5,6},{6,7},{8,9},{9,10},{10,11},{11... | collective-permute-start | bytes 196616 | tf_op jit(solution)/shard_map/ppermute | solution.py:355
  49.9 5.5 %collective-permute-start.1 = (bf16[64,512]{1,0:T(8,128)(2,1)S(1)}, bf16[64,512]{1,0:T(8,128)(2,1)S(1)}, u32[]{:S(2)}, u32[]{:S(2)}) collective-permute-start(bf16[64,512]{1,0:T(8,128)(2,1)S(1)} %get-tuple-element.17), channel_id=1, source_target_pairs={{1,0},{2,1},{3,2},{4,3},{5,4},{6,5},{7,6},{9,8},{10,9},{11,10},{12... | collective-permute-start | bytes 196616 | tf_op jit(solution)/shard_map/ppermute | solution.py:356
  53.7 1.8 %copy-start.2 = (bf16[64,512]{1,0:T(8,128)(2,1)}, bf16[64,512]{1,0:T(8,128)(2,1)S(1)}, u32[]{:S(2)}) copy-start(bf16[64,512]{1,0:T(8,128)(2,1)S(1)} %collective-permute-done.before_ref) | copy-start | bytes 196612
  55.5 0.6 copy-start.3
  56.1 28.2 %copy-start = (bf16[512,512]{1,0:T(8,128)(2,1)S(1)}, bf16[512,512]{1,0:T(8,128)(2,1)}, u32[]{:S(2)}) copy-start(bf16[512,512]{1,0:T(8,128)(2,1)} %constant.21.clone.synth_hbm) | copy-start | bytes 1572868
  56.1 28.2 %copy-start.1 = (f32[16]{0:T(128)S(1)}, f32[16]{0:T(128)}, u32[]{:S(2)}) copy-start(f32[16]{0:T(128)} %taper_ref.3) | copy-start | bytes 196

commit v6 on v5

--- a/solution.py
+++ b/solution.py
@@ -17,6 +17,7 @@
 GROUPS = 4
 CHUNKS = 8
 UNROLL = 8
+HEAD = 4
 F32 = jnp.float32
 BF16 = jnp.bfloat16
 
@@ -41,15 +42,9 @@
     return jnp.concatenate([values, jnp.zeros((cap - lines, cap), values.dtype)], axis=0).T
 
 
-def order_kernel(owner_ref, rows_hbm, out_hbm, sems):
-    copies = []
-    for g in range(rows_hbm.shape[0]):
-        copies.append(
-            pltpu.make_async_copy(rows_hbm.at[g], out_hbm.at[owner_ref[g]], sems.at[g])
-        )
-        copies[g].start()
-    for copy in copies:
-        copy.wait()
+def order_kernel(owner_ref, rows_ref, out_ref):
+    for g in range(rows_ref.shape[0]):
+        out_ref[owner_ref[g]] = rows_ref[g : g + 1, :]
 
 
 def first_entries(rows):
@@ -86,9 +81,9 @@
 
 
 def spectra_kernel(
-    lists_ref, traces_hbm, table_hbm, spectra_hbm, out_hbm,
-    traces_ref, table_ref, spectra_ref, rows_ref, held_ref, out_ref, distinct_ref, asked_ref,
-    in_sems, table_sem, asked_sem, store_sems, out_sems,
+    lists_ref, traces_hbm, table_hbm, first_hbm, last_hbm, out_hbm,
+    traces_ref, table_ref, edge_ref, rows_ref, held_ref, out_ref, distinct_ref, asked_ref,
+    in_sems, table_sem, asked_sem, edge_sems, out_sems,
 ):
     parts = len(range(0, traces_ref.shape[0], STEP))
     table = pltpu.make_async_copy(table_hbm, table_ref, table_sem)
@@ -98,9 +93,6 @@
     for b in range(parts):
         at = pl.ds(b * STEP, STEP)
         loads.append(pltpu.make_async_copy(traces_hbm.at[at], traces_ref.at[at], in_sems.at[b]))
-        stores.append(
-            pltpu.make_async_copy(spectra_ref.at[at], spectra_hbm.at[at], store_sems.at[b])
-        )
         loads[b].start()
     lists = lists_ref[...]
     columns, place = first_entries(lists)
@@ -119,9 +111,12 @@
         spectra = jnp.dot(
             traces_ref[at, :], table_ref[...], preferred_element_type=F32
         ).astype(BF16)
-        spectra_ref[at, :] = spectra
         put_rows(rows_ref, PAD + b * STEP * 4, spectra.astype(F32))
-        stores[b].start()
+        for edge, hbm, part, first in ((0, first_hbm, 0, 0), (1, last_hbm, parts - 1, STEP - HALO)):
+            if b == part:
+                edge_ref[edge] = spectra[first : first + HALO]
+                stores.append(pltpu.make_async_copy(edge_ref.at[edge], hbm, edge_sems.at[edge]))
+                stores[edge].start()
     asking.wait()
     peers = asked_ref.shape[0]
     each = peers // GROUPS
@@ -182,26 +177,34 @@
 
 
 def sources_kernel(
-    src_ref, spectra_hbm, before_ref, after_ref, out_ref, spectra_ref, all_ref, held_ref, sem
+    src_ref, traces_hbm, table_hbm, before_ref, after_ref, out_ref,
+    traces_ref, table_ref, all_ref, held_ref, sems,
 ):
     step = pl.program_id(0)
 
     @pl.when(step == 0)
     def _():
-        own = spectra_ref.shape[0]
-        copy = pltpu.make_async_copy(spectra_hbm, spectra_ref, sem)
-        copy.start()
+        own = traces_ref.shape[0]
+        copies = [
+            pltpu.make_async_copy(traces_hbm, traces_ref, sems.at[0]),
+            pltpu.make_async_copy(table_hbm, table_ref, sems.at[1]),
+        ]
+        for copy in copies:
+            copy.start()
         put_rows(all_ref, PAD, before_ref[...].astype(F32))
         put_rows(all_ref, PAD + (HALO + own) * 4, after_ref[...].astype(F32))
-        copy.wait()
+        for copy in copies:
+            copy.wait()
 
         def one(b, _):
-            at = pl.multiple_of(b * TILE, TILE)
-            block = spectra_ref[pl.ds(at, TILE), :].astype(F32)
-            put_rows(all_ref, PAD + HALO * 4 + at * 4, block)
+            at = pl.multiple_of(b * STEP, STEP)
+            spectra = jnp.dot(
+                traces_ref[pl.ds(at, STEP), :], table_ref[...], preferred_element_type=F32
+            ).astype(BF16)
+            put_rows(all_ref, PAD + HALO * 4 + at * 4, spectra.astype(F32))
             return 0
 
-        lax.fori_loop(0, own // TILE, one, 0)
+        lax.fori_loop(0, own // STEP, one, 0)
 
     def one(c, _):
         base = pl.multiple_of(c * 64, 64)
@@ -255,14 +258,9 @@
     sub = lax.broadcasted_iota(jnp.int32, (TILE, TILE), 0)
     out = lax.broadcasted_iota(jnp.int32, (outs, TILE), 0)
 
-    def some(c, _):
-        @pl.when(c * UNROLL < tiles)
-        def _():
-            for u in range(UNROLL // chunk):
-                load(c * (UNROLL // chunk) + u).wait()
-
-        for u in range(UNROLL):
-            meet = meet_ref[c * UNROLL + u]
+    def some(base, count):
+        for u in range(count):
+            meet = meet_ref[base + u]
             t = meet & 63
             b = meet // 64
             at = pl.multiple_of(jnp.minimum(b, last) * TILE, TILE)
@@ -274,17 +272,39 @@
             right = lax.dot_general(
                 hot, arrived_ref[pl.ds(at, TILE), :], (((0,), (0,)), ((), ())),
                 preferred_element_type=F32,
-            )
-            right = right.astype(BF16)
+            ).astype(BF16)
             left = source_ref[t]
             sr, si, rr, ri = left[:, :half], left[:, half:], right[:, :half], right[:, half:]
             product = jnp.concatenate([sr * rr - si * ri, sr * ri + si * rr], axis=1)
             product_ref[u * TILE : (u + 1) * TILE, :] = product
             hot_ref[:, u * TILE : (u + 1) * TILE] = spread
-        sum_ref[...] += jnp.dot(hot_ref[...], product_ref[...], preferred_element_type=F32)
+        width = count * TILE
+        sum_ref[...] += jnp.dot(
+            hot_ref[:, :width], product_ref[:width, :], preferred_element_type=F32
+        )
+
+    load(0).wait()
+    some(0, HEAD)
+
+    def later(c, _):
+        base = HEAD + c * UNROLL
+
+        @pl.when(base < tiles)
+        def _():
+            for u in range(UNROLL // chunk):
+                part = base // chunk + u
+
+                @pl.when(part < CHUNKS)
+                def _():
+                    load(part).wait()
+
+        some(base, UNROLL)
         return 0
 
-    lax.fori_loop(0, meet_ref.shape[0] // UNROLL, some, 0)
+    rest = (meets - HEAD) % UNROLL
+    lax.fori_loop(0, (meets - HEAD) // UNROLL, later, 0)
+    if rest:
+        some(meets - rest, rest)
     synth_copy.wait()
     summed = sum_ref[...].astype(BF16)
     out_ref[...] = jnp.dot(summed, synth_ref[...], preferred_element_type=F32).astype(BF16)
@@ -315,25 +335,29 @@
     cap = fetch_rows.shape[1]
     lists = pl.pallas_call(
         order_kernel,
-        in_specs=[SMEM, HBM],
-        out_specs=HBM,
+        in_specs=[SMEM, VMEM],
+        out_specs=VMEM,
         out_shape=shape((sails, 1, cap), jnp.int32),
-        scratch_shapes=[pltpu.SemaphoreType.DMA((sails,))],
         compiler_params=params(56),
         name="order",
-    )(line_owner, fetch_rows.reshape(sails, 1, cap))
+    )(line_owner, fetch_rows)
     lists = lax.all_to_all(lists, "sail", split_axis=0, concat_axis=0, tiled=True)
     fetched = sails * DISTINCT
     parts = tr_rows // STEP
-    spectra, outgoing = pl.pallas_call(
+    table = forward_table(samples)
+    first, last, outgoing = pl.pallas_call(
         spectra_kernel,
         in_specs=[VMEM, HBM, HBM],
-        out_specs=[HBM, HBM],
-        out_shape=[shape((tr_rows, samples), BF16), shape((fetched, samples), BF16)],
+        out_specs=[HBM, HBM, HBM],
+        out_shape=[
+            shape((HALO, samples), BF16),
+            shape((HALO, samples), BF16),
+            shape((fetched, samples), BF16),
+        ],
         scratch_shapes=[
             pltpu.VMEM((tr_rows, samples), BF16),
             pltpu.VMEM((samples, samples), BF16),
-            pltpu.VMEM((tr_rows, samples), BF16),
+            pltpu.VMEM((2, HALO, samples), BF16),
             pltpu.VMEM((tr_rows * 4 + 2 * PAD, 128), F32),
             pltpu.VMEM((fetched * 4, 128), F32),
             pltpu.VMEM((fetched, samples), BF16),
@@ -342,18 +366,18 @@
             pltpu.SemaphoreType.DMA((parts,)),
             pltpu.SemaphoreType.DMA,
             pltpu.SemaphoreType.DMA,
-            pltpu.SemaphoreType.DMA((parts,)),
+            pltpu.SemaphoreType.DMA((2,)),
             pltpu.SemaphoreType.DMA((GROUPS,)),
         ],
         compiler_params=params(56),
         name="spectra",
-    )(lists.reshape(sails, cap), traces, forward_table(samples))
+    )(lists.reshape(sails, cap), traces, table)
     arrived = lax.all_to_all(
         outgoing.reshape(sails, DISTINCT, samples), "sail", split_axis=0, concat_axis=0, tiled=True
     ).reshape(fetched, samples)
     up = [(i, i + 1) for i in range(cables - 1)]
-    before = lax.ppermute(spectra[tr_rows - HALO :], "cable", up)
-    after = lax.ppermute(spectra[:HALO], "cable", [(j, i) for i, j in up])
+    before = lax.ppermute(last, "cable", up)
+    after = lax.ppermute(first, "cable", [(j, i) for i, j in up])
     key, value = pl.pallas_call(
         slots_kernel,
         in_specs=[SMEM] + [VMEM] * 4,
@@ -369,23 +393,24 @@
     tiles = count // TILE
     blocks = fetched // TILE
     ends = key.reshape(tiles, TILE)[:, :: TILE - 1].T // (16 * outs * TILE)
-    meets = -(-(tiles + blocks) // UNROLL) * UNROLL
+    meets = -(-(tiles + blocks) // HEAD) * HEAD
     sources = pl.pallas_call(
         sources_kernel,
         grid=(8,),
-        in_specs=[SMEM, HBM, VMEM, VMEM],
+        in_specs=[SMEM, HBM, HBM, VMEM, VMEM],
         out_specs=pl.BlockSpec((count // 8, samples), lambda b: (b, 0)),
         out_shape=shape((count, samples), BF16),
         scratch_shapes=[
             pltpu.VMEM((tr_rows, samples), BF16),
+            pltpu.VMEM((samples, samples), BF16),
             pltpu.VMEM(((tr_rows + 2 * HALO) * 4 + 2 * PAD, 128), F32),
             pltpu.VMEM((count // 8 * 4, 128), F32),
-            pltpu.SemaphoreType.DMA,
+            pltpu.SemaphoreType.DMA((2,)),
         ],
         compiler_params=params(56),
         name="sources",
         cost_estimate=cost(0, 40 << 20),
-    )(value, spectra, before, after)
+    )(value, traces, table, before, after)
     return pl.pallas_call(
         pairs_kernel,
         in_specs=[SMEM, SMEM, VMEM, HBM, VMEM, HBM],

time: 93.5 us -> 92.2 us (0.986)
  transfers between devices with their start and end apart: 3 -> 3, of which waited for: 2 -> 2; matrix products, arithmetic and copies ran while one was open for 9% -> 8% of each run, Pallas kernels for 20% -> 22%
where the time goes in v6:
time: 92.2 us; the launch traced here: 91.6 us
  Pallas kernels  37.1 us (40%)
  blocking collectives  21.3 us (23%)
  waiting for transfers between devices  15.5 us (17%)
  starting transfers between devices  9.71 us (11%)
  other arithmetic  7.11 us (8%)
    all_to_all x1, blocking collectives, body(): lax.all_to_all(lists, 'sail', split_axis=0, concat_axis=0, tiled=True)  21.3 us
    pallas_call x1, Pallas kernels, body(): pl.pallas_call(sources_kernel, grid=(8,), in_specs=[SMEM, HBM, HBM, VMEM,...  15.3 us
    all_to_all x1, waiting for transfers between devices, body(): lax.all_to_all(outgoing.reshape(sails, DISTINCT, samples), 'sail', split_...  13.7 us
    pallas_call x1, Pallas kernels, body(): pl.pallas_call(pairs_kernel, in_specs=[SMEM, SMEM, VMEM, HBM, VMEM, HBM],...  8.44 us
    pallas_call x1, Pallas kernels, body(): pl.pallas_call(spectra_kernel, in_specs=[VMEM, HBM, HBM], out_specs=[HBM,...  7.26 us
    sort x1, other arithmetic, body(): lax.sort((key.reshape(-1), value.reshape(-1)), num_keys=1, is_stable=False)  7.09 us
    pallas_call x1, Pallas kernels, body(): pl.pallas_call(slots_kernel, in_specs=[SMEM] + [VMEM] * 4, out_specs=[VME...  4.73 us
    all_to_all x1, starting transfers between devices, body(): lax.all_to_all(outgoing.reshape(sails, DISTINCT, samples), 'sail', split_...  4.15 us
  transfers between devices with their start and end apart: 3, of which 2 were waited for; matrix products, arithmetic and copies ran while one was open for 8% of the time, Pallas kernels for 22%

profile of v6, /device:TPU:4, one launch (start us, length us, event | category | flops | bytes accessed | tf_op | source)
XLA Modules:
  0.0 91.6 jit_solution(9222116967951996629)
XLA Ops:
  0.0 1.4 %order.1 = s32[32,1,128]{2,1,0:T(1,128)} custom-call(s32[32]{0:T(128)} %owner_ref.3, s32[32,128]{1,0:T(8,128)} %rows_ref.3), custom_call_target="tpu_custom_call" | custom-call | tf_op jit(solution)/shard_map/order/pallas_call | solution.py:336
  1.4 21.3 %all_to_all.10 = s32[32,1,128]{2,1,0:T(1,128)} all-to-all(s32[32,1,128]{2,1,0:T(1,128)} %order.1), channel_id=1, replica_groups=mesh['sail'=32,'cable'=8] {'sail'}, dimensions={0} | all-to-all | bytes 32768 | tf_op jit(solution)/shard_map/all_to_all | solution.py:344
  22.7 7.3 %spectra.1 = (bf16[64,512]{1,0:T(8,128)(2,1)}, bf16[64,512]{1,0:T(8,128)(2,1)}, bf16[2048,512]{1,0:T(8,128)(2,1)}) custom-call(s32[32,128]{1,0:T(8,128)} %bitcast.25, bf16[2048,512]{1,0:T(8,128)(2,1)} %traces_hbm.3, bf16[512,512]{1,0:T(8,128)(2,1)} %constant.20.clone.table_hbm), custom_call_target="tpu_custom_call" | custom-call | tf_op jit(solution)/shard_map/spectra/pallas_call | solution.py:348
  29.9 0.0 copy-start.5
  29.9 0.0 copy-start.4
  29.9 4.2 %all-to-all-start.1 = ((bf16[32,64,512]{2,1,0:T(8,128)(2,1)}), bf16[32,64,512]{2,1,0:T(8,128)(2,1)S(1)}, u32[]{:S(2)}, u32[]{:S(2)}) async-start(bf16[32,64,512]{2,1,0:T(8,128)(2,1)} %bitcast.24), calls=%async_computation.1 | async-start | bytes 4194304 | tf_op jit(solution)/shard_map/all_to_all | solution.py:375
  34.1 4.7 %slots.1 = (s32[64,128]{1,0:T(8,128)}, s32[64,128]{1,0:T(8,128)}) custom-call(s32[32]{0:T(128)} %owner_ref.3, s32[32,128]{1,0:T(8,128)} %rows_ref.3, s32[64,128]{1,0:T(8,128)} %src_ref.1, s32[64,128]{1,0:T(8,128)} %rcv_ref.1, s32[64,128]{1,0:T(8,128)} %taper_ref.2), custom_call_target="tpu_custom_call" | custom-call | bytes 10485760 | tf_op jit(solution)/shard_map/slots/pallas_call | solution.py:381
  38.8 7.1 %sort.15 = (s32[8192]{0:T(1024)S(1)}, s32[8192]{0:T(1024)}) sort(s32[8192]{0:T(1024)} %bitcast.26, s32[8192]{0:T(1024)} %bitcast.27), dimensions={0}, to_apply=%region_0.0 | sort | flops 106496 | bytes 131072 | tf_op jit(solution)/shard_map/sort | solution.py:392
  45.9 0.1 slice.3
  46.0 0.0 copy-done.5
  46.0 1.9 %collective-permute-start = (bf16[64,512]{1,0:T(8,128)(2,1)S(1)}, bf16[64,512]{1,0:T(8,128)(2,1)S(1)}, u32[]{:S(2)}, u32[]{:S(2)}) collective-permute-start(bf16[64,512]{1,0:T(8,128)(2,1)S(1)} %copy-done.5), channel_id=1, source_target_pairs={{0,1},{1,2},{2,3},{3,4},{4,5},{5,6},{6,7},{8,9},{9,10},{10,11},{11... | collective-permute-start | bytes 196616 | tf_op jit(solution)/shard_map/ppermute | solution.py:379
  47.9 0.0 copy-done.4
  48.0 3.6 %collective-permute-start.1 = (bf16[64,512]{1,0:T(8,128)(2,1)S(1)}, bf16[64,512]{1,0:T(8,128)(2,1)S(1)}, u32[]{:S(2)}, u32[]{:S(2)}) collective-permute-start(bf16[64,512]{1,0:T(8,128)(2,1)S(1)} %copy-done.4), channel_id=1, source_target_pairs={{1,0},{2,1},{3,2},{4,3},{5,4},{6,5},{7,6},{9,8},{10,9},{11,10},{12... | collective-permute-start | bytes 196616 | tf_op jit(solution)/shard_map/ppermute | solution.py:380
  51.6 0.1 copy.12.ends_ref
  51.7 0.0 collective-permute-done.before_ref
  51.7 0.0 copy-start.2
  51.7 1.8 %collective-permute-done.1.after_ref = bf16[64,512]{1,0:T(8,128)(2,1)S(1)} collective-permute-done((bf16[64,512]{1,0:T(8,128)(2,1)S(1)}, bf16[64,512]{1,0:T(8,128)(2,1)S(1)}, u32[]{:S(2)}, u32[]{:S(2)}) %collective-permute-start.1) | collective-permute-done | bytes 65568 | tf_op jit(solution)/shard_map/ppermute | solution.py:380
  53.5 0.0 copy-start.3
  53.5 0.0 copy-done.2
  53.5 0.6 copy-done.3
  54.1 0.0 copy-start
  54.1 0.0 copy-start.1
  54.1 15.3 %sources.1 = bf16[8192,512]{1,0:T(8,128)(2,1)} custom-call(s32[8192]{0:T(1024)} %get-tuple-element.15.src_ref, bf16[2048,512]{1,0:T(8,128)(2,1)} %traces_hbm.3, bf16[512,512]{1,0:T(8,128)(2,1)} %constant.20.clone.table_hbm, bf16[64,512]{1,0:T(8,128)(2,1)} %copy-done.2, bf16[64,512]{1,0:T(8,128)(2,1)} %copy-done.3), custom_call_target="tpu_custom_call" | custom-call | bytes 41943040 | tf_op jit(solution)/shard_map/sources/pallas_call | solution.py:397
  69.5 13.7 %all-to-all-done.1 = bf16[32,64,512]{2,1,0:T(8,128)(2,1)S(1)} async-done(((bf16[32,64,512]{2,1,0:T(8,128)(2,1)}), bf16[32,64,512]{2,1,0:T(8,128)(2,1)S(1)}, u32[]{:S(2)}, u32[]{:S(2)}) %all-to-all-start.1) | async-done | bytes 2097184 | tf_op jit(solution)/shard_map/all_to_all | solution.py:375
  83.2 0.0 copy-done
  83.2 0.0 copy-done.1
  83.2 8.4 %pairs.1 = bf16[64,512]{1,0:T(8,128)(2,1)} custom-call(s32[2,32]{1,0:T(2,128)S(1)} %copy.12.ends_ref, f32[16]{0:T(128)S(1)} %copy-done.1, s32[32,256]{1,0:T(8,128)S(1)} %reshape.24.key_ref, bf16[32,256,512]{2,1,0:T(8,128)(2,1)} %bitcast.23, bf16[2048,512]{1,0:T(8,128)(2,1)S(1)} %bitcast.22, bf16[512,512]{1,0:T(8,128)(2,1)S(1)} %copy-done), custom_call_target="tpu_custom_call" | custom-call | tf_op jit(solution)/shard_map/pairs/pallas_call | solution.py:414
  (2 shorter events, 0.0 us)
Async XLA Ops:
  29.9 16.1 %copy-start.5 = (bf16[64,512]{1,0:T(8,128)(2,1)S(1)}, bf16[64,512]{1,0:T(8,128)(2,1)}, u32[]{:S(2)}) copy-start(bf16[64,512]{1,0:T(8,128)(2,1)} %get-tuple-element.16) | copy-start | bytes 196612
  29.9 18.0 %copy-start.4 = (bf16[64,512]{1,0:T(8,128)(2,1)S(1)}, bf16[64,512]{1,0:T(8,128)(2,1)}, u32[]{:S(2)}) copy-start(bf16[64,512]{1,0:T(8,128)(2,1)} %get-tuple-element.17) | copy-start | bytes 196612
  29.9 53.2 %all-to-all-start.1 = ((bf16[32,64,512]{2,1,0:T(8,128)(2,1)}), bf16[32,64,512]{2,1,0:T(8,128)(2,1)S(1)}, u32[]{:S(2)}, u32[]{:S(2)}) async-start(bf16[32,64,512]{2,1,0:T(8,128)(2,1)} %bitcast.24), calls=%async_computation.1 | async-start | bytes 4194304 | tf_op jit(solution)/shard_map/all_to_all | solution.py:375
  46.0 5.7 %collective-permute-start = (bf16[64,512]{1,0:T(8,128)(2,1)S(1)}, bf16[64,512]{1,0:T(8,128)(2,1)S(1)}, u32[]{:S(2)}, u32[]{:S(2)}) collective-permute-start(bf16[64,512]{1,0:T(8,128)(2,1)S(1)} %copy-done.5), channel_id=1, source_target_pairs={{0,1},{1,2},{2,3},{3,4},{4,5},{5,6},{6,7},{8,9},{9,10},{10,11},{11... | collective-permute-start | bytes 196616 | tf_op jit(solution)/shard_map/ppermute | solution.py:379
  48.0 5.5 %collective-permute-start.1 = (bf16[64,512]{1,0:T(8,128)(2,1)S(1)}, bf16[64,512]{1,0:T(8,128)(2,1)S(1)}, u32[]{:S(2)}, u32[]{:S(2)}) collective-permute-start(bf16[64,512]{1,0:T(8,128)(2,1)S(1)} %copy-done.4), channel_id=1, source_target_pairs={{1,0},{2,1},{3,2},{4,3},{5,4},{6,5},{7,6},{9,8},{10,9},{11,10},{12... | collective-permute-start | bytes 196616 | tf_op jit(solution)/shard_map/ppermute | solution.py:380
  51.7 1.8 %copy-start.2 = (bf16[64,512]{1,0:T(8,128)(2,1)}, bf16[64,512]{1,0:T(8,128)(2,1)S(1)}, u32[]{:S(2)}) copy-start(bf16[64,512]{1,0:T(8,128)(2,1)S(1)} %collective-permute-done.before_ref) | copy-start | bytes 196612
  53.5 0.6 copy-start.3
  54.1 29.1 %copy-start = (bf16[512,512]{1,0:T(8,128)(2,1)S(1)}, bf16[512,512]{1,0:T(8,128)(2,1)}, u32[]{:S(2)}) copy-start(bf16[512,512]{1,0:T(8,128)(2,1)} %constant.21.clone.synth_hbm) | copy-start | bytes 1572868
  54.1 29.1 %copy-start.1 = (f32[16]{0:T(128)S(1)}, f32[16]{0:T(128)}, u32[]{:S(2)}) copy-start(f32[16]{0:T(128)} %taper_ref.3) | copy-start | bytes 196

commit v7 on v6

--- a/solution.py
+++ b/solution.py
@@ -13,8 +13,8 @@
 DISTINCT = 64
 PAD = 8
 TILE = 256
-STEP = 512
-GROUPS = 4
+STEP = 1024
+PITCH = 5
 CHUNKS = 8
 UNROLL = 8
 HEAD = 4
@@ -65,7 +65,7 @@
 
 def put_rows(ref, start, block):
     for q in range(4):
-        at = pl.ds(start + q, block.shape[0], stride=4)
+        at = pl.ds(start + q, block.shape[0], stride=PITCH)
         ref[at, :] = block[:, 128 * q : 128 * (q + 1)]
 
 
@@ -78,6 +78,14 @@
     for q in range(4):
         part = held_ref[pl.ds(base * 4 + q, count, stride=4), :]
         out_ref[pl.ds(base, count), 128 * q : 128 * (q + 1)] = part.astype(BF16)
+
+
+def groups(peers):
+    sizes = []
+    while peers > 2:
+        sizes.append(peers // 2)
+        peers -= peers // 2
+    return sizes + [peers]
 
 
 def spectra_kernel(
@@ -101,7 +109,7 @@
     for g in range(lists.shape[0]):
         match = places[:, g : g + 1] == lane
         picked = jnp.max(jnp.where(match, columns[:, g : g + 1], 0), axis=0, keepdims=True)
-        distinct_ref[g : g + 1, :] = picked * 4
+        distinct_ref[g : g + 1, :] = picked * PITCH
     asking = pltpu.make_async_copy(distinct_ref, asked_ref, asked_sem)
     asking.start()
     table.wait()
@@ -111,7 +119,7 @@
         spectra = jnp.dot(
             traces_ref[at, :], table_ref[...], preferred_element_type=F32
         ).astype(BF16)
-        put_rows(rows_ref, PAD + b * STEP * 4, spectra.astype(F32))
+        put_rows(rows_ref, PAD + b * STEP * PITCH, spectra.astype(F32))
         for edge, hbm, part, first in ((0, first_hbm, 0, 0), (1, last_hbm, parts - 1, STEP - HALO)):
             if b == part:
                 edge_ref[edge] = spectra[first : first + HALO]
@@ -119,19 +127,20 @@
                 stores[edge].start()
     asking.wait()
     peers = asked_ref.shape[0]
-    each = peers // GROUPS
     sends = []
-    for g in range(GROUPS):
+    done = 0
+    for n, each in enumerate(groups(peers)):
 
         def one(p, _):
             base = pl.multiple_of(p * DISTINCT, DISTINCT)
             gather_rows(lambda k: asked_ref[p, k], rows_ref, held_ref, out_ref, base, DISTINCT)
             return 0
 
-        lax.fori_loop(g * each, (g + 1) * each, one, 0)
-        at = pl.ds(g * each * DISTINCT, each * DISTINCT)
-        sends.append(pltpu.make_async_copy(out_ref.at[at], out_hbm.at[at], out_sems.at[g]))
-        sends[g].start()
+        lax.fori_loop(done, done + each, one, 0)
+        at = pl.ds(done * DISTINCT, each * DISTINCT)
+        sends.append(pltpu.make_async_copy(out_ref.at[at], out_hbm.at[at], out_sems.at[n]))
+        sends[n].start()
+        done += each
     for copy in stores + sends:
         copy.wait()
 
@@ -170,7 +179,7 @@
         rows = jnp.concatenate(rows, axis=0).astype(jnp.int32)
         out = lax.broadcasted_iota(jnp.int32, (8, cap), 0) + at
         key_ref[pl.ds(at, 8), :] = (rows * outs + out) * 16 + taper_ref[pl.ds(at, 8), :]
-        value_ref[pl.ds(at, 8), :] = src_ref[pl.ds(at, 8), :] * 4
+        value_ref[pl.ds(at, 8), :] = src_ref[pl.ds(at, 8), :] * PITCH
         return 0
 
     lax.fori_loop(0, outs // 8, some, 0)
@@ -192,7 +201,7 @@
         for copy in copies:
             copy.start()
         put_rows(all_ref, PAD, before_ref[...].astype(F32))
-        put_rows(all_ref, PAD + (HALO + own) * 4, after_ref[...].astype(F32))
+        put_rows(all_ref, PAD + (HALO + own) * PITCH, after_ref[...].astype(F32))
         for copy in copies:
             copy.wait()
 
@@ -201,7 +210,7 @@
             spectra = jnp.dot(
                 traces_ref[pl.ds(at, STEP), :], table_ref[...], preferred_element_type=F32
             ).astype(BF16)
-            put_rows(all_ref, PAD + HALO * 4 + at * 4, spectra.astype(F32))
+            put_rows(all_ref, PAD + (HALO + at) * PITCH, spectra.astype(F32))
             return 0
 
         lax.fori_loop(0, own // STEP, one, 0)
@@ -216,8 +225,8 @@
 
 
 def pairs_kernel(
-    ends_ref, taper_ref, key_ref, source_hbm, arrived_ref, synth_hbm, out_ref,
-    source_ref, synth_ref, sum_ref, weight_ref, hot_ref, product_ref, meet_ref, sems, synth_sem,
+    meet_ref, taper_ref, key_ref, source_hbm, arrived_ref, synth_hbm, out_ref,
+    source_ref, synth_ref, sum_ref, weight_ref, hot_ref, product_ref, sems, synth_sem,
 ):
     tiles, _, samples = source_ref.shape
     outs = out_ref.shape[0]
@@ -234,21 +243,6 @@
     synth_copy = pltpu.make_async_copy(synth_hbm, synth_ref, synth_sem)
     synth_copy.start()
     meets = meet_ref.shape[0]
-
-    def blank(e, _):
-        meet_ref[e] = (meets - tiles) * 64 + tiles - 1
-        return 0
-
-    lax.fori_loop(tiles, meets, blank, 0)
-
-    def meet(t, count):
-        def add(b, count):
-            meet_ref[count] = b * 64 + t
-            return count + 1
-
-        return lax.fori_loop(ends_ref[0, t], ends_ref[1, t] + 1, add, count)
-
-    lax.fori_loop(0, tiles, meet, 0)
     entry = key_ref[...] & 15
     weights = jnp.zeros(entry.shape, F32)
     for k in range(taper_ref.shape[0]):
@@ -308,6 +302,19 @@
     synth_copy.wait()
     summed = sum_ref[...].astype(BF16)
     out_ref[...] = jnp.dot(summed, synth_ref[...], preferred_element_type=F32).astype(BF16)
+
+
+def meet_list(ends, meets):
+    tiles = ends.shape[1]
+    counts = ends[1] - ends[0] + 1
+    tile = jnp.arange(tiles, dtype=jnp.int32)
+    ahead = jnp.sum(jnp.where(tile[None, :] < tile[:, None], counts[None, :], 0), axis=1)
+    place = jnp.arange(meets, dtype=jnp.int32)[:, None]
+    inside = (place >= ahead[None, :]) & (place < (ahead + counts)[None, :])
+    value = (ends[0] + place - ahead[None, :]) * 64 + tile[None, :]
+    listed = jnp.sum(jnp.where(inside, value, 0), axis=1)
+    used = jnp.any(inside, axis=1)
+    return jnp.where(used, listed, (meets - tiles) * 64 + tiles - 1).astype(jnp.int32)
 
 
 VMEM = pl.BlockSpec(memory_space=pltpu.VMEM)
@@ -358,8 +365,8 @@
             pltpu.VMEM((tr_rows, samples), BF16),
             pltpu.VMEM((samples, samples), BF16),
             pltpu.VMEM((2, HALO, samples), BF16),
-            pltpu.VMEM((tr_rows * 4 + 2 * PAD, 128), F32),
-            pltpu.VMEM((fetched * 4, 128), F32),
+            pltpu.VMEM((tr_rows * PITCH + 2 * PAD, 128), F32),
+            pltpu.VMEM((fetched * 4 + PAD, 128), F32),
             pltpu.VMEM((fetched, samples), BF16),
             pltpu.VMEM((sails, cap), jnp.int32),
             pltpu.SMEM((sails, cap), jnp.int32),
@@ -367,7 +374,7 @@
             pltpu.SemaphoreType.DMA,
             pltpu.SemaphoreType.DMA,
             pltpu.SemaphoreType.DMA((2,)),
-            pltpu.SemaphoreType.DMA((GROUPS,)),
+            pltpu.SemaphoreType.DMA((len(groups(sails)),)),
         ],
         compiler_params=params(56),
         name="spectra",
@@ -403,8 +410,8 @@
         scratch_shapes=[
             pltpu.VMEM((tr_rows, samples), BF16),
             pltpu.VMEM((samples, samples), BF16),
-            pltpu.VMEM(((tr_rows + 2 * HALO) * 4 + 2 * PAD, 128), F32),
-            pltpu.VMEM((count // 8 * 4, 128), F32),
+            pltpu.VMEM(((tr_rows + 2 * HALO) * PITCH + 2 * PAD, 128), F32),
+            pltpu.VMEM((count // 8 * 4 + PAD, 128), F32),
             pltpu.SemaphoreType.DMA((2,)),
         ],
         compiler_params=params(56),
@@ -423,14 +430,13 @@
             pltpu.VMEM((tiles, TILE), F32),
             pltpu.VMEM((outs, UNROLL * TILE), BF16),
             pltpu.VMEM((UNROLL * TILE, samples), BF16),
-            pltpu.SMEM((meets,), jnp.int32),
             pltpu.SemaphoreType.DMA((CHUNKS,)),
             pltpu.SemaphoreType.DMA,
         ],
         compiler_params=params(50),
         name="pairs",
     )(
-        ends, taper_table, key.reshape(tiles, TILE), sources.reshape(tiles, TILE, samples), arrived,
+        meet_list(ends, meets), taper_table, key.reshape(tiles, TILE), sources.reshape(tiles, TILE, samples), arrived,
         synthesis_table(samples, aper),
     )
 

time: 92.2 us -> 91.8 us (level)
  transfers between devices with their start and end apart: 3 -> 3, of which waited for: 2 -> 2; matrix products, arithmetic and copies ran while one was open for 8% -> 9% of each run, Pallas kernels for 22% -> 22%
where the time goes in v7:
time: 91.8 us; the launch traced here: 91.2 us
  Pallas kernels  36.2 us (39%)
  blocking collectives  21.1 us (23%)
  waiting for transfers between devices  15.4 us (17%)
  starting transfers between devices  9.72 us (11%)
  other arithmetic  7.79 us (8%)
    all_to_all x1, blocking collectives, body(): lax.all_to_all(lists, 'sail', split_axis=0, concat_axis=0, tiled=True)  21.1 us
    pallas_call x1, Pallas kernels, body(): pl.pallas_call(sources_kernel, grid=(8,), in_specs=[SMEM, HBM, HBM, VMEM,...  15 us
    all_to_all x1, waiting for transfers between devices, body(): lax.all_to_all(outgoing.reshape(sails, DISTINCT, samples), 'sail', split_...  13.5 us
    pallas_call x1, Pallas kernels, body(): pl.pallas_call(pairs_kernel, in_specs=[SMEM, SMEM, VMEM, HBM, VMEM, HBM],...  8.42 us
    sort x1, other arithmetic, body(): lax.sort((key.reshape(-1), value.reshape(-1)), num_keys=1, is_stable=False)  7.09 us
    pallas_call x1, Pallas kernels, body(): pl.pallas_call(spectra_kernel, in_specs=[VMEM, HBM, HBM], out_specs=[HBM,...  6.78 us
    pallas_call x1, Pallas kernels, body(): pl.pallas_call(slots_kernel, in_specs=[SMEM] + [VMEM] * 4, out_specs=[VME...  4.71 us
    all_to_all x1, starting transfers between devices, body(): lax.all_to_all(outgoing.reshape(sails, DISTINCT, samples), 'sail', split_...  4.15 us
  transfers between devices with their start and end apart: 3, of which 2 were waited for; matrix products, arithmetic and copies ran while one was open for 9% of the time, Pallas kernels for 22%

profile of v7, /device:TPU:4, one launch (start us, length us, event | category | flops | bytes accessed | tf_op | source)
XLA Modules:
  0.0 91.2 jit_solution(14766316140136674372)
XLA Ops:
  0.0 1.4 %order.1 = s32[32,1,128]{2,1,0:T(1,128)} custom-call(s32[32]{0:T(128)} %owner_ref.3, s32[32,128]{1,0:T(8,128)} %rows_ref.3), custom_call_target="tpu_custom_call" | custom-call | tf_op jit(solution)/shard_map/order/pallas_call | solution.py:343
  1.4 21.1 %all_to_all.10 = s32[32,1,128]{2,1,0:T(1,128)} all-to-all(s32[32,1,128]{2,1,0:T(1,128)} %order.1), channel_id=1, replica_groups=mesh['sail'=32,'cable'=8] {'sail'}, dimensions={0} | all-to-all | bytes 32768 | tf_op jit(solution)/shard_map/all_to_all | solution.py:351
  22.5 6.8 %spectra.1 = (bf16[64,512]{1,0:T(8,128)(2,1)}, bf16[64,512]{1,0:T(8,128)(2,1)}, bf16[2048,512]{1,0:T(8,128)(2,1)}) custom-call(s32[32,128]{1,0:T(8,128)} %bitcast.26, bf16[2048,512]{1,0:T(8,128)(2,1)} %traces_hbm.3, bf16[512,512]{1,0:T(8,128)(2,1)} %constant.28.clone.table_hbm), custom_call_target="tpu_custom_call" | custom-call | tf_op jit(solution)/shard_map/spectra/pallas_call | solution.py:355
  29.3 0.0 copy-start.5
  29.3 0.0 copy-start.4
  29.3 4.2 %all-to-all-start.1 = ((bf16[32,64,512]{2,1,0:T(8,128)(2,1)}), bf16[32,64,512]{2,1,0:T(8,128)(2,1)S(1)}, u32[]{:S(2)}, u32[]{:S(2)}) async-start(bf16[32,64,512]{2,1,0:T(8,128)(2,1)} %bitcast.25), calls=%async_computation.1 | async-start | bytes 4194304 | tf_op jit(solution)/shard_map/all_to_all | solution.py:382
  33.5 4.7 %slots.1 = (s32[64,128]{1,0:T(8,128)}, s32[64,128]{1,0:T(8,128)}) custom-call(s32[32]{0:T(128)} %owner_ref.3, s32[32,128]{1,0:T(8,128)} %rows_ref.3, s32[64,128]{1,0:T(8,128)} %src_ref.1, s32[64,128]{1,0:T(8,128)} %rcv_ref.1, s32[64,128]{1,0:T(8,128)} %taper_ref.2), custom_call_target="tpu_custom_call" | custom-call | bytes 10485760 | tf_op jit(solution)/shard_map/slots/pallas_call | solution.py:388
  38.2 7.1 %sort.15 = (s32[8192]{0:T(1024)S(1)}, s32[8192]{0:T(1024)}) sort(s32[8192]{0:T(1024)} %bitcast.27, s32[8192]{0:T(1024)} %bitcast.28), dimensions={0}, to_apply=%region_0.0 | sort | flops 106496 | bytes 131072 | tf_op jit(solution)/shard_map/sort | solution.py:399
  45.3 0.1 slice.10
  45.4 0.2 fusion.6
  45.6 0.1 select_reduce_fusion.1
  45.7 0.1 copy.15
  45.8 0.2 slice_reduce_fusion
  46.0 0.1 fusion.5
  46.1 0.1 select_reduce_fusion
  46.2 0.0 copy-done.5
  46.2 1.9 %collective-permute-start = (bf16[64,512]{1,0:T(8,128)(2,1)S(1)}, bf16[64,512]{1,0:T(8,128)(2,1)S(1)}, u32[]{:S(2)}, u32[]{:S(2)}) collective-permute-start(bf16[64,512]{1,0:T(8,128)(2,1)S(1)} %copy-done.5), channel_id=1, source_target_pairs={{0,1},{1,2},{2,3},{3,4},{4,5},{5,6},{6,7},{8,9},{9,10},{10,11},{11... | collective-permute-start | bytes 196616 | tf_op jit(solution)/shard_map/ppermute | solution.py:386
  48.1 0.0 copy-done.4
  48.1 3.6 %collective-permute-start.1 = (bf16[64,512]{1,0:T(8,128)(2,1)S(1)}, bf16[64,512]{1,0:T(8,128)(2,1)S(1)}, u32[]{:S(2)}, u32[]{:S(2)}) collective-permute-start(bf16[64,512]{1,0:T(8,128)(2,1)S(1)} %copy-done.4), channel_id=1, source_target_pairs={{1,0},{2,1},{3,2},{4,3},{5,4},{6,5},{7,6},{9,8},{10,9},{11,10},{12... | collective-permute-start | bytes 196616 | tf_op jit(solution)/shard_map/ppermute | solution.py:387
  51.8 0.0 collective-permute-done.before_ref
  51.8 0.0 copy-start.2
  51.8 1.8 %collective-permute-done.1.after_ref = bf16[64,512]{1,0:T(8,128)(2,1)S(1)} collective-permute-done((bf16[64,512]{1,0:T(8,128)(2,1)S(1)}, bf16[64,512]{1,0:T(8,128)(2,1)S(1)}, u32[]{:S(2)}, u32[]{:S(2)}) %collective-permute-start.1) | collective-permute-done | bytes 65568 | tf_op jit(solution)/shard_map/ppermute | solution.py:387
  53.6 0.0 copy-start.3
  53.6 0.0 copy-done.2
  53.6 0.6 copy-done.3
  54.3 0.0 copy-start
  54.3 0.0 copy-start.1
  54.3 15.0 %sources.1 = bf16[8192,512]{1,0:T(8,128)(2,1)} custom-call(s32[8192]{0:T(1024)} %get-tuple-element.15.src_ref, bf16[2048,512]{1,0:T(8,128)(2,1)} %traces_hbm.3, bf16[512,512]{1,0:T(8,128)(2,1)} %constant.28.clone.table_hbm, bf16[64,512]{1,0:T(8,128)(2,1)} %copy-done.2, bf16[64,512]{1,0:T(8,128)(2,1)} %copy-done.3), custom_call_target="tpu_custom_call" | custom-call | bytes 41943040 | tf_op jit(solution)/shard_map/sources/pallas_call | solution.py:404
  69.2 13.5 %all-to-all-done.1 = bf16[32,64,512]{2,1,0:T(8,128)(2,1)S(1)} async-done(((bf16[32,64,512]{2,1,0:T(8,128)(2,1)}), bf16[32,64,512]{2,1,0:T(8,128)(2,1)S(1)}, u32[]{:S(2)}, u32[]{:S(2)}) %all-to-all-start.1) | async-done | bytes 2097184 | tf_op jit(solution)/shard_map/all_to_all | solution.py:382
  82.7 0.0 copy-done
  82.7 0.0 copy-done.1
  82.7 8.4 %pairs.1 = bf16[64,512]{1,0:T(8,128)(2,1)} custom-call(s32[40]{0:T(128)S(1)} %broadcast_select_fusion.meet_ref, f32[16]{0:T(128)S(1)} %copy-done.1, s32[32,256]{1,0:T(8,128)S(1)} %reshape.26.key_ref, bf16[32,256,512]{2,1,0:T(8,128)(2,1)} %bitcast.24, bf16[2048,512]{1,0:T(8,128)(2,1)S(1)} %bitcast.23, bf16[512,512]{1,0:T(8,128)(2,1)S(1)} %copy-done), custom_call_target="tpu_custom_call" | custom-call | tf_op jit(solution)/shard_map/pairs/pallas_call | solution.py:421
  (3 shorter events, 0.0 us)
Async XLA Ops:
  29.3 16.9 %copy-start.5 = (bf16[64,512]{1,0:T(8,128)(2,1)S(1)}, bf16[64,512]{1,0:T(8,128)(2,1)}, u32[]{:S(2)}) copy-start(bf16[64,512]{1,0:T(8,128)(2,1)} %get-tuple-element.16) | copy-start | bytes 196612
  29.3 18.8 %copy-start.4 = (bf16[64,512]{1,0:T(8,128)(2,1)S(1)}, bf16[64,512]{1,0:T(8,128)(2,1)}, u32[]{:S(2)}) copy-start(bf16[64,512]{1,0:T(8,128)(2,1)} %get-tuple-element.17) | copy-start | bytes 196612
  29.3 53.4 %all-to-all-start.1 = ((bf16[32,64,512]{2,1,0:T(8,128)(2,1)}), bf16[32,64,512]{2,1,0:T(8,128)(2,1)S(1)}, u32[]{:S(2)}, u32[]{:S(2)}) async-start(bf16[32,64,512]{2,1,0:T(8,128)(2,1)} %bitcast.25), calls=%async_computation.1 | async-start | bytes 4194304 | tf_op jit(solution)/shard_map/all_to_all | solution.py:382
  46.2 5.6 %collective-permute-start = (bf16[64,512]{1,0:T(8,128)(2,1)S(1)}, bf16[64,512]{1,0:T(8,128)(2,1)S(1)}, u32[]{:S(2)}, u32[]{:S(2)}) collective-permute-start(bf16[64,512]{1,0:T(8,128)(2,1)S(1)} %copy-done.5), channel_id=1, source_target_pairs={{0,1},{1,2},{2,3},{3,4},{4,5},{5,6},{6,7},{8,9},{9,10},{10,11},{11... | collective-permute-start | bytes 196616 | tf_op jit(solution)/shard_map/ppermute | solution.py:386
  48.1 5.5 %collective-permute-start.1 = (bf16[64,512]{1,0:T(8,128)(2,1)S(1)}, bf16[64,512]{1,0:T(8,128)(2,1)S(1)}, u32[]{:S(2)}, u32[]{:S(2)}) collective-permute-start(bf16[64,512]{1,0:T(8,128)(2,1)S(1)} %copy-done.4), channel_id=1, source_target_pairs={{1,0},{2,1},{3,2},{4,3},{5,4},{6,5},{7,6},{9,8},{10,9},{11,10},{12... | collective-permute-start | bytes 196616 | tf_op jit(solution)/shard_map/ppermute | solution.py:387
  51.8 1.9 %copy-start.2 = (bf16[64,512]{1,0:T(8,128)(2,1)}, bf16[64,512]{1,0:T(8,128)(2,1)S(1)}, u32[]{:S(2)}) copy-start(bf16[64,512]{1,0:T(8,128)(2,1)S(1)} %collective-permute-done.before_ref) | copy-start | bytes 196612
  53.6 0.6 copy-start.3
  54.3 28.5 %copy-start = (bf16[512,512]{1,0:T(8,128)(2,1)S(1)}, bf16[512,512]{1,0:T(8,128)(2,1)}, u32[]{:S(2)}) copy-start(bf16[512,512]{1,0:T(8,128)(2,1)} %constant.29.clone.synth_hbm) | copy-start | bytes 1572868
  54.3 28.5 %copy-start.1 = (f32[16]{0:T(128)S(1)}, f32[16]{0:T(128)}, u32[]{:S(2)}) copy-start(f32[16]{0:T(128)} %taper_ref.3) | copy-start | bytes 196

commit v8 on v7

--- a/solution.py
+++ b/solution.py
@@ -89,11 +89,13 @@
 
 
 def spectra_kernel(
-    lists_ref, traces_hbm, table_hbm, first_hbm, last_hbm, out_hbm,
-    traces_ref, table_ref, edge_ref, rows_ref, held_ref, out_ref, distinct_ref, asked_ref,
-    in_sems, table_sem, asked_sem, edge_sems, out_sems,
+    lists_hbm, traces_hbm, table_hbm, first_hbm, last_hbm, out_hbm,
+    traces_ref, table_ref, edge_ref, rows_ref, held_ref, out_ref, lists_ref, distinct_ref, asked_ref,
+    in_sems, table_sem, lists_sem, asked_sem, edge_sems, out_sems,
 ):
     parts = len(range(0, traces_ref.shape[0], STEP))
+    listing = pltpu.make_async_copy(lists_hbm, lists_ref, lists_sem)
+    listing.start()
     table = pltpu.make_async_copy(table_hbm, table_ref, table_sem)
     table.start()
     loads = []
@@ -102,6 +104,7 @@
         at = pl.ds(b * STEP, STEP)
         loads.append(pltpu.make_async_copy(traces_hbm.at[at], traces_ref.at[at], in_sems.at[b]))
         loads[b].start()
+    listing.wait()
     lists = lists_ref[...]
     columns, place = first_entries(lists)
     places = turned(place)
@@ -354,7 +357,7 @@
     table = forward_table(samples)
     first, last, outgoing = pl.pallas_call(
         spectra_kernel,
-        in_specs=[VMEM, HBM, HBM],
+        in_specs=[HBM, HBM, HBM],
         out_specs=[HBM, HBM, HBM],
         out_shape=[
             shape((HALO, samples), BF16),
@@ -369,8 +372,10 @@
             pltpu.VMEM((fetched * 4 + PAD, 128), F32),
             pltpu.VMEM((fetched, samples), BF16),
             pltpu.VMEM((sails, cap), jnp.int32),
+            pltpu.VMEM((sails, cap), jnp.int32),
             pltpu.SMEM((sails, cap), jnp.int32),
             pltpu.SemaphoreType.DMA((parts,)),
+            pltpu.SemaphoreType.DMA,
             pltpu.SemaphoreType.DMA,
             pltpu.SemaphoreType.DMA,
             pltpu.SemaphoreType.DMA((2,)),

time: 91.8 us -> 92.2 us (level)
  transfers between devices with their start and end apart: 3 -> 3, of which waited for: 2 -> 2; matrix products, arithmetic and copies ran while one was open for 9% -> 9% of each run, Pallas kernels for 22% -> 21%
where the time goes in v8:
time: 92.2 us; the launch traced here: 91.6 us
  Pallas kernels  36.7 us (40%)
  blocking collectives  21.1 us (23%)
  waiting for transfers between devices  15.4 us (17%)
  starting transfers between devices  9.72 us (11%)
  other arithmetic  7.79 us (8%)
    all_to_all x1, blocking collectives, body(): lax.all_to_all(lists, 'sail', split_axis=0, concat_axis=0, tiled=True)  21.1 us
    pallas_call x1, Pallas kernels, body(): pl.pallas_call(sources_kernel, grid=(8,), in_specs=[SMEM, HBM, HBM, VMEM,...  14.9 us
    all_to_all x1, waiting for transfers between devices, body(): lax.all_to_all(outgoing.reshape(sails, DISTINCT, samples), 'sail', split_...  13.5 us
    pallas_call x1, Pallas kernels, body(): pl.pallas_call(pairs_kernel, in_specs=[SMEM, SMEM, VMEM, HBM, VMEM, HBM],...  8.42 us
    pallas_call x1, Pallas kernels, body(): pl.pallas_call(spectra_kernel, in_specs=[HBM, HBM, HBM], out_specs=[HBM,...  7.22 us
    sort x1, other arithmetic, body(): lax.sort((key.reshape(-1), value.reshape(-1)), num_keys=1, is_stable=False)  7.09 us
    pallas_call x1, Pallas kernels, body(): pl.pallas_call(slots_kernel, in_specs=[SMEM] + [VMEM] * 4, out_specs=[VME...  4.71 us
    all_to_all x1, starting transfers between devices, body(): lax.all_to_all(outgoing.reshape(sails, DISTINCT, samples), 'sail', split_...  4.15 us
  transfers between devices with their start and end apart: 3, of which 2 were waited for; matrix products, arithmetic and copies ran while one was open for 9% of the time, Pallas kernels for 21%

profile of v8, /device:TPU:4, one launch (start us, length us, event | category | flops | bytes accessed | tf_op | source)
XLA Modules:
  0.0 91.6 jit_solution(9811840206949079373)
XLA Ops:
  0.0 1.4 %order.1 = s32[32,1,128]{2,1,0:T(1,128)} custom-call(s32[32]{0:T(128)} %owner_ref.3, s32[32,128]{1,0:T(8,128)} %rows_ref.3), custom_call_target="tpu_custom_call" | custom-call | tf_op jit(solution)/shard_map/order/pallas_call | solution.py:346
  1.4 21.1 %all_to_all.10 = s32[32,1,128]{2,1,0:T(1,128)} all-to-all(s32[32,1,128]{2,1,0:T(1,128)} %order.1), channel_id=1, replica_groups=mesh['sail'=32,'cable'=8] {'sail'}, dimensions={0} | all-to-all | bytes 32768 | tf_op jit(solution)/shard_map/all_to_all | solution.py:354
  22.5 7.2 %spectra.1 = (bf16[64,512]{1,0:T(8,128)(2,1)}, bf16[64,512]{1,0:T(8,128)(2,1)}, bf16[2048,512]{1,0:T(8,128)(2,1)}) custom-call(s32[32,128]{1,0:T(8,128)} %bitcast.26, bf16[2048,512]{1,0:T(8,128)(2,1)} %traces_hbm.3, bf16[512,512]{1,0:T(8,128)(2,1)} %constant.28.clone.table_hbm), custom_call_target="tpu_custom_call" | custom-call | tf_op jit(solution)/shard_map/spectra/pallas_call | solution.py:358
  29.7 0.0 copy-start.5
  29.7 0.0 copy-start.4
  29.8 4.2 %all-to-all-start.1 = ((bf16[32,64,512]{2,1,0:T(8,128)(2,1)}), bf16[32,64,512]{2,1,0:T(8,128)(2,1)S(1)}, u32[]{:S(2)}, u32[]{:S(2)}) async-start(bf16[32,64,512]{2,1,0:T(8,128)(2,1)} %bitcast.25), calls=%async_computation.1 | async-start | bytes 4194304 | tf_op jit(solution)/shard_map/all_to_all | solution.py:387
  33.9 4.7 %slots.1 = (s32[64,128]{1,0:T(8,128)}, s32[64,128]{1,0:T(8,128)}) custom-call(s32[32]{0:T(128)} %owner_ref.3, s32[32,128]{1,0:T(8,128)} %rows_ref.3, s32[64,128]{1,0:T(8,128)} %src_ref.1, s32[64,128]{1,0:T(8,128)} %rcv_ref.1, s32[64,128]{1,0:T(8,128)} %taper_ref.2), custom_call_target="tpu_custom_call" | custom-call | bytes 10485760 | tf_op jit(solution)/shard_map/slots/pallas_call | solution.py:393
  38.6 7.1 %sort.15 = (s32[8192]{0:T(1024)S(1)}, s32[8192]{0:T(1024)}) sort(s32[8192]{0:T(1024)} %bitcast.27, s32[8192]{0:T(1024)} %bitcast.28), dimensions={0}, to_apply=%region_0.0 | sort | flops 106496 | bytes 131072 | tf_op jit(solution)/shard_map/sort | solution.py:404
  45.7 0.1 slice.10
  45.8 0.2 fusion.6
  46.0 0.1 select_reduce_fusion.1
  46.1 0.1 copy.15
  46.2 0.2 slice_reduce_fusion
  46.4 0.1 fusion.5
  46.5 0.1 select_reduce_fusion
  46.6 0.0 copy-done.5
  46.6 1.9 %collective-permute-start = (bf16[64,512]{1,0:T(8,128)(2,1)S(1)}, bf16[64,512]{1,0:T(8,128)(2,1)S(1)}, u32[]{:S(2)}, u32[]{:S(2)}) collective-permute-start(bf16[64,512]{1,0:T(8,128)(2,1)S(1)} %copy-done.5), channel_id=1, source_target_pairs={{0,1},{1,2},{2,3},{3,4},{4,5},{5,6},{6,7},{8,9},{9,10},{10,11},{11... | collective-permute-start | bytes 196616 | tf_op jit(solution)/shard_map/ppermute | solution.py:391
  48.5 0.0 copy-done.4
  48.6 3.6 %collective-permute-start.1 = (bf16[64,512]{1,0:T(8,128)(2,1)S(1)}, bf16[64,512]{1,0:T(8,128)(2,1)S(1)}, u32[]{:S(2)}, u32[]{:S(2)}) collective-permute-start(bf16[64,512]{1,0:T(8,128)(2,1)S(1)} %copy-done.4), channel_id=1, source_target_pairs={{1,0},{2,1},{3,2},{4,3},{5,4},{6,5},{7,6},{9,8},{10,9},{11,10},{12... | collective-permute-start | bytes 196616 | tf_op jit(solution)/shard_map/ppermute | solution.py:392
  52.2 0.0 collective-permute-done.before_ref
  52.2 0.0 copy-start.2
  52.2 1.8 %collective-permute-done.1.after_ref = bf16[64,512]{1,0:T(8,128)(2,1)S(1)} collective-permute-done((bf16[64,512]{1,0:T(8,128)(2,1)S(1)}, bf16[64,512]{1,0:T(8,128)(2,1)S(1)}, u32[]{:S(2)}, u32[]{:S(2)}) %collective-permute-start.1) | collective-permute-done | bytes 65568 | tf_op jit(solution)/shard_map/ppermute | solution.py:392
  54.1 0.0 copy-start.3
  54.1 0.0 copy-done.2
  54.1 0.6 copy-done.3
  54.7 0.0 copy-start
  54.7 0.0 copy-start.1
  54.7 14.9 %sources.1 = bf16[8192,512]{1,0:T(8,128)(2,1)} custom-call(s32[8192]{0:T(1024)} %get-tuple-element.15.src_ref, bf16[2048,512]{1,0:T(8,128)(2,1)} %traces_hbm.3, bf16[512,512]{1,0:T(8,128)(2,1)} %constant.28.clone.table_hbm, bf16[64,512]{1,0:T(8,128)(2,1)} %copy-done.2, bf16[64,512]{1,0:T(8,128)(2,1)} %copy-done.3), custom_call_target="tpu_custom_call" | custom-call | bytes 41943040 | tf_op jit(solution)/shard_map/sources/pallas_call | solution.py:409
  69.7 13.5 %all-to-all-done.1 = bf16[32,64,512]{2,1,0:T(8,128)(2,1)S(1)} async-done(((bf16[32,64,512]{2,1,0:T(8,128)(2,1)}), bf16[32,64,512]{2,1,0:T(8,128)(2,1)S(1)}, u32[]{:S(2)}, u32[]{:S(2)}) %all-to-all-start.1) | async-done | bytes 2097184 | tf_op jit(solution)/shard_map/all_to_all | solution.py:387
  83.2 0.0 copy-done
  83.2 0.0 copy-done.1
  83.2 8.4 %pairs.1 = bf16[64,512]{1,0:T(8,128)(2,1)} custom-call(s32[40]{0:T(128)S(1)} %broadcast_select_fusion.meet_ref, f32[16]{0:T(128)S(1)} %copy-done.1, s32[32,256]{1,0:T(8,128)S(1)} %reshape.26.key_ref, bf16[32,256,512]{2,1,0:T(8,128)(2,1)} %bitcast.24, bf16[2048,512]{1,0:T(8,128)(2,1)S(1)} %bitcast.23, bf16[512,512]{1,0:T(8,128)(2,1)S(1)} %copy-done), custom_call_target="tpu_custom_call" | custom-call | tf_op jit(solution)/shard_map/pairs/pallas_call | solution.py:426
  (3 shorter events, 0.0 us)
Async XLA Ops:
  29.7 16.9 %copy-start.5 = (bf16[64,512]{1,0:T(8,128)(2,1)S(1)}, bf16[64,512]{1,0:T(8,128)(2,1)}, u32[]{:S(2)}) copy-start(bf16[64,512]{1,0:T(8,128)(2,1)} %get-tuple-element.16) | copy-start | bytes 196612
  29.7 18.8 %copy-start.4 = (bf16[64,512]{1,0:T(8,128)(2,1)S(1)}, bf16[64,512]{1,0:T(8,128)(2,1)}, u32[]{:S(2)}) copy-start(bf16[64,512]{1,0:T(8,128)(2,1)} %get-tuple-element.17) | copy-start | bytes 196612
  29.8 53.4 %all-to-all-start.1 = ((bf16[32,64,512]{2,1,0:T(8,128)(2,1)}), bf16[32,64,512]{2,1,0:T(8,128)(2,1)S(1)}, u32[]{:S(2)}, u32[]{:S(2)}) async-start(bf16[32,64,512]{2,1,0:T(8,128)(2,1)} %bitcast.25), calls=%async_computation.1 | async-start | bytes 4194304 | tf_op jit(solution)/shard_map/all_to_all | solution.py:387
  46.6 5.6 %collective-permute-start = (bf16[64,512]{1,0:T(8,128)(2,1)S(1)}, bf16[64,512]{1,0:T(8,128)(2,1)S(1)}, u32[]{:S(2)}, u32[]{:S(2)}) collective-permute-start(bf16[64,512]{1,0:T(8,128)(2,1)S(1)} %copy-done.5), channel_id=1, source_target_pairs={{0,1},{1,2},{2,3},{3,4},{4,5},{5,6},{6,7},{8,9},{9,10},{10,11},{11... | collective-permute-start | bytes 196616 | tf_op jit(solution)/shard_map/ppermute | solution.py:391
  48.6 5.5 %collective-permute-start.1 = (bf16[64,512]{1,0:T(8,128)(2,1)S(1)}, bf16[64,512]{1,0:T(8,128)(2,1)S(1)}, u32[]{:S(2)}, u32[]{:S(2)}) collective-permute-start(bf16[64,512]{1,0:T(8,128)(2,1)S(1)} %copy-done.4), channel_id=1, source_target_pairs={{1,0},{2,1},{3,2},{4,3},{5,4},{6,5},{7,6},{9,8},{10,9},{11,10},{12... | collective-permute-start | bytes 196616 | tf_op jit(solution)/shard_map/ppermute | solution.py:392
  52.2 1.9 %copy-start.2 = (bf16[64,512]{1,0:T(8,128)(2,1)}, bf16[64,512]{1,0:T(8,128)(2,1)S(1)}, u32[]{:S(2)}) copy-start(bf16[64,512]{1,0:T(8,128)(2,1)S(1)} %collective-permute-done.before_ref) | copy-start | bytes 196612
  54.1 0.6 copy-start.3
  54.7 28.5 %copy-start = (bf16[512,512]{1,0:T(8,128)(2,1)S(1)}, bf16[512,512]{1,0:T(8,128)(2,1)}, u32[]{:S(2)}) copy-start(bf16[512,512]{1,0:T(8,128)(2,1)} %constant.29.clone.synth_hbm) | copy-start | bytes 1572868
  54.7 28.5 %copy-start.1 = (f32[16]{0:T(128)S(1)}, f32[16]{0:T(128)}, u32[]{:S(2)}) copy-start(f32[16]{0:T(128)} %taper_ref.3) | copy-start | bytes 196
